TPU v7x, 128 devices: a whole 4x4x4 slice. The times are simulated.
128 devices in a mesh: grp: 4 (over z), seq: 32 (over x, y, core).
Axes of the slice: x: 4, y: 4, z: 4, core: 2. Of those that a mesh axis runs over, the one named last changes fastest.
Arguments:
- projected: bfloat16 [32768, 3072], P(('grp', 'seq')), may hold values from -6 to 6
- conv_weight: float32 [4, 3072], replicated, may hold values from -3 to 3
- beta: float32 [8, 32768], P(None, ('grp', 'seq')), may hold values from 0 to 0.1, as said below
- gain: float32 [128], replicated, may hold values from 0.5 to 1.5
Outputs:
- normed: bfloat16 [32768, 1024], P(('grp', 'seq'))
Inputs may be any that keep to these rules, and one draw needn't show every extreme that they name: `beta`: each head has its own rate, varying over tokens and devices, with a few stretches at the largest value.
All inputs are finite; a program needn't handle non-finite values.
Results may differ from a plain program's by a relative error of at most 0.001.
Values may be sent and summed in bfloat16 or wider, within the bound.
No kernel may reach another device: no remote copies, remote signals or barrier semaphores. Data moves between devices by JAX's collectives and lax.ppermute only.
A program may use at most 320 MiB of HBM per device.

v0:
```python
import jax
import jax.numpy as jnp
from jax import lax
from jax.sharding import PartitionSpec as P

H = 8
DK = 128
KCONV = 4
SPAN = 128


def passed_along(block, axis, distance):
    devices = range(lax.axis_size(axis))
    route = [(i - distance, i) for i in devices if i - distance in devices]
    return lax.ppermute(block, axis, route)


def carried_in(array, axis, combine, identity):
    size, place = (lax.axis_size(axis), lax.axis_index(axis))
    everything = jax.tree.map(lambda part: lax.all_gather(part, axis), array)
    start = jax.tree.map(
        lambda part, zero: jnp.broadcast_to(jnp.asarray(zero, part.dtype), part.shape),
        array,
        identity,
    )

    def hop(k, before):
        reached = k < place
        new = combine(before, jax.tree.map(lambda part: part[k], everything))
        return jax.tree.map(lambda a, b: jnp.where(reached, a, b), new, before)

    return lax.fori_loop(0, size, hop, start)


def contract(form, left, right):
    return jnp.einsum(form, left, right, precision=lax.Precision.HIGHEST)


def conv_silu(extended, conv_weight, rows):
    mixed = jnp.zeros((rows, extended.shape[1]), jnp.float32)
    for offset in range(KCONV):
        mixed = mixed + conv_weight[offset] * extended[offset : offset + rows]
    return jax.nn.silu(mixed)


def unit_rows(values):
    return values / jnp.sqrt(jnp.sum(values * values, -1, keepdims=True) + 1e-06)


def split_heads(mixed):
    rows = mixed.shape[0]
    parts = mixed.reshape(rows // SPAN, SPAN, 3, H, DK).transpose(2, 3, 0, 1, 4)
    return (unit_rows(parts[0]), unit_rows(parts[1]), parts[2])


def unit_lower_inverse(inner, size):
    negated = -inner
    power = negated
    result = jnp.eye(size, dtype=jnp.float32) + negated
    reach = 2
    while reach < size:
        power = contract("...ij,...jk->...ik", power, power)
        result = result + contract("...ij,...jk->...ik", result, power)
        reach = reach * 2
    return result


def span_terms(queries, keys, values, beta_rates):
    size = keys.shape[-2]
    strict = jnp.tril(jnp.ones((size, size), jnp.float32), -1)
    inclusive = jnp.tril(jnp.ones((size, size), jnp.float32), 0)
    inner = contract("...id,...jd->...ij", beta_rates * keys, keys) * strict
    inverse = unit_lower_inverse(inner, size)
    right_side = jnp.concatenate([beta_rates * keys, beta_rates * values], -1)
    solved = contract("...ij,...jd->...id", inverse, right_side)
    width = keys.shape[-1]
    scores = contract("...id,...jd->...ij", queries, keys) * inclusive
    return (solved[..., :width], solved[..., width:], scores)


def finish(outputs, gain):
    rows = outputs.shape[0]
    spread = jnp.sqrt(jnp.mean(outputs * outputs, -1, keepdims=True) + 1e-06)
    return (outputs / spread * gain).astype(jnp.bfloat16).reshape(rows, H * DK)


def merge_partials(earlier, later):
    return (
        contract("hij,hjk->hik", later[0], earlier[0]),
        contract("hij,hjk->hik", later[0], earlier[1]) + later[1],
    )


def shards(projected, conv_weight, beta, gain):
    rows = projected.shape[0]
    rim = passed_along(projected[rows - (KCONV - 1) :], ("grp", "seq"), 1)
    extended = jnp.concatenate([rim, projected], 0).astype(jnp.float32)
    mixed = conv_silu(extended, conv_weight, rows)
    queries, keys, values = split_heads(mixed)
    beta_rates = beta.reshape(H, rows // SPAN, SPAN, 1)
    w_keys, u_values, scores = span_terms(queries, keys, values, beta_rates)
    ordered = tuple(
        (item.transpose(1, 0, 2, 3) for item in (queries, keys, w_keys, u_values, scores))
    )
    identity_matrix = jnp.broadcast_to(jnp.eye(DK, dtype=jnp.float32), (H, DK, DK))
    zero_state = jnp.zeros((H, DK, DK), jnp.float32)

    def compose(stacked, block):
        block_queries, block_keys, block_decay_keys, block_u, block_scores = block
        padded_u = jnp.concatenate([jnp.zeros_like(block_u), block_u], -1)
        fresh = padded_u - contract("hcd,hde->hce", block_decay_keys, stacked)
        return (stacked + contract("hcd,hce->hde", block_keys, fresh), None)

    stacked, _ = lax.scan(compose, jnp.concatenate([identity_matrix, zero_state], -1), ordered)
    local = (stacked[..., :DK], stacked[..., DK:])
    neutral = (identity_matrix, zero_state)
    incoming = carried_in(local, ("grp", "seq"), merge_partials, neutral)
    entering = incoming[1]

    def advance(state, block):
        block_queries, block_keys, block_decay_keys, block_u, block_scores = block
        fresh = block_u - contract("hcd,hde->hce", block_decay_keys, state)
        output = contract("hcd,hde->hce", block_queries, state) + contract(
            "hcj,hjd->hcd", block_scores, fresh
        )
        state = state + contract("hcd,hce->hde", block_keys, fresh)
        return (state, output)

    _, outputs = lax.scan(advance, entering, ordered)
    outputs = outputs.transpose(0, 2, 1, 3).reshape(rows, H, DK)
    return finish(outputs, gain)


def solution(mesh):
    placed = (P(("grp", "seq"), None), P(), P(None, ("grp", "seq")), P())
    return jax.shard_map(
        shards, mesh=mesh, in_specs=placed, out_specs=P(("grp", "seq"), None), check_vma=False
    )
```

profile of v0, /device:TPU:1, one launch (start us, length us, event | category | flops | bytes accessed | tf_op | source)
XLA Modules:
  0.0 661.5 jit_solution(17612799516075336468)
XLA Ops:
  7.5 4.6 collective-permute-start
  14.5 1.9 multiply_bitcast_fusion
  18.2 2.8 fusion.37
  22.2 2.2 convolution_add_fusion.9
  25.6 2.5 broadcast_multiply_fusion
  40.2 2.1 fusion.32
  43.6 6.9 %while.36 = (s32[]{:T(128)}, f32[8,128,256]{2,1,0:T(8,128)S(1)}, f32[2,8,128,128]{2,3,1,0:T(8,128)S(1)}, f32[2,8,128,128]{3,2,1,0:T(8,128)S(1)}, f32[2,8,128,128]{3,2,1,0:T(8,128)}, /*index=5*/s32[]{:T(128)}) while((s32[]{:T(128)}, f32[8,128,256]{2,1,0:T(8,128)S(1)}, f32[2,8,128,128]{2,3,1,0:T(8,128)S(1)}, f32[2,8,128,128]{3,2,1,0:T(8,128)S(1)}, ...), condition=%wide.region_2.3_spmd, body=%wide.region_1.2_spmd.sunk | while | flops 805830656 | bytes 7864409 | solution.py:114
  43.7 2.1 convolution_subtract_fusion.4
  47.1 2.1 convolution_subtract_fusion.4
  52.4 5.1 fusion.36
  57.5 161.0 %all-gather.7.cloned.1.call-done = f32[1024,128,128]{2,1,0:T(8,128)} async-done(((f32[8,128,128]{2,1,0:T(8,128)}), f32[1024,128,128]{2,1,0:T(8,128)}) %all-gather.7.cloned.1.call-update) | async-done | bytes 67108880 | tf_op jit(solution)/shard_map/all_gather | solution.py:20
  218.6 166.9 %all-gather.5.cloned.1.call-done = f32[1024,128,128]{2,1,0:T(8,128)} async-done(((f32[8,128,128]{2,1,0:T(8,128)}), f32[1024,128,128]{2,1,0:T(8,128)}) %all-gather.5.cloned.1.call-update) | async-done | bytes 67108880 | tf_op jit(solution)/shard_map/all_gather | solution.py:20
  385.5 251.9 %while.38 = (s32[]{:T(128)}, f32[8,128,128]{2,1,0:T(8,128)S(1)}, s32[]{:T(128)}, f32[128,8,128,128]{3,2,1,0:T(8,128)}, f32[128,8,128,128]{3,2,1,0:T(8,128)}, /*index=5*/s32[]{:T(128)}, s32[]{:T(128)}) while((s32[]{:T(128)}, f32[8,128,128]{2,1,0:T(8,128)S(1)}, s32[]{:T(128)}, f32[128,8,128,128]{3,2,1,0:T(8,128)}, ...), condition=%wide.region_4.5_spmd.clone, body=%wide.region_3.4_spmd.clone.sunk | while | flops 201850880 | bytes 3672679 | solution.py:32
  385.5 1.9 fusion.125
  387.5 1.9 fusion.125
  391.4 1.9 fusion.125
  393.4 1.9 fusion.125
  395.3 1.9 fusion.125
  397.3 1.9 fusion.125
  401.2 1.9 fusion.125
  403.2 1.9 fusion.125
  409.1 1.9 fusion.125
  411.1 1.9 fusion.125
  417.0 1.9 fusion.125
  418.9 1.9 fusion.125
  420.9 1.9 fusion.125
  426.8 1.9 fusion.125
  428.8 1.9 fusion.125
  434.7 1.9 fusion.125
  436.7 1.9 fusion.125
  442.6 1.9 fusion.125
  444.5 1.9 fusion.125
  446.5 1.9 fusion.125
  452.4 1.9 fusion.125
  454.4 1.9 fusion.125
  458.3 1.9 fusion.125
  460.3 1.9 fusion.125
  466.2 1.9 fusion.125
  468.1 1.9 fusion.125
  472.1 1.9 fusion.125
  476.0 1.9 fusion.125
  478.0 1.9 fusion.125
  483.9 1.9 fusion.125
  485.9 1.9 fusion.125
  491.8 1.9 fusion.125
  493.7 1.9 fusion.125
  497.7 1.9 fusion.125
  501.6 1.9 fusion.125
  503.6 1.9 fusion.125
  509.5 1.9 fusion.125
  511.4 1.9 fusion.125
  515.4 1.9 fusion.125
  517.3 1.9 fusion.125
  523.2 1.9 fusion.125
  525.2 1.9 fusion.125
  527.2 1.9 fusion.125
  533.1 1.9 fusion.125
  535.1 1.9 fusion.125
  541.0 1.9 fusion.125
  548.8 1.9 fusion.125
  574.4 1.9 fusion.125
  600.0 1.9 fusion.125
  625.6 1.9 fusion.125
  637.3 12.3 %while.37 = (s32[]{:T(128)}, f32[8,128,128]{2,1,0:T(8,128)S(1)}, f32[2,8,128,128]{3,2,1,0:T(8,128)}, f32[2,8,128,128]{2,3,1,0:T(8,128)S(1)}, f32[2,8,128,128]{3,...) while((s32[]{:T(128)}, f32[8,128,128]{2,1,0:T(8,128)S(1)}, ...), condition=%wide.region_7.8_spmd, body=%wide.region_6.7_spmd.sunk | while | flops 805699584 | bytes 20449472 | solution.py:129
  (286 shorter events, 194.7 us)
Async XLA Ops:
  6.5 45.9 %copy-start = (f32[128]{0:T(128)S(1)}, f32[128]{0:T(128)}, u32[]{:S(2)}) copy-start(f32[128]{0:T(128)} %param.13) | copy-start | bytes 1540
  6.5 7.5 %copy-start.8 = (bf16[256,3072]{1,0:T(8,128)(2,1)S(1)}, bf16[256,3072]{1,0:T(8,128)(2,1)}, u32[]{:S(2)}) copy-start(bf16[256,3072]{1,0:T(8,128)(2,1)} %param.10) | copy-start | bytes 4718596
  6.5 212.0 %all-gather.7.cloned.1.call-start = ((), (), s32[]{:S(2)}) async-start(), calls=%async_computation.1 | async-start | bytes 67633152 | tf_op jit(solution)/shard_map/all_gather | solution.py:20
  7.5 6.6 collective-permute-start
  17.6 8.0 %copy-start.1 = (f32[2,128,3,8,128]{4,1,0,3,2:T(8,128)}, f32[2,128,3,8,128]{4,1,0,3,2:T(8,128)S(1)}, u32[]{:S(2)}) copy-start(f32[2,128,3,8,128]{4,1,0,3,2:T(8,128)S(1)} %copy.57) | copy-start | bytes 9437188
  29.6 1.2 copy-start.3
  37.8 2.3 copy-start.6
  37.8 2.3 copy-start.7
  51.6 333.8 %all-gather.5.cloned.1.call-start = ((), (), s32[]{:S(2)}) async-start(), calls=%async_computation | async-start | bytes 67633152 | tf_op jit(solution)/shard_map/all_gather | solution.py:20
  637.3 4.4 copy-start.2
  637.4 4.4 copy-start.4
  642.5 1.0 copy-start.5
  643.5 4.4 copy-start.2
  643.5 4.4 copy-start.4
  648.6 1.0 copy-start.5
Sparse Core Ops, SparseCore 0:
  51.7 166.7 all-gather.6
  221.7 163.7 all-gather.4
where the time goes:
time: 665 us; the launch traced here: 662 us
  waiting for transfers between devices  329 us (49%)
  matrix products  284 us (43%)
  local copies, waits for them, and re-layouts  16.9 us (3%)
  between operations  13.8 us (2%)
  other arithmetic  8.39 us (1%)
    all_gather x2, waiting for transfers between devices, carried_in(): everything = jax.tree.map(lambda part: lax.all_gather(part, axis), array)  328 us
    dot_general x155, matrix products, contract(): return jnp.einsum(form, left, right, precision=lax.Precision.HIGHEST)  284 us
  transfers between devices with their start and end apart: 3, of which 2 were waited for; matrix products, arithmetic and copies ran while one was open for 1% of the time, Pallas kernels for 0%

commit v1 on v0

v1 whole, which is shorter than its diff:
```python
import functools

import jax
import jax.numpy as jnp
from jax import lax
from jax.experimental import pallas as pl
from jax.experimental.pallas import tpu as pltpu
from jax.sharding import Mesh
from jax.sharding import PartitionSpec as P

H = 8
DK = 128
KCONV = 4
HALF = H // 2
ROWS = 256
F32, BF16 = jnp.float32, jnp.bfloat16
ALL = ("z", "x", "y", "core")
VMEM_BYTES = 48 * 1024 * 1024


def split(a):
    high = a.astype(BF16)
    return high, (a - high.astype(F32)).astype(BF16)


def dot(a, b):
    return jnp.dot(a, b, preferred_element_type=F32)


def mm(a, b):
    a_high, a_low = split(a)
    b_high, b_low = split(b)
    wide = jnp.concatenate([b_high, b_low], 1)
    r = dot(jnp.concatenate([a_high, a_low], 1), jnp.concatenate([wide, wide], 0))
    n = b.shape[1]
    return r[:, :n] + r[:, n:]


def mmw(a, b):
    a_high, a_low = split(a)
    b_high, b_low = split(b)
    if a.shape[1] == 128:
        r = dot(jnp.concatenate([a_high, a_low], 1), jnp.concatenate([b_high, b_high], 0))
        return r + dot(a_high, b_low)
    return (dot(a_high, b_high) + dot(a_low, b_high)) + dot(a_high, b_low)


def places(size):
    r = lax.broadcasted_iota(jnp.int32, (size, size), 0)
    c = lax.broadcasted_iota(jnp.int32, (size, size), 1)
    return r, c


def unit_lower_inverses(inners):
    r, c = places(128)
    eye = (r == c).astype(F32)
    n1 = [jnp.where((r // 16) == (c // 16), -a, 0.0) for a in inners]
    n2 = [mm(n, n) for n in n1]
    n4 = [mm(n, n) for n in n2]
    inv = [(eye + a) + mm(eye + a, b) for a, b in zip(n1, n2)]
    n8 = [mm(n, n) for n in n4]
    inv = [d + mm(d, n) for d, n in zip(inv, n4)]
    inv = [d + mm(d, n) for d, n in zip(inv, n8)]
    for size in (16, 32, 64):
        below = ((r // (2 * size)) == (c // (2 * size))) & ((r // size) != (c // size))
        part = [mm(jnp.where(below, a, 0.0), d) for a, d in zip(inners, inv)]
        inv = [d - mm(d, m) for d, m in zip(inv, part)]
    return inv


def unit(values):
    return values * lax.rsqrt(jnp.sum(values * values, -1, keepdims=True) + 1e-06)


def local_kernel(
    at, xq, xk, xv, rq, rk, rv, wq, wk, wv, beta, trans_out, q_out, o_out, scratch
):
    heads = range(HALF)

    def mixed(p, x, rim, w, h):
        cols = slice(h * DK, (h + 1) * DK)
        scratch[p, h, 5:8, :] = rim[:, cols].astype(F32)
        scratch[p, h, 8 : 8 + ROWS, :] = x[:, cols].astype(F32)
        acc = w[0:1, cols] * scratch[p, h, 5 : 5 + ROWS, :]
        for j in range(1, KCONV):
            acc = acc + w[j : j + 1, cols] * scratch[p, h, 5 + j : 5 + j + ROWS, :]
        return acc / (1.0 + jnp.exp(-acc))

    keys = [unit(mixed(1, xk, rk, wk, h)) for h in heads]
    queries = [unit(mixed(0, xq, rq, wq, h)) for h in heads]
    values = [mixed(2, xv, rv, wv, h) for h in heads]
    rates = [beta[h].reshape(1, ROWS) for h in heads]
    keys_t = [k.T for k in keys]
    r, c = places(ROWS)
    grams = [mmw(jnp.concatenate([q, k], 0), kt) for q, k, kt in zip(queries, keys, keys_t)]
    scores = [jnp.where(r >= c, g[:ROWS] * b, 0.0) for g, b in zip(grams, rates)]
    inner = [jnp.where(r > c, g[ROWS:] * b, 0.0) for g, b in zip(grams, rates)]
    right = [jnp.concatenate([k, v], 1) for k, v in zip(keys, values)]
    inv = unit_lower_inverses([a[:128, :128] for a in inner] + [a[128:, 128:] for a in inner])
    first = [mmw(d, x[:128]) for d, x in zip(inv[:HALF], right)]
    rest = [x[128:] - mmw(a[128:, :128], y) for x, a, y in zip(right, inner, first)]
    second = [mmw(d, z) for d, z in zip(inv[HALF:], rest)]
    solved = [jnp.concatenate([a, b], 0) for a, b in zip(first, second)]
    trans = [mmw(kt * b, y) for kt, b, y in zip(keys_t, rates, solved)]
    r, c = places(DK)
    for h in heads:
        trans_out[h, :, :DK] = jnp.where(r == c, 1.0, 0.0) - trans[h][:, :DK]
        trans_out[h, :, DK:] = trans[h][:, DK:]
    out = [mmw(s, y) for s, y in zip(scores, solved)]
    for h in heads:
        q_out[h] = queries[h] - out[h][:, :DK]
        o_out[h] = out[h][:, DK:]


def compose(later, earlier):
    m = mmw(later[:, :DK], earlier)
    return jnp.concatenate([m[:, :DK], m[:, DK:] + later[:, DK:]], 1)


def enter(trans, state):
    return mm(trans[:, :DK], state) + trans[:, DK:]


def pair_kernel(at, kept, came, *outs):
    y, core = at[2], at[3]
    for d in range(4):
        j = lax.rem(y + d, 4)
        own, other = kept[j], came[j]
        outs[d][...] = compose(
            jnp.where(core == 0, other, own), jnp.where(core == 0, own, other)
        )


def ring_prefix(place, blocks, held):
    for d, block in enumerate(blocks):
        held[lax.rem(place + 4 - d, 4)] = block[...]


def y_kernel(at, b0, b1, b2, b3, total, prefixes, held):
    ring_prefix(at[2], (b0, b1, b2, b3), held)
    one = held[0]
    two = compose(held[1], one)
    upper = compose(held[3], held[2])
    prefixes[0] = one
    prefixes[1] = two
    prefixes[2] = compose(held[2], two)
    total[...] = compose(upper, two)


def x_kernel(at, b0, b1, b2, b3, total, prefix, held):
    x = at[1]
    ring_prefix(x, (b0, b1, b2, b3), held)
    one = held[0]
    two = compose(held[1], one)
    upper = compose(held[3], held[2])
    three = compose(held[2], two)
    r, c = places(DK)
    none = jnp.concatenate([jnp.where(r == c, 1.0, 0.0), jnp.zeros((DK, DK), F32)], 1)
    low = jnp.where(x == 0, none, one)
    high = jnp.where(x == 2, two, three)
    prefix[...] = jnp.where(x < 2, low, high)
    total[...] = compose(upper, two)


def z_kernel(at, b1, b2, b3, x_prefix, y_prefixes, s0, s1, s2, s3, states):
    y, z = at[2], at[0]
    state = jnp.where(z >= 3, b3[:, DK:], 0.0)
    state = enter(b2[...], state)
    state = enter(b1[...], state)
    state = enter(x_prefix[...], state)
    states[0] = state
    for i in range(3):
        states[i + 1] = enter(y_prefixes[i], state)
    for d, out in enumerate((s0, s1, s2, s3)):
        out[...] = states[lax.rem(y + d, 4)]


def core_kernel(at, kept, came, s0, s1, s2, s3, stays, goes):
    y, core = at[2], at[3]
    for d, state in enumerate((s0, s1, s2, s3)):
        j = lax.rem(y + 4 - d, 4)
        first = state[...]
        second = enter(jnp.where(core == 0, kept[j], came[j]), first)
        stays[j] = jnp.where(core == 0, first, second)
        goes[j] = jnp.where(core == 0, second, first)


def final_kernel(at, q_own, o_own, s_own, q_far, o_far, s_far, gain, out):
    core = at[3]

    def finish(q, o, s, base):
        for h in range(HALF):
            r = mm(q[h], s[h]) + o[h]
            r = r * lax.rsqrt(jnp.mean(r * r, -1, keepdims=True) + 1e-06) * gain[...]
            cols = pl.ds(pl.multiple_of((base + h) * DK, DK), DK)
            out[:, cols] = r.astype(BF16)

    finish(q_own, o_own, s_own, core * HALF)
    finish(q_far, o_far, s_far, (1 - core) * HALF)


def whole(shape):
    return pl.BlockSpec(shape, lambda *_: (0,) * len(shape))


def call(kernel, at, args, outs, scratch=(), flops=0):
    args = list(args)
    return pl.pallas_call(
        kernel,
        grid_spec=pltpu.PrefetchScalarGridSpec(
            num_scalar_prefetch=1,
            grid=(1,),
            in_specs=[whole(a.shape) for a in args],
            out_specs=[whole(o.shape) for o in outs],
            scratch_shapes=list(scratch),
        ),
        out_shape=list(outs),
        cost_estimate=pl.CostEstimate(flops=flops, bytes_accessed=2**20, transcendentals=0),
        compiler_params=pltpu.CompilerParams(vmem_limit_bytes=VMEM_BYTES),
    )(at, *args)


def local_call(at, projected, rim, weight, beta, other):
    def group(a):
        return 1 - a[3] if other else a[3]

    def cols(rows, part):
        return pl.BlockSpec((rows, HALF * DK), lambda i, a: (0, 2 * part + group(a)))

    return pl.pallas_call(
        local_kernel,
        grid_spec=pltpu.PrefetchScalarGridSpec(
            num_scalar_prefetch=1,
            grid=(1,),
            in_specs=[cols(ROWS, p) for p in range(3)]
            + [cols(KCONV - 1, p) for p in range(3)]
            + [cols(KCONV, p) for p in range(3)]
            + [pl.BlockSpec((HALF, 1, ROWS), lambda i, a: (group(a), 0, 0))],
            out_specs=[
                whole((HALF, DK, 2 * DK)),
                whole((HALF, ROWS, DK)),
                whole((HALF, ROWS, DK)),
            ],
            scratch_shapes=[pltpu.VMEM((3, HALF, ROWS + 8, DK), F32)],
        ),
        out_shape=[
            jax.ShapeDtypeStruct((HALF, DK, 2 * DK), F32),
            jax.ShapeDtypeStruct((HALF, ROWS, DK), F32),
            jax.ShapeDtypeStruct((HALF, ROWS, DK), F32),
        ],
        cost_estimate=pl.CostEstimate(
            flops=4 * 10**9, bytes_accessed=3 * 2**20, transcendentals=10**6
        ),
        compiler_params=pltpu.CompilerParams(vmem_limit_bytes=VMEM_BYTES),
    )(at, *[projected] * 3, *[rim] * 3, *[weight] * 3, beta)


def swap(block):
    return lax.ppermute(block, "core", [(0, 1), (1, 0)])


def shift(block, axis, distance, wrap=True):
    n = lax.axis_size(axis)
    route = [(i, (i + distance) % n) for i in range(n) if wrap or i + distance < n]
    return lax.ppermute(block, axis, route)


def shards(projected, weight, beta, gain):
    at = jnp.stack([lax.axis_index(a) for a in ALL]).astype(jnp.int32)
    count = lax.axis_size(ALL)
    rim = lax.ppermute(
        projected[ROWS - (KCONV - 1) :], ALL, [(i, i + 1) for i in range(count - 1)]
    )
    beta = beta.reshape(H, 1, ROWS)
    sent, q_far, o_far = local_call(at, projected, rim, weight, beta, True)
    came = swap(sent)
    kept, q_own, o_own = local_call(at, projected, rim, weight, beta, False)

    block = jax.ShapeDtypeStruct((DK, 2 * DK), F32)
    state = jax.ShapeDtypeStruct((DK, DK), F32)
    three = jax.ShapeDtypeStruct((3, DK, 2 * DK), F32)
    held = pltpu.VMEM((4, DK, 2 * DK), F32)
    chip = call(pair_kernel, at, (kept, came), [block] * 4)
    ring = [chip[0]] + [shift(chip[d], "y", d) for d in (1, 2, 3)]
    total, y_prefixes = call(y_kernel, at, ring, [block, three], [held])
    ring = [total] + [shift(total, "x", d) for d in (1, 2, 3)]
    total, x_prefix = call(x_kernel, at, ring, [block, block], [held])
    line = [shift(total, "z", d, False) for d in (1, 2, 3)]
    states = call(
        z_kernel,
        at,
        (*line, x_prefix, y_prefixes),
        [state] * 4,
        [pltpu.VMEM((4, DK, DK), F32)],
    )
    states = [states[0]] + [shift(states[d], "y", d) for d in (1, 2, 3)]
    four = jax.ShapeDtypeStruct((HALF, DK, DK), F32)
    s_own, goes = call(core_kernel, at, (kept, came, *states), [four] * 2)
    s_far = swap(goes)
    (out,) = call(
        final_kernel,
        at,
        (q_own, o_own, s_own, q_far, o_far, s_far, gain.reshape(1, DK)),
        [jax.ShapeDtypeStruct((ROWS, H * DK), BF16)],
    )
    return out


def solution(mesh):
    grid = Mesh(mesh.devices.reshape(4, 4, 4, 2), ALL)
    placed = (P(ALL, None), P(), P(None, ALL), P())
    return jax.shard_map(
        shards, mesh=grid, in_specs=placed, out_specs=P(ALL, None), check_vma=False
    )
```

time: 665 us -> 75.8 us (0.11)
  waiting for transfers between devices: 329 us -> 21.1 us
  matrix products: 284 us -> 0 us
  starting transfers between devices: 4.64 us -> 32.1 us
  Pallas kernels: 0 us -> 18.3 us
  between operations: 13.8 us -> 0.13 us
  local copies, waits for them, and re-layouts: 16.9 us -> 3.73 us
  other arithmetic: 8.39 us -> 0.08 us
    all_gather x2 -> x0, waiting for transfers between devices: 328 us -> none  [carried_in(): everything = jax.tree.map(lambda part: lax.all_gather(part, axis), array)]
    dot_general x155 -> x0, matrix products: 284 us -> none  [contract(): return jnp.einsum(form, left, right, precision=lax.Precision.HIGHEST)]
    ppermute x1 -> x15, starting transfers between devices: 4.59 us -> 32.1 us  [the longest x12 25.2 us: shift(): return lax.ppermute(block, axis, route)]
    ppermute x1 -> x15, waiting for transfers between devices: 0.01 us -> 21.1 us  [the longest x12 19.8 us: shift(): return lax.ppermute(block, axis, route)]
    pallas_call x0 -> x8, Pallas kernels: none -> 18.3 us  [the longest x2 11.3 us: local_call(): pl.pallas_call(local_kernel, grid_spec=pltpu.PrefetchScalarGridSpec(num_s...]
    while x143 -> x0, local copies, waits for them, and re-layouts: 9.29 us -> none
  transfers between devices with their start and end apart: 3 -> 15, of which waited for: 2 -> 11; matrix products, arithmetic and copies ran while one was open for 1% -> 1% of each run, Pallas kernels for 0% -> 7%
where the time goes in v1:
time: 75.8 us; the launch traced here: 75.4 us
  starting transfers between devices  32.1 us (42%)
  waiting for transfers between devices  21.1 us (28%)
  Pallas kernels  18.3 us (24%)
  local copies, waits for them, and re-layouts  3.73 us (5%)
    ppermute x12, starting transfers between devices, shift(): return lax.ppermute(block, axis, route)  25.2 us
    ppermute x12, waiting for transfers between devices, shift(): return lax.ppermute(block, axis, route)  19.8 us
    pallas_call x2, Pallas kernels, local_call(): pl.pallas_call(local_kernel, grid_spec=pltpu.PrefetchScalarGridSpec(num_s...  11.3 us
    pallas_call x6, Pallas kernels, call(): pl.pallas_call(kernel, grid_spec=pltpu.PrefetchScalarGridSpec(num_scalar_...  7.02 us
    ppermute x1, starting transfers between devices, shards(): lax.ppermute(projected[ROWS - (KCONV - 1):], ALL, [(i, i + 1) for i in ra...  4.59 us
    ppermute x2, starting transfers between devices, swap(): return lax.ppermute(block, 'core', [(0, 1), (1, 0)])  2.4 us
    unnamed x6, local copies, waits for them, and re-layouts  2.21 us
  transfers between devices with their start and end apart: 15, of which 11 were waited for; matrix products, arithmetic and copies ran while one was open for 1% of the time, Pallas kernels for 7%

profile of v1, /device:TPU:1, one launch (start us, length us, event | category | flops | bytes accessed | tf_op | source)
XLA Modules:
  0.0 75.4 jit_solution(12288476822646196838)
XLA Ops:
  0.0 0.8 %slice.3 = bf16[3,3072]{1,0:T(4,128)(2,1)S(1)} slice(bf16[256,3072]{1,0:T(8,128)(2,1)} %xv.3), slice={[253:256], [0:3072]} | slice | bytes 36864 | tf_op jit(solution)/shard_map/slice | solution.py:272
  0.8 4.6 %collective-permute-start = (bf16[3,3072]{1,0:T(4,128)(2,1)S(1)}, bf16[3,3072]{1,0:T(4,128)(2,1)S(1)}, u32[]{:S(2)}, u32[]{:S(2)}) collective-permute-start(bf16[3,3072]{1,0:T(4,128)(2,1)S(1)} %slice.3), channel_id=1, source_target_pairs={{0,1},{1,2},{2,3},{3,4},{4,5},{5,6},{6,7},{7,8},{8,9},{9,10},{10,1... | collective-permute-start | bytes 55304 | tf_op jit(solution)/shard_map/ppermute | solution.py:271
  5.4 0.1 pad_add_fusion.at
  5.5 0.7 reshape.6.beta
  6.2 0.1 collective-permute-done.rq.rk.rv
  6.3 0.0 copy-start.1
  6.3 1.4 %copy-done.1 = bf16[256,3072]{1,0:T(8,128)(2,1)S(1)} copy-done((bf16[256,3072]{1,0:T(8,128)(2,1)S(1)}, bf16[256,3072]{1,0:T(8,128)(2,1)}, u32[]{:S(2)}) %copy-start.1) | copy-done | bytes 1572888
  7.8 0.0 copy-start.2
  7.8 0.8 %copy-done.2 = f32[4,3072]{1,0:T(4,128)S(1)} copy-done((f32[4,3072]{1,0:T(4,128)S(1)}, f32[4,3072]{1,0:T(4,128)}, u32[]{:S(2)}) %copy-start.2) | copy-done | bytes 49176
  8.6 5.6 %shard_map.47 = (f32[4,128,256]{2,1,0:T(8,128)S(1)}, f32[4,256,128]{2,1,0:T(8,128)S(1)}, f32[4,256,128]{2,1,0:T(8,128)S(1)}) custom-call(s32[4]{0:T(128)S(1)} %pad_add_fusion.at, bf16[256,3072]{1,0:T(8,128)(2,1)S(1)} %copy-done.1, bf16[256,3072]{1,0:T(8,128)(2,1)S(1)} %copy-done.1, bf16[256,3072]{1,0:T(8,128)(2,1)S(1)} %copy-done.1, ...), custom_call_target="tpu_custom_call" | custom-call | flops 4000000000 | bytes 3145728 | tf_op jit(solution)/shard_map/pallas_call | solution.py:230
  14.2 0.1 collective-permute-start.1
  14.3 5.7 %shard_map.46 = (f32[4,128,256]{2,1,0:T(8,128)S(1)}, f32[4,256,128]{2,1,0:T(8,128)S(1)}, f32[4,256,128]{2,1,0:T(8,128)S(1)}) custom-call(s32[4]{0:T(128)S(1)} %pad_add_fusion.at, bf16[256,3072]{1,0:T(8,128)(2,1)S(1)} %copy-done.1, bf16[256,3072]{1,0:T(8,128)(2,1)S(1)} %copy-done.1, bf16[256,3072]{1,0:T(8,128)(2,1)S(1)} %copy-done.1, ...), custom_call_target="tpu_custom_call" | custom-call | flops 4000000000 | bytes 3145728 | tf_op jit(solution)/shard_map/pallas_call | solution.py:230
  19.9 0.0 collective-permute-done.1.came
  20.0 0.9 %shard_map.48 = (f32[128,256]{1,0:T(8,128)S(1)}, f32[128,256]{1,0:T(8,128)S(1)}, f32[128,256]{1,0:T(8,128)S(1)}, f32[128,256]{1,0:T(8,128)S(1)}) custom-call(s32[4]{0:T(128)S(1)} %pad_add_fusion.at, f32[4,128,256]{2,1,0:T(8,128)S(1)} %get-tuple-element.27.kept, f32[4,128,256]{2,1,0:T(8,128)S(1)} %collective-permute-done.1.came), custom_call_target="tpu_custom_call" | custom-call | bytes 1048576 | tf_op jit(solution)/shard_map/pallas_call | solution.py:208
  20.8 2.5 %collective-permute-start.2 = (f32[128,256]{1,0:T(8,128)S(1)}, f32[128,256]{1,0:T(8,128)S(1)}, u32[]{:S(2)}, u32[]{:S(2)}) collective-permute-start(f32[128,256]{1,0:T(8,128)S(1)} %get-tuple-element.30), channel_id=1, source_target_pairs={{0,2},{2,4},{4,6},{6,0},{1,3},{3,5},{5,7},{7,1},{8,10},{10,12},{12... | collective-permute-start | bytes 393224 | tf_op jit(solution)/shard_map/ppermute | solution.py:265
  23.3 2.6 %collective-permute-start.3 = (f32[128,256]{1,0:T(8,128)S(1)}, f32[128,256]{1,0:T(8,128)S(1)}, u32[]{:S(2)}, u32[]{:S(2)}) collective-permute-start(f32[128,256]{1,0:T(8,128)S(1)} %get-tuple-element.31), channel_id=1, source_target_pairs={{0,4},{2,6},{4,0},{6,2},{1,5},{3,7},{5,1},{7,3},{8,12},{10,14},{12... | collective-permute-start | bytes 393224 | tf_op jit(solution)/shard_map/ppermute | solution.py:265
  25.9 1.1 %collective-permute-start.4 = (f32[128,256]{1,0:T(8,128)S(1)}, f32[128,256]{1,0:T(8,128)S(1)}, u32[]{:S(2)}, u32[]{:S(2)}) collective-permute-start(f32[128,256]{1,0:T(8,128)S(1)} %get-tuple-element.32), channel_id=1, source_target_pairs={{0,6},{2,0},{4,2},{6,4},{1,7},{3,1},{5,3},{7,5},{8,14},{10,8},{12,... | collective-permute-start | bytes 393224 | tf_op jit(solution)/shard_map/ppermute | solution.py:265
  27.0 1.6 %collective-permute-done.2.b1 = f32[128,256]{1,0:T(8,128)S(1)} collective-permute-done((f32[128,256]{1,0:T(8,128)S(1)}, f32[128,256]{1,0:T(8,128)S(1)}, u32[]{:S(2)}, u32[]{:S(2)}) %collective-permute-start.2) | collective-permute-done | bytes 131104 | tf_op jit(solution)/shard_map/ppermute | solution.py:265
  28.6 3.8 %collective-permute-done.3.b2 = f32[128,256]{1,0:T(8,128)S(1)} collective-permute-done((f32[128,256]{1,0:T(8,128)S(1)}, f32[128,256]{1,0:T(8,128)S(1)}, u32[]{:S(2)}, u32[]{:S(2)}) %collective-permute-start.3) | collective-permute-done | bytes 131104 | tf_op jit(solution)/shard_map/ppermute | solution.py:265
  32.4 0.0 collective-permute-done.4.b3
  32.4 0.0 copy-start
  32.4 1.0 %shard_map.49 = (f32[128,256]{1,0:T(8,128)S(1)}, f32[3,128,256]{2,1,0:T(8,128)S(1)}) custom-call(s32[4]{0:T(128)S(1)} %pad_add_fusion.at, f32[128,256]{1,0:T(8,128)S(1)} %get-tuple-element.29.b0, f32[128,256]{1,0:T(8,128)S(1)} %collective-permute-done.2.b1, f32[128,256]{1,0:T(8,128)S(1)} %collective-permute-done.3.b2, f32[128,256]{1,0:T(8,128)S(1)} %collective-permute-done.4.b3), custom_call_target="tpu_custom_call" | custom-call | bytes 1048576 | tf_op jit(solution)/shard_map/pallas_call | solution.py:208
  33.4 3.7 %collective-permute-start.7 = (f32[128,256]{1,0:T(8,128)S(1)}, f32[128,256]{1,0:T(8,128)S(1)}, u32[]{:S(2)}, u32[]{:S(2)}) collective-permute-start(f32[128,256]{1,0:T(8,128)S(1)} %get-tuple-element.33.b0), channel_id=1, source_target_pairs={{0,24},{8,0},{16,8},{24,16},{1,25},{9,1},{17,9},{25,17},{2,26},{10... | collective-permute-start | bytes 393224 | tf_op jit(solution)/shard_map/ppermute | solution.py:265
  37.1 0.5 collective-permute-start.6
  37.7 0.6 collective-permute-start.5
  38.3 1.2 %collective-permute-done.7.b3 = f32[128,256]{1,0:T(8,128)S(1)} collective-permute-done((f32[128,256]{1,0:T(8,128)S(1)}, f32[128,256]{1,0:T(8,128)S(1)}, u32[]{:S(2)}, u32[]{:S(2)}) %collective-permute-start.7) | collective-permute-done | bytes 131104 | tf_op jit(solution)/shard_map/ppermute | solution.py:265
  39.5 3.1 %collective-permute-done.6.b2 = f32[128,256]{1,0:T(8,128)S(1)} collective-permute-done((f32[128,256]{1,0:T(8,128)S(1)}, f32[128,256]{1,0:T(8,128)S(1)}, u32[]{:S(2)}, u32[]{:S(2)}) %collective-permute-start.6) | collective-permute-done | bytes 131104 | tf_op jit(solution)/shard_map/ppermute | solution.py:265
  42.6 3.6 %collective-permute-done.5.b1 = f32[128,256]{1,0:T(8,128)S(1)} collective-permute-done((f32[128,256]{1,0:T(8,128)S(1)}, f32[128,256]{1,0:T(8,128)S(1)}, u32[]{:S(2)}, u32[]{:S(2)}) %collective-permute-start.5) | collective-permute-done | bytes 131104 | tf_op jit(solution)/shard_map/ppermute | solution.py:265
  46.2 1.0 %shard_map.50 = (f32[128,256]{1,0:T(8,128)S(1)}, f32[128,256]{1,0:T(8,128)S(1)}) custom-call(s32[4]{0:T(128)S(1)} %pad_add_fusion.at, f32[128,256]{1,0:T(8,128)S(1)} %get-tuple-element.33.b0, f32[128,256]{1,0:T(8,128)S(1)} %collective-permute-done.5.b1, f32[128,256]{1,0:T(8,128)S(1)} %collective-permute-done.6.b2, f32[128,256]{1,0:T(8,128)S(1)} %collective-permute-done.7.b3), custom_call_target="tpu_custom_call" | custom-call | bytes 1048576 | tf_op jit(solution)/shard_map/pallas_call | solution.py:208
  47.2 5.7 %collective-permute-start.10 = (f32[128,256]{1,0:T(8,128)S(1)}, f32[128,256]{1,0:T(8,128)S(1)}, u32[]{:S(2)}, u32[]{:S(2)}) collective-permute-start(f32[128,256]{1,0:T(8,128)S(1)} %get-tuple-element.34), channel_id=1, source_target_pairs={{0,96},{1,97},{2,98},{3,99},{4,100},{5,101},{6,102},{7,103},{8,104... | collective-permute-start | bytes 393224 | tf_op jit(solution)/shard_map/ppermute | solution.py:265
  52.9 1.3 %collective-permute-start.9 = (f32[128,256]{1,0:T(8,128)S(1)}, f32[128,256]{1,0:T(8,128)S(1)}, u32[]{:S(2)}, u32[]{:S(2)}) collective-permute-start(f32[128,256]{1,0:T(8,128)S(1)} %get-tuple-element.34), channel_id=1, source_target_pairs={{0,64},{32,96},{1,65},{33,97},{2,66},{34,98},{3,67},{35,99},{4,68}... | collective-permute-start | bytes 393224 | tf_op jit(solution)/shard_map/ppermute | solution.py:265
  54.2 2.5 %collective-permute-start.8 = (f32[128,256]{1,0:T(8,128)S(1)}, f32[128,256]{1,0:T(8,128)S(1)}, u32[]{:S(2)}, u32[]{:S(2)}) collective-permute-start(f32[128,256]{1,0:T(8,128)S(1)} %get-tuple-element.34), channel_id=1, source_target_pairs={{0,32},{32,64},{64,96},{1,33},{33,65},{65,97},{2,34},{34,66},{66,9... | collective-permute-start | bytes 393224 | tf_op jit(solution)/shard_map/ppermute | solution.py:265
  56.7 0.0 collective-permute-done.10.b3
  56.7 0.0 collective-permute-done.9.b2
  56.8 2.4 %collective-permute-done.8.b1 = f32[128,256]{1,0:T(8,128)S(1)} collective-permute-done((f32[128,256]{1,0:T(8,128)S(1)}, f32[128,256]{1,0:T(8,128)S(1)}, u32[]{:S(2)}, u32[]{:S(2)}) %collective-permute-start.8) | collective-permute-done | bytes 131104 | tf_op jit(solution)/shard_map/ppermute | solution.py:265
  59.2 1.3 %shard_map.51 = (f32[128,128]{1,0:T(8,128)S(1)}, f32[128,128]{1,0:T(8,128)S(1)}, f32[128,128]{1,0:T(8,128)S(1)}, f32[128,128]{1,0:T(8,128)S(1)}) custom-call(s32[4]{0:T(128)S(1)} %pad_add_fusion.at, f32[128,256]{1,0:T(8,128)S(1)} %collective-permute-done.8.b1, f32[128,256]{1,0:T(8,128)S(1)} %collective-permute-done.9.b2, ...), custom_call_target="tpu_custom_call" | custom-call | bytes 1048576 | tf_op jit(solution)/shard_map/pallas_call | solution.py:208
  60.5 1.7 %collective-permute-start.11 = (f32[128,128]{1,0:T(8,128)S(1)}, f32[128,128]{1,0:T(8,128)S(1)}, u32[]{:S(2)}, u32[]{:S(2)}) collective-permute-start(f32[128,128]{1,0:T(8,128)S(1)} %get-tuple-element.38), channel_id=1, source_target_pairs={{0,2},{2,4},{4,6},{6,0},{1,3},{3,5},{5,7},{7,1},{8,10},{10,12},{12... | collective-permute-start | bytes 196616 | tf_op jit(solution)/shard_map/ppermute | solution.py:265
  62.2 3.0 %collective-permute-start.12 = (f32[128,128]{1,0:T(8,128)S(1)}, f32[128,128]{1,0:T(8,128)S(1)}, u32[]{:S(2)}, u32[]{:S(2)}) collective-permute-start(f32[128,128]{1,0:T(8,128)S(1)} %get-tuple-element.39), channel_id=1, source_target_pairs={{0,4},{2,6},{4,0},{6,2},{1,5},{3,7},{5,1},{7,3},{8,12},{10,14},{12... | collective-permute-start | bytes 196616 | tf_op jit(solution)/shard_map/ppermute | solution.py:265
  65.1 0.0 collective-permute-start.13
  65.1 0.5 collective-permute-done.11.s1
  65.6 2.0 %collective-permute-done.12.s2 = f32[128,128]{1,0:T(8,128)S(1)} collective-permute-done((f32[128,128]{1,0:T(8,128)S(1)}, f32[128,128]{1,0:T(8,128)S(1)}, u32[]{:S(2)}, u32[]{:S(2)}) %collective-permute-start.12) | collective-permute-done | bytes 65568 | tf_op jit(solution)/shard_map/ppermute | solution.py:265
  67.6 1.6 %collective-permute-done.13.s3 = f32[128,128]{1,0:T(8,128)S(1)} collective-permute-done((f32[128,128]{1,0:T(8,128)S(1)}, f32[128,128]{1,0:T(8,128)S(1)}, u32[]{:S(2)}, u32[]{:S(2)}) %collective-permute-start.13) | collective-permute-done | bytes 65568 | tf_op jit(solution)/shard_map/ppermute | solution.py:265
  69.2 0.8 %shard_map.52 = (f32[4,128,128]{2,1,0:T(8,128)S(1)}, f32[4,128,128]{2,1,0:T(8,128)S(1)}) custom-call(s32[4]{0:T(128)S(1)} %pad_add_fusion.at, f32[4,128,256]{2,1,0:T(8,128)S(1)} %get-tuple-element.27.kept, f32[4,128,256]{2,1,0:T(8,128)S(1)} %collective-permute-done.1.came, f32[128,128]{1,0:T(8,128)S(1)} %get-tuple-element.37.s0, ...), custom_call_target="tpu_custom_call" | custom-call | bytes 1048576 | tf_op jit(solution)/shard_map/pallas_call | solution.py:208
  70.0 2.3 %collective-permute-start.14 = (f32[4,128,128]{2,1,0:T(8,128)S(1)}, f32[4,128,128]{2,1,0:T(8,128)S(1)}, u32[]{:S(2)}, u32[]{:S(2)}) collective-permute-start(f32[4,128,128]{2,1,0:T(8,128)S(1)} %get-tuple-element.44), channel_id=1, source_target_pairs={{0,1},{1,0},{2,3},{3,2},{4,5},{5,4},{6,7},{7,6},{8,9},{9,8},{10,11... | collective-permute-start | bytes 786440 | tf_op jit(solution)/shard_map/ppermute | solution.py:259
  72.3 1.2 %collective-permute-done.14.s_far = f32[4,128,128]{2,1,0:T(8,128)S(1)} collective-permute-done((f32[4,128,128]{2,1,0:T(8,128)S(1)}, f32[4,128,128]{2,1,0:T(8,128)S(1)}, u32[]{:S(2)}, u32[]{:S(2)}) %collective-permute-start.14) | collective-permute-done | bytes 262176 | tf_op jit(solution)/shard_map/ppermute | solution.py:259
  73.5 0.0 copy-done
  73.5 2.0 %shard_map.53 = bf16[256,1024]{1,0:T(8,128)(2,1)} custom-call(s32[4]{0:T(128)S(1)} %pad_add_fusion.at, f32[4,256,128]{2,1,0:T(8,128)S(1)} %get-tuple-element.25.q_own, f32[4,256,128]{2,1,0:T(8,128)S(1)} %get-tuple-element.26.o_own, f32[4,128,128]{2,1,0:T(8,128)S(1)} %get-tuple-element.41.s_own, f32[4,256,128]{2,1,0:T(8,128)S(1)} %get-tuple-element.42.q_far, ...), custom_call_target="tpu_custom_call" | custom-call | bytes 1048576 | tf_op jit(solution)/shard_map/pallas_call | solution.py:208
Async XLA Ops:
  0.8 5.5 %collective-permute-start = (bf16[3,3072]{1,0:T(4,128)(2,1)S(1)}, bf16[3,3072]{1,0:T(4,128)(2,1)S(1)}, u32[]{:S(2)}, u32[]{:S(2)}) collective-permute-start(bf16[3,3072]{1,0:T(4,128)(2,1)S(1)} %slice.3), channel_id=1, source_target_pairs={{0,1},{1,2},{2,3},{3,4},{4,5},{5,6},{6,7},{7,8},{8,9},{9,10},{10,1... | collective-permute-start | bytes 55304 | tf_op jit(solution)/shard_map/ppermute | solution.py:271
  6.3 1.4 %copy-start.1 = (bf16[256,3072]{1,0:T(8,128)(2,1)S(1)}, bf16[256,3072]{1,0:T(8,128)(2,1)}, u32[]{:S(2)}) copy-start(bf16[256,3072]{1,0:T(8,128)(2,1)} %xv.3) | copy-start | bytes 4718596
  7.8 0.8 %copy-start.2 = (f32[4,3072]{1,0:T(4,128)S(1)}, f32[4,3072]{1,0:T(4,128)}, u32[]{:S(2)}) copy-start(f32[4,3072]{1,0:T(4,128)} %wv.3) | copy-start | bytes 147460
  14.2 5.8 %collective-permute-start.1 = (f32[4,128,256]{2,1,0:T(8,128)S(1)}, f32[4,128,256]{2,1,0:T(8,128)S(1)}, u32[]{:S(2)}, u32[]{:S(2)}) collective-permute-start(f32[4,128,256]{2,1,0:T(8,128)S(1)} %get-tuple-element.28), channel_id=1, source_target_pairs={{0,1},{1,0},{2,3},{3,2},{4,5},{5,4},{6,7},{7,6},{8,9},{9,8},{10,11... | collective-permute-start | bytes 1572872 | tf_op jit(solution)/shard_map/ppermute | solution.py:259
  20.8 7.8 %collective-permute-start.2 = (f32[128,256]{1,0:T(8,128)S(1)}, f32[128,256]{1,0:T(8,128)S(1)}, u32[]{:S(2)}, u32[]{:S(2)}) collective-permute-start(f32[128,256]{1,0:T(8,128)S(1)} %get-tuple-element.30), channel_id=1, source_target_pairs={{0,2},{2,4},{4,6},{6,0},{1,3},{3,5},{5,7},{7,1},{8,10},{10,12},{12... | collective-permute-start | bytes 393224 | tf_op jit(solution)/shard_map/ppermute | solution.py:265
  23.3 9.1 %collective-permute-start.3 = (f32[128,256]{1,0:T(8,128)S(1)}, f32[128,256]{1,0:T(8,128)S(1)}, u32[]{:S(2)}, u32[]{:S(2)}) collective-permute-start(f32[128,256]{1,0:T(8,128)S(1)} %get-tuple-element.31), channel_id=1, source_target_pairs={{0,4},{2,6},{4,0},{6,2},{1,5},{3,7},{5,1},{7,3},{8,12},{10,14},{12... | collective-permute-start | bytes 393224 | tf_op jit(solution)/shard_map/ppermute | solution.py:265
  25.9 6.5 %collective-permute-start.4 = (f32[128,256]{1,0:T(8,128)S(1)}, f32[128,256]{1,0:T(8,128)S(1)}, u32[]{:S(2)}, u32[]{:S(2)}) collective-permute-start(f32[128,256]{1,0:T(8,128)S(1)} %get-tuple-element.32), channel_id=1, source_target_pairs={{0,6},{2,0},{4,2},{6,4},{1,7},{3,1},{5,3},{7,5},{8,14},{10,8},{12,... | collective-permute-start | bytes 393224 | tf_op jit(solution)/shard_map/ppermute | solution.py:265
  32.4 41.1 %copy-start = (f32[128]{0:T(128)S(1)}, f32[128]{0:T(128)}, u32[]{:S(2)}) copy-start(f32[128]{0:T(128)} %param.7) | copy-start | bytes 1540
  33.4 6.0 %collective-permute-start.7 = (f32[128,256]{1,0:T(8,128)S(1)}, f32[128,256]{1,0:T(8,128)S(1)}, u32[]{:S(2)}, u32[]{:S(2)}) collective-permute-start(f32[128,256]{1,0:T(8,128)S(1)} %get-tuple-element.33.b0), channel_id=1, source_target_pairs={{0,24},{8,0},{16,8},{24,16},{1,25},{9,1},{17,9},{25,17},{2,26},{10... | collective-permute-start | bytes 393224 | tf_op jit(solution)/shard_map/ppermute | solution.py:265
  37.1 5.4 %collective-permute-start.6 = (f32[128,256]{1,0:T(8,128)S(1)}, f32[128,256]{1,0:T(8,128)S(1)}, u32[]{:S(2)}, u32[]{:S(2)}) collective-permute-start(f32[128,256]{1,0:T(8,128)S(1)} %get-tuple-element.33.b0), channel_id=1, source_target_pairs={{0,16},{8,24},{16,0},{24,8},{1,17},{9,25},{17,1},{25,9},{2,18},{10... | collective-permute-start | bytes 393224 | tf_op jit(solution)/shard_map/ppermute | solution.py:265
  37.7 8.5 %collective-permute-start.5 = (f32[128,256]{1,0:T(8,128)S(1)}, f32[128,256]{1,0:T(8,128)S(1)}, u32[]{:S(2)}, u32[]{:S(2)}) collective-permute-start(f32[128,256]{1,0:T(8,128)S(1)} %get-tuple-element.33.b0), channel_id=1, source_target_pairs={{0,8},{8,16},{16,24},{24,0},{1,9},{9,17},{17,25},{25,1},{2,10},{10... | collective-permute-start | bytes 393224 | tf_op jit(solution)/shard_map/ppermute | solution.py:265
  47.2 9.6 %collective-permute-start.10 = (f32[128,256]{1,0:T(8,128)S(1)}, f32[128,256]{1,0:T(8,128)S(1)}, u32[]{:S(2)}, u32[]{:S(2)}) collective-permute-start(f32[128,256]{1,0:T(8,128)S(1)} %get-tuple-element.34), channel_id=1, source_target_pairs={{0,96},{1,97},{2,98},{3,99},{4,100},{5,101},{6,102},{7,103},{8,104... | collective-permute-start | bytes 393224 | tf_op jit(solution)/shard_map/ppermute | solution.py:265
  52.9 3.8 %collective-permute-start.9 = (f32[128,256]{1,0:T(8,128)S(1)}, f32[128,256]{1,0:T(8,128)S(1)}, u32[]{:S(2)}, u32[]{:S(2)}) collective-permute-start(f32[128,256]{1,0:T(8,128)S(1)} %get-tuple-element.34), channel_id=1, source_target_pairs={{0,64},{32,96},{1,65},{33,97},{2,66},{34,98},{3,67},{35,99},{4,68}... | collective-permute-start | bytes 393224 | tf_op jit(solution)/shard_map/ppermute | solution.py:265
  54.2 4.9 %collective-permute-start.8 = (f32[128,256]{1,0:T(8,128)S(1)}, f32[128,256]{1,0:T(8,128)S(1)}, u32[]{:S(2)}, u32[]{:S(2)}) collective-permute-start(f32[128,256]{1,0:T(8,128)S(1)} %get-tuple-element.34), channel_id=1, source_target_pairs={{0,32},{32,64},{64,96},{1,33},{33,65},{65,97},{2,34},{34,66},{66,9... | collective-permute-start | bytes 393224 | tf_op jit(solution)/shard_map/ppermute | solution.py:265
  60.5 5.1 %collective-permute-start.11 = (f32[128,128]{1,0:T(8,128)S(1)}, f32[128,128]{1,0:T(8,128)S(1)}, u32[]{:S(2)}, u32[]{:S(2)}) collective-permute-start(f32[128,128]{1,0:T(8,128)S(1)} %get-tuple-element.38), channel_id=1, source_target_pairs={{0,2},{2,4},{4,6},{6,0},{1,3},{3,5},{5,7},{7,1},{8,10},{10,12},{12... | collective-permute-start | bytes 196616 | tf_op jit(solution)/shard_map/ppermute | solution.py:265
  62.2 5.4 %collective-permute-start.12 = (f32[128,128]{1,0:T(8,128)S(1)}, f32[128,128]{1,0:T(8,128)S(1)}, u32[]{:S(2)}, u32[]{:S(2)}) collective-permute-start(f32[128,128]{1,0:T(8,128)S(1)} %get-tuple-element.39), channel_id=1, source_target_pairs={{0,4},{2,6},{4,0},{6,2},{1,5},{3,7},{5,1},{7,3},{8,12},{10,14},{12... | collective-permute-start | bytes 196616 | tf_op jit(solution)/shard_map/ppermute | solution.py:265
  65.1 4.1 %collective-permute-start.13 = (f32[128,128]{1,0:T(8,128)S(1)}, f32[128,128]{1,0:T(8,128)S(1)}, u32[]{:S(2)}, u32[]{:S(2)}) collective-permute-start(f32[128,128]{1,0:T(8,128)S(1)} %get-tuple-element.40), channel_id=1, source_target_pairs={{0,6},{2,0},{4,2},{6,4},{1,7},{3,1},{5,3},{7,5},{8,14},{10,8},{12,... | collective-permute-start | bytes 196616 | tf_op jit(solution)/shard_map/ppermute | solution.py:265
  70.0 3.5 %collective-permute-start.14 = (f32[4,128,128]{2,1,0:T(8,128)S(1)}, f32[4,128,128]{2,1,0:T(8,128)S(1)}, u32[]{:S(2)}, u32[]{:S(2)}) collective-permute-start(f32[4,128,128]{2,1,0:T(8,128)S(1)} %get-tuple-element.44), channel_id=1, source_target_pairs={{0,1},{1,0},{2,3},{3,2},{4,5},{5,4},{6,7},{7,6},{8,9},{9,8},{10,11... | collective-permute-start | bytes 786440 | tf_op jit(solution)/shard_map/ppermute | solution.py:259

commit v2 on v1

v2 whole, which is shorter than its diff:
```python
import functools

import jax
import jax.numpy as jnp
from jax import lax
from jax.experimental import pallas as pl
from jax.experimental.pallas import tpu as pltpu
from jax.sharding import Mesh
from jax.sharding import PartitionSpec as P

H = 8
DK = 128
KCONV = 4
HALF = H // 2
ROWS = 256
F32, BF16 = jnp.float32, jnp.bfloat16
ALL = ("z", "x", "y", "core")
VMEM_BYTES = 48 * 1024 * 1024
MIX_BYTES = 103 * 512 * 1024


def split(a):
    high = a.astype(BF16)
    return high, (a - high.astype(F32)).astype(BF16)


def dot(a, b):
    return jnp.dot(a, b, preferred_element_type=F32)


def mm(a, b):
    a_high, a_low = split(a)
    b_high, b_low = split(b)
    wide = jnp.concatenate([b_high, b_low], 1)
    r = dot(jnp.concatenate([a_high, a_low], 1), jnp.concatenate([wide, wide], 0))
    n = b.shape[1]
    return r[:, :n] + r[:, n:]


def mmw(a, b):
    a_high, a_low = split(a)
    b_high, b_low = split(b)
    if a.shape[1] == 128:
        r = dot(jnp.concatenate([a_high, a_low], 1), jnp.concatenate([b_high, b_high], 0))
        return r + dot(a_high, b_low)
    return (dot(a_high, b_high) + dot(a_low, b_high)) + dot(a_high, b_low)


def places(size):
    r = lax.broadcasted_iota(jnp.int32, (size, size), 0)
    c = lax.broadcasted_iota(jnp.int32, (size, size), 1)
    return r, c


def mm64(a, b):
    high = a.astype(BF16)
    wide = high.astype(F32)
    both = (wide + pltpu.roll(a - wide, 64, 1)).astype(BF16)
    b_high, b_low = split(b)
    return dot(
        jnp.concatenate([both, high], 1), jnp.concatenate([b_high, b_high, b_low, b_low], 0)
    )


def alternate(a, size):
    return jnp.concatenate([a[i : i + size] for i in range(size, 128, 2 * size)], 0)


def between(upper, lower, size):
    parts = []
    for i in range(0, 64, size):
        parts += [upper[i : i + size], lower[i : i + size]]
    return jnp.concatenate(parts, 0)


def half_inverses(inners):
    r, c = places(128)
    lane = lax.broadcasted_iota(jnp.int32, (16, 128), 1)
    row = lax.broadcasted_iota(jnp.int32, (16, 128), 0)
    folded = []
    for a in inners:
        f = jnp.zeros((16, 128), F32)
        for b in range(8):
            f = jnp.where(lane // 16 == b, a[16 * b : 16 * b + 16], f)
        folded.append(f)
    inv = [jnp.where(row == lane % 16, 1.0, 0.0)] * len(inners)
    for j in range(15):
        spread = (lane // 16) * 16 + j
        inv = [
            x
            - jnp.where(
                row > j, jnp.take_along_axis(f, spread, axis=1, mode="promise_in_bounds"), 0.0
            )
            * x[j : j + 1]
            for f, x in zip(folded, inv)
        ]
    inv = [jnp.where(r // 16 == c // 16, jnp.concatenate([x] * 8, 0), 0.0) for x in inv]
    zero = jnp.zeros((64, 128), F32)
    for size in (16, 32):
        below = ((r // (2 * size)) == (c // (2 * size))) & ((r // size) != (c // size))
        part = [mm(alternate(jnp.where(below, a, 0.0), size), d) for a, d in zip(inners, inv)]
        low = [
            alternate(d, size) - mm(alternate(d, size), between(zero, m, size))
            for d, m in zip(inv, part)
        ]
        inv = [
            between(
                jnp.concatenate([d[i : i + size] for i in range(0, 128, 2 * size)], 0), x, size
            )
            for d, x in zip(inv, low)
        ]
    return inv


def unit(values):
    return values * lax.rsqrt(jnp.sum(values * values, -1, keepdims=True) + 1e-06)


def silu(a):
    return a / (1.0 + jnp.exp(-a))


def taps(w, rows, scratch, count):
    acc = w[0:1, :] * scratch[5 : 5 + count, :]
    for j in range(1, KCONV):
        acc = acc + w[j : j + 1, :] * scratch[5 + j : 5 + j + count, :]
    return silu(acc)


def columns(h):
    return slice(h * DK, (h + 1) * DK)


HEADS = range(HALF)


def mix_kernel(at, x_all, w_all, keys_out, values_out, x_out, w_out, x_in, scratch, sems):
    copies = []
    for g in range(2):
        for p in range(2):
            begin = pl.multiple_of(
                ((p + 1) * H + half_of(at, g == 0) * HALF) * DK, HALF * DK
            )
            one = pltpu.make_async_copy(
                w_all.at[:, pl.ds(begin, HALF * DK)], w_out.at[g, p], sems.at[0, g, p]
            )
            one.start()
            two = pltpu.make_async_copy(
                x_all.at[:, pl.ds(begin, HALF * DK)], x_in.at[g, p], sems.at[1, g, p]
            )
            two.start()
            copies.append((one, two))
    for g in range(2):
        for p in range(2):
            for copy in copies[2 * g + p]:
                copy.wait()
            for h in HEADS:
                held = scratch.at[g, p, h]
                held[0:8, :] = jnp.zeros((8, DK), F32)
                held[8 : 8 + ROWS, :] = x_in[g, p, :, columns(h)].astype(F32)
                x_out[g, p, :, columns(h)] = held[8:16, :]
                m = taps(w_out[g, p, :, columns(h)], ROWS, held, ROWS)
                if p == 0:
                    keys_out[g * HALF + h] = unit(m)
                else:
                    values_out[g * HALF + h] = m


def first_rows(rim, x, w, scratch, h):
    scratch[5:8, :] = rim[:, columns(h)].astype(F32)
    scratch[8:16, :] = x[:, columns(h)]
    return taps(w[:, columns(h)], 8, scratch, 8)


def local_kernel(
    at, keys_in, values_in, x, w, rk, rv, beta, trans_out, keys_out, solved_out, scratch, *, other
):
    half = half_of(at, other)
    keys = [
        jnp.concatenate(
            [unit(first_rows(rk, x.at[0, 0], w.at[0, 0], scratch.at[0, h], h)), keys_in[h, 8:, :]], 0
        )
        for h in HEADS
    ]
    values = [
        jnp.concatenate(
            [first_rows(rv, x.at[0, 1], w.at[0, 1], scratch.at[1, h], h), values_in[h, 8:, :]], 0
        )
        for h in HEADS
    ]
    keys_t = [k.T * beta[pl.ds(half * HALF + h, 1), :] for h, k in zip(HEADS, keys)]
    r, c = places(128)
    strict = r > c
    top = [jnp.where(strict, mm(k[:128], kt[:, :128]), 0.0) for k, kt in zip(keys, keys_t)]
    below = [mmw(k[128:], kt) for k, kt in zip(keys, keys_t)]
    inner = top + [jnp.where(strict, a[:, 128:], 0.0) for a in below]
    right = [jnp.concatenate([k, v], 1) for k, v in zip(keys, values)]
    inv = half_inverses(inner)
    left = lax.broadcasted_iota(jnp.int32, (64, 128), 1) < 64

    def solve(diagonal, strictly, x):
        first = [mm64(d[:64], b[:64]) for d, b in zip(diagonal, x)]
        rest = [
            b[64:] - mm64(jnp.where(left, a[64:], 0.0), y) for b, a, y in zip(x, strictly, first)
        ]
        second = [mm64(d[64:], z) for d, z in zip(diagonal, rest)]
        return [jnp.concatenate([a, b], 0) for a, b in zip(first, second)]

    first = solve(inv[:HALF], inner[:HALF], [x[:128] for x in right])
    rest = [x[128:] - mmw(a[:, :128], y) for x, a, y in zip(right, below, first)]
    second = solve(inv[HALF:], inner[HALF:], rest)
    solved = [jnp.concatenate([a, b], 0) for a, b in zip(first, second)]
    trans = [mmw(kt, y) for kt, y in zip(keys_t, solved)]
    for h in HEADS:
        trans_out[h, :, :DK] = jnp.where(r == c, 1.0, 0.0) - trans[h][:, :DK]
        trans_out[h, :, DK:] = trans[h][:, DK:]
        keys_out[h] = keys_t[h]
        solved_out[h] = solved[h]


def output_kernel(at, xq, rq, wq, keys_t, solved, q_out, o_out, token, scratch):
    token[...] = jnp.zeros_like(token)
    queries = []
    for h in HEADS:
        held = scratch.at[h]
        held[5:8, :] = rq[:, columns(h)].astype(F32)
        held[8 : 8 + ROWS, :] = xq[:, columns(h)].astype(F32)
        queries.append(unit(taps(wq[:, columns(h)], ROWS, held, ROWS)))
    r, c = places(ROWS)
    scores = [jnp.where(r >= c, mmw(q, keys_t[h]), 0.0) for h, q in zip(HEADS, queries)]
    out = [mmw(s, solved[h]) for h, s in zip(HEADS, scores)]
    for h in HEADS:
        q_out[h] = queries[h] - out[h][:, :DK]
        o_out[h] = out[h][:, DK:]


def compose(later, earlier):
    m = mmw(later[:, :DK], earlier)
    return jnp.concatenate([m[:, :DK], m[:, DK:] + later[:, DK:]], 1)


def enter(trans, state):
    return mm(trans[:, :DK], state) + trans[:, DK:]


def ordered(own_first, own, other):
    return jnp.where(own_first, other, own), jnp.where(own_first, own, other)


def chip_kernel(at, kept, came, *outs):
    for d in range(4):
        j = lax.rem(at[2] + d, 4)
        outs[d][...] = compose(*ordered(at[3] == 0, kept[j], came[j]))


def y_kernel(at, b0, b1, b2, b3, total, prefixes, held):
    y = at[2]
    for d, block in enumerate((b0, b1, b2, b3)):
        held[lax.rem(y + 4 - d, 4)] = block[...]
    one = held[0]
    two = compose(held[1], one)
    upper = compose(held[3], held[2])
    prefixes[0] = one
    prefixes[1] = two
    prefixes[2] = compose(held[2], two)
    total[...] = compose(upper, two)


def x_kernel(at, b0, b1, b2, b3, total, prefix, held):
    x = at[1]
    for d, block in enumerate((b0, b1, b2, b3)):
        held[lax.rem(x + 4 - d, 4)] = block[...]
    one = held[0]
    two = compose(held[1], one)
    upper = compose(held[3], held[2])
    three = compose(held[2], two)
    r, c = places(DK)
    none = jnp.concatenate([jnp.where(r == c, 1.0, 0.0), jnp.zeros((DK, DK), F32)], 1)
    prefix[...] = jnp.where(
        x < 2, jnp.where(x == 0, none, one), jnp.where(x == 2, two, three)
    )
    total[...] = compose(upper, two)


def z_kernel(at, b1, b2, b3, x_prefix, y_prefixes, s0, s1, s2, s3, states):
    y, z = at[2], at[0]
    state = jnp.where(z >= 3, b3[:, DK:], 0.0)
    state = jnp.where(z >= 2, enter(b2[...], state), 0.0)
    state = jnp.where(z >= 1, enter(b1[...], state), 0.0)
    state = enter(x_prefix[...], state)
    states[0] = state
    for i in range(3):
        states[i + 1] = enter(y_prefixes[i], state)
    for d, out in enumerate((s0, s1, s2, s3)):
        out[...] = states[lax.rem(y + d, 4)]


def core_kernel(at, kept, came, s0, s1, s2, s3, stays, goes):
    y, low = at[2], at[3] == 0
    for d, state in enumerate((s0, s1, s2, s3)):
        j = lax.rem(y + 4 - d, 4)
        first = state[...]
        second = enter(jnp.where(low, kept[j], came[j]), first)
        stays[j] = jnp.where(low, first, second)
        goes[j] = jnp.where(low, second, first)


def finished(q, o, s, gain, h):
    r = mm(q[h], s[h]) + o[h]
    return (r * lax.rsqrt(jnp.mean(r * r, -1, keepdims=True) + 1e-06) * gain[...]).astype(BF16)


def final_own_kernel(at, q, o, s, gain, out):
    for h in HEADS:
        out[:, columns(h)] = finished(q, o, s, gain, h)


def final_kernel(at, q, o, s, gain, own, out):
    half = HALF * DK
    out[:, pl.ds(pl.multiple_of(at[3] * half, half), half)] = own[...]
    for h in HEADS:
        begin = pl.multiple_of((1 - at[3]) * half + h * DK, DK)
        out[:, pl.ds(begin, DK)] = finished(q, o, s, gain, h)


def whole(shape):
    return pl.BlockSpec(shape, lambda *_: (0,) * len(shape))


ANYWHERE = pl.BlockSpec(memory_space=pl.ANY)


def call(
    kernel, at, args, in_specs, outs, out_specs, scratch=(), after=(), vmem=VMEM_BYTES
):
    args, after = list(args), list(after)

    def body(at_ref, *refs):
        kernel(at_ref, *refs[: len(args)], *refs[len(args) + len(after) :])

    return pl.pallas_call(
        body,
        grid_spec=pltpu.PrefetchScalarGridSpec(
            num_scalar_prefetch=1,
            grid=(1,),
            in_specs=list(in_specs) + [ANYWHERE] * len(after),
            out_specs=list(out_specs),
            scratch_shapes=list(scratch),
        ),
        out_shape=list(outs),
        cost_estimate=pl.CostEstimate(flops=10**6, bytes_accessed=2**10, transcendentals=0),
        compiler_params=pltpu.CompilerParams(vmem_limit_bytes=vmem),
    )(at, *args, *after)


def step(kernel, at, args, outs, scratch=(), after=()):
    return call(
        kernel,
        at,
        args,
        [whole(a.shape) for a in args],
        outs,
        [whole(o.shape) for o in outs],
        scratch,
        after,
    )


def half_of(a, other):
    return 1 - a[3] if other else a[3]


def cols(rows, part, other):
    return pl.BlockSpec((rows, HALF * DK), lambda i, a: (0, 2 * part + half_of(a, other)))


def shaped(*shape):
    return jax.ShapeDtypeStruct(shape, F32)


def mix_call(at, projected, weight):
    hbm = pl.BlockSpec(memory_space=pltpu.HBM)
    outs = [shaped(H, ROWS, DK)] * 2 + [shaped(2, 2, 8, HALF * DK), shaped(2, 2, KCONV, HALF * DK)]
    return call(
        mix_kernel,
        at,
        [projected, weight],
        [hbm, hbm],
        outs,
        [whole(o.shape) for o in outs],
        [
            pltpu.VMEM((2, 2, ROWS, HALF * DK), BF16),
            pltpu.VMEM((2, 2, HALF, ROWS + 8, DK), F32),
            pltpu.SemaphoreType.DMA((2, 2, 2)),
        ],
        vmem=MIX_BYTES,
    )


def local_call(at, mixes, rim, beta, other):
    keys, values, x, w = mixes
    place = int(not other)
    block = pl.BlockSpec((HALF, ROWS, DK), lambda i, a: (place, 0, 0))
    specs = [block, block]
    specs += [pl.BlockSpec((1, *a.shape[1:]), lambda i, a: (place, 0, 0, 0)) for a in (x, w)]
    specs += [cols(KCONV - 1, 1, other), cols(KCONV - 1, 2, other), whole(beta.shape)]
    outs = [shaped(HALF, DK, 2 * DK), shaped(HALF, DK, ROWS), shaped(HALF, ROWS, 2 * DK)]
    return call(
        functools.partial(local_kernel, other=other),
        at,
        [keys, values, x, w, rim, rim, beta],
        specs,
        outs,
        [whole(o.shape) for o in outs],
        [pltpu.VMEM((2, HALF, 16, DK), F32)],
    )


def output_call(at, projected, rim, weight, keys_t, solved, other):
    specs = [cols(rows, 0, other) for rows in (ROWS, KCONV - 1, KCONV)]
    specs += [whole(keys_t.shape), whole(solved.shape)]
    outs = [shaped(HALF, ROWS, DK), shaped(HALF, ROWS, DK), shaped(8, DK)]
    return call(
        output_kernel,
        at,
        [projected, rim, weight, keys_t, solved],
        specs,
        outs,
        [whole(o.shape) for o in outs],
        [pltpu.VMEM((HALF, ROWS + 8, DK), F32)],
    )


def swap(block):
    return lax.ppermute(block, "core", [(0, 1), (1, 0)])


def shift(block, axis, distance):
    n = lax.axis_size(axis)
    return lax.ppermute(block, axis, [(i, (i + distance) % n) for i in range(n)])


def shards(projected, weight, beta, gain):
    at = jnp.stack([lax.axis_index(a) for a in ALL]).astype(jnp.int32)
    count = lax.axis_size(ALL)
    rim = lax.ppermute(
        projected[ROWS - (KCONV - 1) :], ALL, [(i, i + 1) for i in range(count - 1)]
    )
    gain = gain.reshape(1, DK)
    one, state = shaped(DK, 2 * DK), shaped(DK, DK)

    mixes = mix_call(at, projected, weight)
    sent, keys_far, solved_far = local_call(at, mixes, rim, beta, True)
    came = swap(sent)
    kept, keys_own, solved_own = local_call(at, mixes, rim, beta, False)
    chip = step(chip_kernel, at, (kept, came), [one] * 4)

    held = pltpu.VMEM((4, DK, 2 * DK), F32)
    ring = [chip[0]] + [shift(chip[d], "y", d) for d in (1, 2, 3)]
    q_far, o_far, far_done = output_call(at, projected, rim, weight, keys_far, solved_far, True)
    q_own, o_own, own_done = output_call(at, projected, rim, weight, keys_own, solved_own, False)
    trans, y_prefixes = step(
        y_kernel, at, ring, [one, shaped(3, DK, 2 * DK)], [held], (far_done, own_done)
    )
    ring = [trans] + [shift(trans, "x", d) for d in (1, 2, 3)]
    trans, x_prefix = step(x_kernel, at, ring, [one, one], [held])
    before = [shift(trans, "z", d) for d in (1, 2, 3)]

    states = step(
        z_kernel,
        at,
        (*before, x_prefix, y_prefixes),
        [state] * 4,
        [pltpu.VMEM((4, DK, DK), F32)],
    )
    states = [states[0]] + [shift(states[d], "y", d) for d in (1, 2, 3)]
    s_own, goes = step(core_kernel, at, (kept, came, *states), [shaped(HALF, DK, DK)] * 2)
    s_far = swap(goes)
    half = jax.ShapeDtypeStruct((ROWS, HALF * DK), BF16)
    (own,) = step(final_own_kernel, at, (q_own, o_own, s_own, gain), [half])
    out = jax.ShapeDtypeStruct((ROWS, H * DK), BF16)
    return step(final_kernel, at, (q_far, o_far, s_far, gain, own), [out])[0]


def solution(mesh):
    grid = Mesh(mesh.devices.reshape(4, 4, 4, 2), ALL)
    placed = (P(ALL, None), P(), P(None, ALL), P())
    return jax.shard_map(
        shards, mesh=grid, in_specs=placed, out_specs=P(ALL, None), check_vma=False
    )
```

time: 75.8 us -> 68.3 us (0.901)
  waiting for transfers between devices: 21.1 us -> 14.4 us
  Pallas kernels: 18.3 us -> 21.9 us
  starting transfers between devices: 32.1 us -> 29.8 us
  local copies, waits for them, and re-layouts: 3.73 us -> 1.65 us
    ppermute x12, waiting for transfers between devices: 19.8 us -> 14.2 us  [shift(): lax.ppermute(block, axis, [(i, (i + distance) % n) for i in range(n)])]
    ppermute x12, starting transfers between devices: 25.2 us -> 20.3 us  [shift(): lax.ppermute(block, axis, [(i, (i + distance) % n) for i in range(n)])]
    pallas_call x8 -> x12, Pallas kernels: 18.3 us -> 21.9 us  [call(): pl.pallas_call(body, grid_spec=pltpu.PrefetchScalarGridSpec(num_scalar_pr...]
    ppermute x2, starting transfers between devices: 2.4 us -> 4.93 us  [swap(): return lax.ppermute(block, 'core', [(0, 1), (1, 0)])]
    unnamed x6 -> x10, local copies, waits for them, and re-layouts: 2.21 us -> 0.82 us
    ppermute x2, waiting for transfers between devices: 1.16 us -> 0.21 us  [swap(): return lax.ppermute(block, 'core', [(0, 1), (1, 0)])]
  transfers between devices with their start and end apart: 15 -> 15, of which waited for: 11 -> 10; matrix products, arithmetic and copies ran while one was open for 1% -> 0% of each run, Pallas kernels for 7% -> 17%
where the time goes in v2:
time: 68.3 us; the launch traced here: 68.1 us
  starting transfers between devices  29.8 us (44%)
  Pallas kernels  21.9 us (32%)
  waiting for transfers between devices  14.4 us (21%)
  local copies, waits for them, and re-layouts  1.65 us (2%)
    pallas_call x12, Pallas kernels, call(): pl.pallas_call(body, grid_spec=pltpu.PrefetchScalarGridSpec(num_scalar_pr...  21.9 us
    ppermute x12, starting transfers between devices, shift(): lax.ppermute(block, axis, [(i, (i + distance) % n) for i in range(n)])  20.3 us
    ppermute x12, waiting for transfers between devices, shift(): lax.ppermute(block, axis, [(i, (i + distance) % n) for i in range(n)])  14.2 us
    ppermute x2, starting transfers between devices, swap(): return lax.ppermute(block, 'core', [(0, 1), (1, 0)])  4.93 us
    ppermute x1, starting transfers between devices, shards(): lax.ppermute(projected[ROWS - (KCONV - 1):], ALL, [(i, i + 1) for i in ra...  4.59 us
  transfers between devices with their start and end apart: 15, of which 10 were waited for; matrix products, arithmetic and copies ran while one was open for 0% of the time, Pallas kernels for 17%

profile of v2, /device:TPU:1, one launch (start us, length us, event | category | flops | bytes accessed | tf_op | source)
XLA Modules:
  0.0 68.1 jit_solution(2371732761825138000)
XLA Ops:
  0.0 0.0 copy-start.3
  0.0 0.8 %slice.3 = bf16[3,3072]{1,0:T(4,128)(2,1)S(1)} slice(bf16[256,3072]{1,0:T(8,128)(2,1)} %refs_0_.5), slice={[253:256], [0:3072]} | slice | bytes 36864 | tf_op jit(solution)/shard_map/slice | solution.py:447
  0.8 4.6 %collective-permute-start = (bf16[3,3072]{1,0:T(4,128)(2,1)S(1)}, bf16[3,3072]{1,0:T(4,128)(2,1)S(1)}, u32[]{:S(2)}, u32[]{:S(2)}) collective-permute-start(bf16[3,3072]{1,0:T(4,128)(2,1)S(1)} %slice.3), channel_id=1, source_target_pairs={{0,1},{1,2},{2,3},{3,4},{4,5},{5,6},{6,7},{7,8},{8,9},{9,10},{10,1... | collective-permute-start | bytes 55304 | tf_op jit(solution)/shard_map/ppermute | solution.py:446
  5.4 0.1 pad_add_fusion.at_ref
  5.5 0.0 copy-start.1
  5.5 0.8 %copy-done.1 = f32[4,3072]{1,0:T(4,128)S(1)} copy-done((f32[4,3072]{1,0:T(4,128)S(1)}, f32[4,3072]{1,0:T(4,128)}, u32[]{:S(2)}) %copy-start.1) | copy-done | bytes 49176
  6.3 3.1 %shard_map.46 = (f32[8,256,128]{2,1,0:T(8,128)S(1)}, f32[8,256,128]{2,1,0:T(8,128)S(1)}, f32[2,2,8,512]{3,2,1,0:T(8,128)S(1)}, f32[2,2,4,512]{3,2,1,0:T(4,128)S(1)}) custom-call(s32[4]{0:T(128)S(1)} %pad_add_fusion.at_ref, bf16[256,3072]{1,0:T(8,128)(2,1)} %refs_0_.5, f32[4,3072]{1,0:T(4,128)S(1)} %copy-done.1), custom_call_target="tpu_custom_call" | custom-call | flops 1000000 | bytes 1024 | tf_op jit(solution)/shard_map/pallas_call | solution.py:341
  9.4 0.0 collective-permute-done.refs_4_.refs_5_.refs_1_
  9.4 0.0 copy-done.3
  9.4 3.8 %shard_map.47 = (f32[4,128,256]{2,1,0:T(8,128)S(1)}, f32[4,128,256]{2,1,0:T(8,128)S(1)}, f32[4,256,256]{2,1,0:T(8,128)S(1)}) custom-call(s32[4]{0:T(128)S(1)} %pad_add_fusion.at_ref, f32[8,256,128]{2,1,0:T(8,128)S(1)} %get-tuple-element.35.refs_0_, f32[8,256,128]{2,1,0:T(8,128)S(1)} %get-tuple-element.36.refs_1_, ...), custom_call_target="tpu_custom_call" | custom-call | flops 1000000 | bytes 1024 | tf_op jit(solution)/shard_map/pallas_call | solution.py:341
  13.2 0.0 copy-start
  13.2 0.0 copy-start.2
  13.2 0.1 collective-permute-start.1
  13.3 3.7 %shard_map.49 = (f32[4,128,256]{2,1,0:T(8,128)S(1)}, f32[4,128,256]{2,1,0:T(8,128)S(1)}, f32[4,256,256]{2,1,0:T(8,128)S(1)}) custom-call(s32[4]{0:T(128)S(1)} %pad_add_fusion.at_ref, f32[8,256,128]{2,1,0:T(8,128)S(1)} %get-tuple-element.35.refs_0_, f32[8,256,128]{2,1,0:T(8,128)S(1)} %get-tuple-element.36.refs_1_, ...), custom_call_target="tpu_custom_call" | custom-call | flops 1000000 | bytes 1024 | tf_op jit(solution)/shard_map/pallas_call | solution.py:341
  17.0 0.0 collective-permute-done.1.refs_1_
  17.0 0.9 %shard_map.50 = (f32[128,256]{1,0:T(8,128)S(1)}, f32[128,256]{1,0:T(8,128)S(1)}, f32[128,256]{1,0:T(8,128)S(1)}, f32[128,256]{1,0:T(8,128)S(1)}) custom-call(s32[4]{0:T(128)S(1)} %pad_add_fusion.at_ref, f32[4,128,256]{2,1,0:T(8,128)S(1)} %get-tuple-element.43.refs_0_, f32[4,128,256]{2,1,0:T(8,128)S(1)} %collective-permute-done.1.refs_1_), custom_call_target="tpu_custom_call" | custom-call | flops 1000000 | bytes 1024 | tf_op jit(solution)/shard_map/pallas_call | solution.py:341
  17.9 1.4 %collective-permute-start.2 = (f32[128,256]{1,0:T(8,128)S(1)}, f32[128,256]{1,0:T(8,128)S(1)}, u32[]{:S(2)}, u32[]{:S(2)}) collective-permute-start(f32[128,256]{1,0:T(8,128)S(1)} %get-tuple-element.46), channel_id=1, source_target_pairs={{0,2},{2,4},{4,6},{6,0},{1,3},{3,5},{5,7},{7,1},{8,10},{10,12},{12... | collective-permute-start | bytes 393224 | tf_op jit(solution)/shard_map/ppermute | solution.py:440
  19.3 2.2 %collective-permute-start.3 = (f32[128,256]{1,0:T(8,128)S(1)}, f32[128,256]{1,0:T(8,128)S(1)}, u32[]{:S(2)}, u32[]{:S(2)}) collective-permute-start(f32[128,256]{1,0:T(8,128)S(1)} %get-tuple-element.47), channel_id=1, source_target_pairs={{0,4},{2,6},{4,0},{6,2},{1,5},{3,7},{5,1},{7,3},{8,12},{10,14},{12... | collective-permute-start | bytes 393224 | tf_op jit(solution)/shard_map/ppermute | solution.py:440
  21.5 1.2 %collective-permute-start.4 = (f32[128,256]{1,0:T(8,128)S(1)}, f32[128,256]{1,0:T(8,128)S(1)}, u32[]{:S(2)}, u32[]{:S(2)}) collective-permute-start(f32[128,256]{1,0:T(8,128)S(1)} %get-tuple-element.48), channel_id=1, source_target_pairs={{0,6},{2,0},{4,2},{6,4},{1,7},{3,1},{5,3},{7,5},{8,14},{10,8},{12,... | collective-permute-start | bytes 393224 | tf_op jit(solution)/shard_map/ppermute | solution.py:440
  22.7 0.0 copy-done
  22.7 0.0 copy-done.2
  22.7 1.8 %shard_map.51 = (f32[4,256,128]{2,1,0:T(8,128)S(1)}, f32[4,256,128]{2,1,0:T(8,128)S(1)}, f32[8,128]{1,0:T(8,128)S(1)}) custom-call(s32[4]{0:T(128)S(1)} %pad_add_fusion.at_ref, bf16[256,3072]{1,0:T(8,128)(2,1)S(1)} %copy-done, bf16[3,3072]{1,0:T(4,128)(2,1)S(1)} %collective-permute-done.refs_4_.refs_5_.refs_1_, f32[4,3072]{1,0:T(4,128)S(1)} %copy-done.2, ...), custom_call_target="tpu_custom_call" | custom-call | flops 1000000 | bytes 1024 | tf_op jit(solution)/shard_map/pallas_call | solution.py:341
  24.5 1.8 %shard_map.48 = (f32[4,256,128]{2,1,0:T(8,128)S(1)}, f32[4,256,128]{2,1,0:T(8,128)S(1)}, f32[8,128]{1,0:T(8,128)S(1)}) custom-call(s32[4]{0:T(128)S(1)} %pad_add_fusion.at_ref, bf16[256,3072]{1,0:T(8,128)(2,1)S(1)} %copy-done, bf16[3,3072]{1,0:T(4,128)(2,1)S(1)} %collective-permute-done.refs_4_.refs_5_.refs_1_, f32[4,3072]{1,0:T(4,128)S(1)} %copy-done.2, ...), custom_call_target="tpu_custom_call" | custom-call | flops 1000000 | bytes 1024 | tf_op jit(solution)/shard_map/pallas_call | solution.py:341
  26.3 0.0 collective-permute-done.2.refs_1_
  26.3 1.1 %collective-permute-done.3.refs_2_ = f32[128,256]{1,0:T(8,128)S(1)} collective-permute-done((f32[128,256]{1,0:T(8,128)S(1)}, f32[128,256]{1,0:T(8,128)S(1)}, u32[]{:S(2)}, u32[]{:S(2)}) %collective-permute-start.3) | collective-permute-done | bytes 131104 | tf_op jit(solution)/shard_map/ppermute | solution.py:440
  27.4 0.0 collective-permute-done.4.refs_3_
  27.4 0.0 copy-start.4
  27.4 1.0 %shard_map.52 = (f32[128,256]{1,0:T(8,128)S(1)}, f32[3,128,256]{2,1,0:T(8,128)S(1)}) custom-call(s32[4]{0:T(128)S(1)} %pad_add_fusion.at_ref, f32[128,256]{1,0:T(8,128)S(1)} %get-tuple-element.45.refs_0_, f32[128,256]{1,0:T(8,128)S(1)} %collective-permute-done.2.refs_1_, f32[128,256]{1,0:T(8,128)S(1)} %collective-permute-done.3.refs_2_, ...), custom_call_target="tpu_custom_call" | custom-call | flops 1000000 | bytes 1024 | tf_op jit(solution)/shard_map/pallas_call | solution.py:341
  28.4 1.3 %collective-permute-start.5 = (f32[128,256]{1,0:T(8,128)S(1)}, f32[128,256]{1,0:T(8,128)S(1)}, u32[]{:S(2)}, u32[]{:S(2)}) collective-permute-start(f32[128,256]{1,0:T(8,128)S(1)} %get-tuple-element.53.refs_0_), channel_id=1, source_target_pairs={{0,8},{8,16},{16,24},{24,0},{1,9},{9,17},{17,25},{25,1},{2,10},{10... | collective-permute-start | bytes 393224 | tf_op jit(solution)/shard_map/ppermute | solution.py:440
  29.7 2.8 %collective-permute-start.6 = (f32[128,256]{1,0:T(8,128)S(1)}, f32[128,256]{1,0:T(8,128)S(1)}, u32[]{:S(2)}, u32[]{:S(2)}) collective-permute-start(f32[128,256]{1,0:T(8,128)S(1)} %get-tuple-element.53.refs_0_), channel_id=1, source_target_pairs={{0,16},{8,24},{16,0},{24,8},{1,17},{9,25},{17,1},{25,9},{2,18},{10... | collective-permute-start | bytes 393224 | tf_op jit(solution)/shard_map/ppermute | solution.py:440
  32.5 0.6 collective-permute-start.7
  33.1 0.6 collective-permute-done.5.refs_1_
  33.7 3.5 %collective-permute-done.6.refs_2_ = f32[128,256]{1,0:T(8,128)S(1)} collective-permute-done((f32[128,256]{1,0:T(8,128)S(1)}, f32[128,256]{1,0:T(8,128)S(1)}, u32[]{:S(2)}, u32[]{:S(2)}) %collective-permute-start.6) | collective-permute-done | bytes 131104 | tf_op jit(solution)/shard_map/ppermute | solution.py:440
  37.2 0.8 %collective-permute-done.7.refs_3_ = f32[128,256]{1,0:T(8,128)S(1)} collective-permute-done((f32[128,256]{1,0:T(8,128)S(1)}, f32[128,256]{1,0:T(8,128)S(1)}, u32[]{:S(2)}, u32[]{:S(2)}) %collective-permute-start.7) | collective-permute-done | bytes 131104 | tf_op jit(solution)/shard_map/ppermute | solution.py:440
  38.0 1.0 %shard_map.53 = (f32[128,256]{1,0:T(8,128)S(1)}, f32[128,256]{1,0:T(8,128)S(1)}) custom-call(s32[4]{0:T(128)S(1)} %pad_add_fusion.at_ref, f32[128,256]{1,0:T(8,128)S(1)} %get-tuple-element.53.refs_0_, f32[128,256]{1,0:T(8,128)S(1)} %collective-permute-done.5.refs_1_, f32[128,256]{1,0:T(8,128)S(1)} %collective-permute-done.6.refs_2_, ...), custom_call_target="tpu_custom_call" | custom-call | flops 1000000 | bytes 1024 | tf_op jit(solution)/shard_map/pallas_call | solution.py:341
  39.1 5.1 %collective-permute-start.10 = (f32[128,256]{1,0:T(8,128)S(1)}, f32[128,256]{1,0:T(8,128)S(1)}, u32[]{:S(2)}, u32[]{:S(2)}) collective-permute-start(f32[128,256]{1,0:T(8,128)S(1)} %get-tuple-element.54), channel_id=1, source_target_pairs={{0,96},{32,0},{64,32},{96,64},{1,97},{33,1},{65,33},{97,65},{2,98}... | collective-permute-start | bytes 393224 | tf_op jit(solution)/shard_map/ppermute | solution.py:440
  44.2 0.0 collective-permute-start.8
  44.2 1.3 %collective-permute-start.9 = (f32[128,256]{1,0:T(8,128)S(1)}, f32[128,256]{1,0:T(8,128)S(1)}, u32[]{:S(2)}, u32[]{:S(2)}) collective-permute-start(f32[128,256]{1,0:T(8,128)S(1)} %get-tuple-element.54), channel_id=1, source_target_pairs={{0,64},{32,96},{64,0},{96,32},{1,65},{33,97},{65,1},{97,33},{2,66}... | collective-permute-start | bytes 393224 | tf_op jit(solution)/shard_map/ppermute | solution.py:440
  45.5 0.6 collective-permute-done.10.refs_2_
  46.1 4.5 %collective-permute-done.8.refs_0_ = f32[128,256]{1,0:T(8,128)S(1)} collective-permute-done((f32[128,256]{1,0:T(8,128)S(1)}, f32[128,256]{1,0:T(8,128)S(1)}, u32[]{:S(2)}, u32[]{:S(2)}) %collective-permute-start.8) | collective-permute-done | bytes 131104 | tf_op jit(solution)/shard_map/ppermute | solution.py:440
  50.6 0.0 collective-permute-done.9.refs_1_
  50.6 1.3 %shard_map.54 = (f32[128,128]{1,0:T(8,128)S(1)}, f32[128,128]{1,0:T(8,128)S(1)}, f32[128,128]{1,0:T(8,128)S(1)}, f32[128,128]{1,0:T(8,128)S(1)}) custom-call(s32[4]{0:T(128)S(1)} %pad_add_fusion.at_ref, f32[128,256]{1,0:T(8,128)S(1)} %collective-permute-done.8.refs_0_, f32[128,256]{1,0:T(8,128)S(1)} %collective-permute-done.9.refs_1_, ...), custom_call_target="tpu_custom_call" | custom-call | flops 1000000 | bytes 1024 | tf_op jit(solution)/shard_map/pallas_call | solution.py:341
  51.9 1.1 %collective-permute-start.11 = (f32[128,128]{1,0:T(8,128)S(1)}, f32[128,128]{1,0:T(8,128)S(1)}, u32[]{:S(2)}, u32[]{:S(2)}) collective-permute-start(f32[128,128]{1,0:T(8,128)S(1)} %get-tuple-element.58), channel_id=1, source_target_pairs={{0,2},{2,4},{4,6},{6,0},{1,3},{3,5},{5,7},{7,1},{8,10},{10,12},{12... | collective-permute-start | bytes 196616 | tf_op jit(solution)/shard_map/ppermute | solution.py:440
  53.0 3.4 %collective-permute-start.12 = (f32[128,128]{1,0:T(8,128)S(1)}, f32[128,128]{1,0:T(8,128)S(1)}, u32[]{:S(2)}, u32[]{:S(2)}) collective-permute-start(f32[128,128]{1,0:T(8,128)S(1)} %get-tuple-element.59), channel_id=1, source_target_pairs={{0,4},{2,6},{4,0},{6,2},{1,5},{3,7},{5,1},{7,3},{8,12},{10,14},{12... | collective-permute-start | bytes 196616 | tf_op jit(solution)/shard_map/ppermute | solution.py:440
  56.4 0.0 collective-permute-start.13
  56.4 0.5 collective-permute-done.11.refs_3_
  56.9 1.9 %collective-permute-done.12.refs_4_ = f32[128,128]{1,0:T(8,128)S(1)} collective-permute-done((f32[128,128]{1,0:T(8,128)S(1)}, f32[128,128]{1,0:T(8,128)S(1)}, u32[]{:S(2)}, u32[]{:S(2)}) %collective-permute-start.12) | collective-permute-done | bytes 65568 | tf_op jit(solution)/shard_map/ppermute | solution.py:440
  58.7 0.8 %collective-permute-done.13.refs_5_ = f32[128,128]{1,0:T(8,128)S(1)} collective-permute-done((f32[128,128]{1,0:T(8,128)S(1)}, f32[128,128]{1,0:T(8,128)S(1)}, u32[]{:S(2)}, u32[]{:S(2)}) %collective-permute-start.13) | collective-permute-done | bytes 65568 | tf_op jit(solution)/shard_map/ppermute | solution.py:440
  59.5 0.8 %shard_map.55 = (f32[4,128,128]{2,1,0:T(8,128)S(1)}, f32[4,128,128]{2,1,0:T(8,128)S(1)}) custom-call(s32[4]{0:T(128)S(1)} %pad_add_fusion.at_ref, f32[4,128,256]{2,1,0:T(8,128)S(1)} %get-tuple-element.43.refs_0_, f32[4,128,256]{2,1,0:T(8,128)S(1)} %collective-permute-done.1.refs_1_, f32[128,128]{1,0:T(8,128)S(1)} %get-tuple-element.57.refs_2_, ...), custom_call_target="tpu_custom_call" | custom-call | flops 1000000 | bytes 1024 | tf_op jit(solution)/shard_map/pallas_call | solution.py:341
  60.3 4.8 %collective-permute-start.14 = (f32[4,128,128]{2,1,0:T(8,128)S(1)}, f32[4,128,128]{2,1,0:T(8,128)S(1)}, u32[]{:S(2)}, u32[]{:S(2)}) collective-permute-start(f32[4,128,128]{2,1,0:T(8,128)S(1)} %get-tuple-element.61), channel_id=1, source_target_pairs={{0,1},{1,0},{2,3},{3,2},{4,5},{5,4},{6,7},{7,6},{8,9},{9,8},{10,11... | collective-permute-start | bytes 786440 | tf_op jit(solution)/shard_map/ppermute | solution.py:435
  65.1 0.0 copy-done.4
  65.1 0.9 %shard_map.56.refs_4_ = bf16[256,512]{1,0:T(8,128)(2,1)S(1)} custom-call(s32[4]{0:T(128)S(1)} %pad_add_fusion.at_ref, f32[4,256,128]{2,1,0:T(8,128)S(1)} %get-tuple-element.62.refs_0_, f32[4,256,128]{2,1,0:T(8,128)S(1)} %get-tuple-element.63.refs_1_, f32[4,128,128]{2,1,0:T(8,128)S(1)} %get-tuple-element.64.refs_2_, f32[1,128]{1,0:T(1,128)S(1)} %bitcast.5), custom_call_target="tpu_custom_call" | custom-call | flops 1000000 | bytes 1024 | tf_op jit(solution)/shard_map/pallas_call | solution.py:341
  66.1 0.2 collective-permute-done.14.refs_2_
  66.3 1.8 %shard_map.57 = bf16[256,1024]{1,0:T(8,128)(2,1)} custom-call(s32[4]{0:T(128)S(1)} %pad_add_fusion.at_ref, f32[4,256,128]{2,1,0:T(8,128)S(1)} %get-tuple-element.41.refs_0_, f32[4,256,128]{2,1,0:T(8,128)S(1)} %get-tuple-element.42.refs_1_, f32[4,128,128]{2,1,0:T(8,128)S(1)} %collective-permute-done.14.refs_2_, f32[1,128]{1,0:T(1,128)S(1)} %bitcast.6, ...), custom_call_target="tpu_custom_call" | custom-call | flops 1000000 | bytes 1024 | tf_op jit(solution)/shard_map/pallas_call | solution.py:341
Async XLA Ops:
  0.0 9.4 %copy-start.3 = (f32[8,256]{1,0:T(8,128)S(1)}, f32[8,256]{1,0:T(8,128)}, u32[]{:S(2)}) copy-start(f32[8,256]{1,0:T(8,128)} %refs_6_.3) | copy-start | bytes 24580
  0.8 8.6 %collective-permute-start = (bf16[3,3072]{1,0:T(4,128)(2,1)S(1)}, bf16[3,3072]{1,0:T(4,128)(2,1)S(1)}, u32[]{:S(2)}, u32[]{:S(2)}) collective-permute-start(bf16[3,3072]{1,0:T(4,128)(2,1)S(1)} %slice.3), channel_id=1, source_target_pairs={{0,1},{1,2},{2,3},{3,4},{4,5},{5,6},{6,7},{7,8},{8,9},{9,10},{10,1... | collective-permute-start | bytes 55304 | tf_op jit(solution)/shard_map/ppermute | solution.py:446
  5.5 0.8 %copy-start.1 = (f32[4,3072]{1,0:T(4,128)S(1)}, f32[4,3072]{1,0:T(4,128)}, u32[]{:S(2)}) copy-start(f32[4,3072]{1,0:T(4,128)} %refs_2_.3) | copy-start | bytes 147460
  13.2 9.5 %copy-start = (bf16[256,3072]{1,0:T(8,128)(2,1)S(1)}, bf16[256,3072]{1,0:T(8,128)(2,1)}, u32[]{:S(2)}) copy-start(bf16[256,3072]{1,0:T(8,128)(2,1)} %refs_0_.5) | copy-start | bytes 4718596
  13.2 9.5 %copy-start.2 = (f32[4,3072]{1,0:T(4,128)S(1)}, f32[4,3072]{1,0:T(4,128)}, u32[]{:S(2)}) copy-start(f32[4,3072]{1,0:T(4,128)} %refs_2_.3) | copy-start | bytes 147460
  13.2 3.9 %collective-permute-start.1 = (f32[4,128,256]{2,1,0:T(8,128)S(1)}, f32[4,128,256]{2,1,0:T(8,128)S(1)}, u32[]{:S(2)}, u32[]{:S(2)}) collective-permute-start(f32[4,128,256]{2,1,0:T(8,128)S(1)} %get-tuple-element.44), channel_id=1, source_target_pairs={{0,1},{1,0},{2,3},{3,2},{4,5},{5,4},{6,7},{7,6},{8,9},{9,8},{10,11... | collective-permute-start | bytes 1572872 | tf_op jit(solution)/shard_map/ppermute | solution.py:435
  17.9 8.4 %collective-permute-start.2 = (f32[128,256]{1,0:T(8,128)S(1)}, f32[128,256]{1,0:T(8,128)S(1)}, u32[]{:S(2)}, u32[]{:S(2)}) collective-permute-start(f32[128,256]{1,0:T(8,128)S(1)} %get-tuple-element.46), channel_id=1, source_target_pairs={{0,2},{2,4},{4,6},{6,0},{1,3},{3,5},{5,7},{7,1},{8,10},{10,12},{12... | collective-permute-start | bytes 393224 | tf_op jit(solution)/shard_map/ppermute | solution.py:440
  19.3 8.1 %collective-permute-start.3 = (f32[128,256]{1,0:T(8,128)S(1)}, f32[128,256]{1,0:T(8,128)S(1)}, u32[]{:S(2)}, u32[]{:S(2)}) collective-permute-start(f32[128,256]{1,0:T(8,128)S(1)} %get-tuple-element.47), channel_id=1, source_target_pairs={{0,4},{2,6},{4,0},{6,2},{1,5},{3,7},{5,1},{7,3},{8,12},{10,14},{12... | collective-permute-start | bytes 393224 | tf_op jit(solution)/shard_map/ppermute | solution.py:440
  21.5 5.9 %collective-permute-start.4 = (f32[128,256]{1,0:T(8,128)S(1)}, f32[128,256]{1,0:T(8,128)S(1)}, u32[]{:S(2)}, u32[]{:S(2)}) collective-permute-start(f32[128,256]{1,0:T(8,128)S(1)} %get-tuple-element.48), channel_id=1, source_target_pairs={{0,6},{2,0},{4,2},{6,4},{1,7},{3,1},{5,3},{7,5},{8,14},{10,8},{12,... | collective-permute-start | bytes 393224 | tf_op jit(solution)/shard_map/ppermute | solution.py:440
  27.4 37.7 %copy-start.4 = (f32[128]{0:T(128)S(1)}, f32[128]{0:T(128)}, u32[]{:S(2)}) copy-start(f32[128]{0:T(128)} %param.7) | copy-start | bytes 1540
  28.4 5.3 %collective-permute-start.5 = (f32[128,256]{1,0:T(8,128)S(1)}, f32[128,256]{1,0:T(8,128)S(1)}, u32[]{:S(2)}, u32[]{:S(2)}) collective-permute-start(f32[128,256]{1,0:T(8,128)S(1)} %get-tuple-element.53.refs_0_), channel_id=1, source_target_pairs={{0,8},{8,16},{16,24},{24,0},{1,9},{9,17},{17,25},{25,1},{2,10},{10... | collective-permute-start | bytes 393224 | tf_op jit(solution)/shard_map/ppermute | solution.py:440
  29.7 7.5 %collective-permute-start.6 = (f32[128,256]{1,0:T(8,128)S(1)}, f32[128,256]{1,0:T(8,128)S(1)}, u32[]{:S(2)}, u32[]{:S(2)}) collective-permute-start(f32[128,256]{1,0:T(8,128)S(1)} %get-tuple-element.53.refs_0_), channel_id=1, source_target_pairs={{0,16},{8,24},{16,0},{24,8},{1,17},{9,25},{17,1},{25,9},{2,18},{10... | collective-permute-start | bytes 393224 | tf_op jit(solution)/shard_map/ppermute | solution.py:440
  32.5 5.5 %collective-permute-start.7 = (f32[128,256]{1,0:T(8,128)S(1)}, f32[128,256]{1,0:T(8,128)S(1)}, u32[]{:S(2)}, u32[]{:S(2)}) collective-permute-start(f32[128,256]{1,0:T(8,128)S(1)} %get-tuple-element.53.refs_0_), channel_id=1, source_target_pairs={{0,24},{8,0},{16,8},{24,16},{1,25},{9,1},{17,9},{25,17},{2,26},{10... | collective-permute-start | bytes 393224 | tf_op jit(solution)/shard_map/ppermute | solution.py:440
  39.1 7.0 %collective-permute-start.10 = (f32[128,256]{1,0:T(8,128)S(1)}, f32[128,256]{1,0:T(8,128)S(1)}, u32[]{:S(2)}, u32[]{:S(2)}) collective-permute-start(f32[128,256]{1,0:T(8,128)S(1)} %get-tuple-element.54), channel_id=1, source_target_pairs={{0,96},{32,0},{64,32},{96,64},{1,97},{33,1},{65,33},{97,65},{2,98}... | collective-permute-start | bytes 393224 | tf_op jit(solution)/shard_map/ppermute | solution.py:440
  44.2 6.4 %collective-permute-start.8 = (f32[128,256]{1,0:T(8,128)S(1)}, f32[128,256]{1,0:T(8,128)S(1)}, u32[]{:S(2)}, u32[]{:S(2)}) collective-permute-start(f32[128,256]{1,0:T(8,128)S(1)} %get-tuple-element.54), channel_id=1, source_target_pairs={{0,32},{32,64},{64,96},{96,0},{1,33},{33,65},{65,97},{97,1},{2,34}... | collective-permute-start | bytes 393224 | tf_op jit(solution)/shard_map/ppermute | solution.py:440
  44.2 6.4 %collective-permute-start.9 = (f32[128,256]{1,0:T(8,128)S(1)}, f32[128,256]{1,0:T(8,128)S(1)}, u32[]{:S(2)}, u32[]{:S(2)}) collective-permute-start(f32[128,256]{1,0:T(8,128)S(1)} %get-tuple-element.54), channel_id=1, source_target_pairs={{0,64},{32,96},{64,0},{96,32},{1,65},{33,97},{65,1},{97,33},{2,66}... | collective-permute-start | bytes 393224 | tf_op jit(solution)/shard_map/ppermute | solution.py:440
  51.9 4.9 %collective-permute-start.11 = (f32[128,128]{1,0:T(8,128)S(1)}, f32[128,128]{1,0:T(8,128)S(1)}, u32[]{:S(2)}, u32[]{:S(2)}) collective-permute-start(f32[128,128]{1,0:T(8,128)S(1)} %get-tuple-element.58), channel_id=1, source_target_pairs={{0,2},{2,4},{4,6},{6,0},{1,3},{3,5},{5,7},{7,1},{8,10},{10,12},{12... | collective-permute-start | bytes 196616 | tf_op jit(solution)/shard_map/ppermute | solution.py:440
  53.0 5.7 %collective-permute-start.12 = (f32[128,128]{1,0:T(8,128)S(1)}, f32[128,128]{1,0:T(8,128)S(1)}, u32[]{:S(2)}, u32[]{:S(2)}) collective-permute-start(f32[128,128]{1,0:T(8,128)S(1)} %get-tuple-element.59), channel_id=1, source_target_pairs={{0,4},{2,6},{4,0},{6,2},{1,5},{3,7},{5,1},{7,3},{8,12},{10,14},{12... | collective-permute-start | bytes 196616 | tf_op jit(solution)/shard_map/ppermute | solution.py:440
  56.4 3.1 %collective-permute-start.13 = (f32[128,128]{1,0:T(8,128)S(1)}, f32[128,128]{1,0:T(8,128)S(1)}, u32[]{:S(2)}, u32[]{:S(2)}) collective-permute-start(f32[128,128]{1,0:T(8,128)S(1)} %get-tuple-element.60), channel_id=1, source_target_pairs={{0,6},{2,0},{4,2},{6,4},{1,7},{3,1},{5,3},{7,5},{8,14},{10,8},{12,... | collective-permute-start | bytes 196616 | tf_op jit(solution)/shard_map/ppermute | solution.py:440
  60.3 6.0 %collective-permute-start.14 = (f32[4,128,128]{2,1,0:T(8,128)S(1)}, f32[4,128,128]{2,1,0:T(8,128)S(1)}, u32[]{:S(2)}, u32[]{:S(2)}) collective-permute-start(f32[4,128,128]{2,1,0:T(8,128)S(1)} %get-tuple-element.61), channel_id=1, source_target_pairs={{0,1},{1,0},{2,3},{3,2},{4,5},{5,4},{6,7},{7,6},{8,9},{9,8},{10,11... | collective-permute-start | bytes 786440 | tf_op jit(solution)/shard_map/ppermute | solution.py:435

commit v3 on v2

v3 whole, which is shorter than its diff:
```python
import functools

import jax
import jax.numpy as jnp
from jax import lax
from jax.experimental import pallas as pl
from jax.experimental.pallas import tpu as pltpu
from jax.sharding import Mesh
from jax.sharding import PartitionSpec as P

H = 8
DK = 128
KCONV = 4
HALF = H // 2
ROWS = 256
F32, BF16 = jnp.float32, jnp.bfloat16
ALL = ("z", "x", "y", "core")
VMEM_BYTES = 48 * 1024 * 1024
MIX_BYTES = 103 * 512 * 1024


def split(a):
    high = a.astype(BF16)
    return high, (a - high.astype(F32)).astype(BF16)


def dot(a, b):
    return jnp.dot(a, b, preferred_element_type=F32)


def mm(a, b):
    a_high, a_low = split(a)
    b_high, b_low = split(b)
    wide = jnp.concatenate([b_high, b_low], 1)
    r = dot(jnp.concatenate([a_high, a_low], 1), jnp.concatenate([wide, wide], 0))
    n = b.shape[1]
    return r[:, :n] + r[:, n:]


def mmw(a, b):
    a_high, a_low = split(a)
    b_high, b_low = split(b)
    if a.shape[1] == 128:
        r = dot(jnp.concatenate([a_high, a_low], 1), jnp.concatenate([b_high, b_high], 0))
        return r + dot(a_high, b_low)
    return (dot(a_high, b_high) + dot(a_low, b_high)) + dot(a_high, b_low)


def places(size):
    r = lax.broadcasted_iota(jnp.int32, (size, size), 0)
    c = lax.broadcasted_iota(jnp.int32, (size, size), 1)
    return r, c


def alternate(a, size):
    return jnp.concatenate([a[i : i + size] for i in range(size, 128, 2 * size)], 0)


def between(upper, lower, size):
    parts = []
    for i in range(0, 64, size):
        parts += [upper[i : i + size], lower[i : i + size]]
    return jnp.concatenate(parts, 0)


def unit_lower_inverses(inners):
    r, c = places(128)
    lane = lax.broadcasted_iota(jnp.int32, (16, 128), 1)
    row = lax.broadcasted_iota(jnp.int32, (16, 128), 0)
    folded = []
    for a in inners:
        f = jnp.zeros((16, 128), F32)
        for b in range(8):
            f = jnp.where(lane // 16 == b, a[16 * b : 16 * b + 16], f)
        folded.append(f)
    inv = [jnp.where(row == lane % 16, 1.0, 0.0)] * len(inners)
    for j in range(15):
        spread = (lane // 16) * 16 + j
        inv = [
            x
            - jnp.where(
                row > j, jnp.take_along_axis(f, spread, axis=1, mode="promise_in_bounds"), 0.0
            )
            * x[j : j + 1]
            for f, x in zip(folded, inv)
        ]
    inv = [jnp.where(r // 16 == c // 16, jnp.concatenate([x] * 8, 0), 0.0) for x in inv]
    zero = jnp.zeros((64, 128), F32)
    for size in (16, 32, 64):
        below = ((r // (2 * size)) == (c // (2 * size))) & ((r // size) != (c // size))
        part = [mm(alternate(jnp.where(below, a, 0.0), size), d) for a, d in zip(inners, inv)]
        low = [
            alternate(d, size) - mm(alternate(d, size), between(zero, m, size))
            for d, m in zip(inv, part)
        ]
        inv = [
            between(
                jnp.concatenate([d[i : i + size] for i in range(0, 128, 2 * size)], 0), x, size
            )
            for d, x in zip(inv, low)
        ]
    return inv


def unit(values):
    return values * lax.rsqrt(jnp.sum(values * values, -1, keepdims=True) + 1e-06)


def silu(a):
    return a / (1.0 + jnp.exp(-a))


def taps(w, rows, scratch, count):
    acc = w[0:1, :] * scratch[5 : 5 + count, :]
    for j in range(1, KCONV):
        acc = acc + w[j : j + 1, :] * scratch[5 + j : 5 + j + count, :]
    return silu(acc)


def columns(h):
    return slice(h * DK, (h + 1) * DK)


def half_of(at, other):
    return 1 - at[3] if other else at[3]


def head_columns(part, half, h):
    return pl.ds(pl.multiple_of((part * H + half * HALF + h) * DK, DK), DK)


HEADS = range(HALF)


def mix_kernel(x_in, w_in, keys_out, values_out, x_out, scratch):
    for p in range(2):
        for h in HEADS:
            held = scratch.at[p, h]
            held[0:8, :] = jnp.zeros((8, DK), F32)
            held[8 : 8 + ROWS, :] = x_in[p, :, columns(h)].astype(F32)
            x_out[p, :, columns(h)] = held[8:16, :]
            m = taps(w_in[p, :, columns(h)], ROWS, held, ROWS)
            if p == 0:
                keys_out[h] = unit(m)
            else:
                values_out[h] = m


def mix_own_kernel(at, x_in, w_in, *refs):
    mix_kernel(x_in, w_in, *refs)


def mix_far_kernel(at, x_all, w_all, *refs):
    keys_out, values_out, x_out, w_far, w_own, x_own, x_far, scratch, sems = refs
    copies = []
    for i, (other, x_to, w_to) in enumerate(((True, x_far, w_far), (False, x_own, w_own))):
        for p in range(2):
            begin = pl.multiple_of(
                ((p + 1) * H + half_of(at, other) * HALF) * DK, HALF * DK
            )
            cols = pl.ds(begin, HALF * DK)
            k = 4 * i + 2 * p
            copies.append(pltpu.make_async_copy(w_all.at[:, cols], w_to.at[p], sems.at[k]))
            copies.append(pltpu.make_async_copy(x_all.at[:, cols], x_to.at[p], sems.at[k + 1]))
    for copy in copies:
        copy.start()
    for copy in copies[:4]:
        copy.wait()
    mix_kernel(x_far, w_far, keys_out, values_out, x_out, scratch)
    for copy in copies[4:]:
        copy.wait()


def rim_of(at, rim, cols):
    first = at[0] + at[1] + at[2] + at[3] == 0
    return jnp.where(first, 0.0, rim[:, cols].astype(F32))


def first_rows(rim, x, w, scratch):
    scratch[5:8, :] = rim
    scratch[8:16, :] = x
    return taps(w, 8, scratch, 8)


def local_kernel(
    at, keys_in, values_in, x, w, rim, beta, trans_out, keys_out, solved_out, scratch, *, other
):
    half = half_of(at, other)

    def with_rim(p, h, rest):
        first = first_rows(
            rim_of(at, rim, head_columns(p + 1, half, h)),
            x[p, :, columns(h)],
            w[p, :, columns(h)],
            scratch.at[p, h],
        )
        return jnp.concatenate([unit(first) if p == 0 else first, rest[h, 8:, :]], 0)

    keys = [with_rim(0, h, keys_in) for h in HEADS]
    values = [with_rim(1, h, values_in) for h in HEADS]
    keys_t = [k.T * beta[pl.ds(half * HALF + h, 1), :] for h, k in zip(HEADS, keys)]
    r, c = places(128)
    strict = r > c
    top = [jnp.where(strict, mm(k[:128], kt[:, :128]), 0.0) for k, kt in zip(keys, keys_t)]
    below = [mmw(k[128:], kt) for k, kt in zip(keys, keys_t)]
    inner = top + [jnp.where(strict, a[:, 128:], 0.0) for a in below]
    right = [jnp.concatenate([k, v], 1) for k, v in zip(keys, values)]
    inv = unit_lower_inverses(inner)
    first = [mmw(d, x[:128]) for d, x in zip(inv[:HALF], right)]
    rest = [x[128:] - mmw(a[:, :128], y) for x, a, y in zip(right, below, first)]
    second = [mmw(d, z) for d, z in zip(inv[HALF:], rest)]
    solved = [jnp.concatenate([a, b], 0) for a, b in zip(first, second)]
    trans = [mmw(kt, y) for kt, y in zip(keys_t, solved)]
    for h in HEADS:
        trans_out[h, :, :DK] = jnp.where(r == c, 1.0, 0.0) - trans[h][:, :DK]
        trans_out[h, :, DK:] = trans[h][:, DK:]
        keys_out[h] = keys_t[h]
        solved_out[h] = solved[h]


def output_kernel(at, x, rim, w, keys_t, solved, q_out, o_out, token, scratch, *, other):
    token[...] = jnp.zeros_like(token)
    half = half_of(at, other)
    queries = []
    for h in HEADS:
        held, cols = scratch.at[h], head_columns(0, half, h)
        held[5:8, :] = rim_of(at, rim, cols)
        held[8 : 8 + ROWS, :] = x[:, cols].astype(F32)
        queries.append(unit(taps(w[:, cols], ROWS, held, ROWS)))
    r, c = places(ROWS)
    scores = [jnp.where(r >= c, mmw(q, keys_t[h]), 0.0) for h, q in zip(HEADS, queries)]
    out = [mmw(s, solved[h]) for h, s in zip(HEADS, scores)]
    for h in HEADS:
        q_out[h] = queries[h] - out[h][:, :DK]
        o_out[h] = out[h][:, DK:]


def compose(later, earlier):
    m = mmw(later[:, :DK], earlier)
    return jnp.concatenate([m[:, :DK], m[:, DK:] + later[:, DK:]], 1)


def enter(trans, state):
    return mm(trans[:, :DK], state) + trans[:, DK:]


def ordered(own_first, own, other):
    return jnp.where(own_first, other, own), jnp.where(own_first, own, other)


def chip_kernel(at, kept, came, *outs):
    for d in range(4):
        j = lax.rem(at[2] + d, 4)
        outs[d][...] = compose(*ordered(at[3] == 0, kept[j], came[j]))


def y_kernel(at, b0, b2, b1, b3, total, prefixes, held):
    y = at[2]
    for d, block in enumerate((b0, b1, b2, b3)):
        held[lax.rem(y + 4 - d, 4)] = block[...]
    one = held[0]
    two = compose(held[1], one)
    upper = compose(held[3], held[2])
    prefixes[0] = one
    prefixes[1] = two
    prefixes[2] = compose(held[2], two)
    total[...] = compose(upper, two)


def x_kernel(at, b0, b1, b3, b2, total, prefix, held):
    x = at[1]
    for d, block in enumerate((b0, b1, b2, b3)):
        held[lax.rem(x + 4 - d, 4)] = block[...]
    one = held[0]
    two = compose(held[1], one)
    upper = compose(held[3], held[2])
    three = compose(held[2], two)
    r, c = places(DK)
    none = jnp.concatenate([jnp.where(r == c, 1.0, 0.0), jnp.zeros((DK, DK), F32)], 1)
    prefix[...] = jnp.where(
        x < 2, jnp.where(x == 0, none, one), jnp.where(x == 2, two, three)
    )
    total[...] = compose(upper, two)


def z_kernel(at, b1, b3, b2, x_prefix, y_prefixes, s0, s1, s2, s3, states):
    y, z = at[2], at[0]
    state = jnp.where(z >= 3, b3[:, DK:], 0.0)
    state = jnp.where(z >= 2, enter(b2[...], state), 0.0)
    state = jnp.where(z >= 1, enter(b1[...], state), 0.0)
    state = enter(x_prefix[...], state)
    states[0] = state
    for i in range(3):
        states[i + 1] = enter(y_prefixes[i], state)
    for d, out in enumerate((s0, s1, s2, s3)):
        out[...] = states[lax.rem(y + d, 4)]


def core_kernel(at, kept, came, s0, s2, s1, s3, stays, goes):
    y, low = at[2], at[3] == 0
    for d, state in enumerate((s0, s1, s2, s3)):
        j = lax.rem(y + 4 - d, 4)
        first = state[...]
        second = enter(jnp.where(low, kept[j], came[j]), first)
        stays[j] = jnp.where(low, first, second)
        goes[j] = jnp.where(low, second, first)


def finished(q, o, s, gain, h):
    r = mm(q[h], s[h]) + o[h]
    return (r * lax.rsqrt(jnp.mean(r * r, -1, keepdims=True) + 1e-06) * gain[...]).astype(BF16)


def final_own_kernel(at, q, o, s, gain, out):
    for h in HEADS:
        out[:, columns(h)] = finished(q, o, s, gain, h)


def final_kernel(at, q, o, s, gain, own, out):
    for h in HEADS:
        out[:, head_columns(0, at[3], h)] = own[:, columns(h)]
        out[:, head_columns(0, 1 - at[3], h)] = finished(q, o, s, gain, h)


class Place:
    def __getitem__(self, i):
        return lax.axis_index(ALL[i])


def step(kernel, args, outs, scratch=(), after=(), vmem=VMEM_BYTES, hbm=()):
    args, after, hbm = list(args), list(after), list(hbm)

    def body(*refs):
        kernel(Place(), *refs[: len(args) + len(hbm)], *refs[len(args) + len(hbm) + len(after) :])

    anywhere = pl.BlockSpec(memory_space=pl.ANY)
    return pl.pallas_call(
        body,
        in_specs=[pl.BlockSpec()] * len(args) + [anywhere] * (len(hbm) + len(after)),
        out_shape=list(outs),
        scratch_shapes=list(scratch),
        cost_estimate=pl.CostEstimate(flops=10**6, bytes_accessed=2**10, transcendentals=0),
        compiler_params=pltpu.CompilerParams(vmem_limit_bytes=vmem),
    )(*args, *hbm, *after)


def shaped(*shape):
    return jax.ShapeDtypeStruct(shape, F32)


def mix_calls(projected, weight):
    mixed = [shaped(HALF, ROWS, DK)] * 2 + [shaped(2, 8, HALF * DK)]
    w, x = shaped(2, KCONV, HALF * DK), jax.ShapeDtypeStruct((2, ROWS, HALF * DK), BF16)
    room = pltpu.VMEM((2, HALF, ROWS + 8, DK), F32)
    *far, w_own, x_own = step(
        mix_far_kernel,
        (),
        [*mixed, w, w, x],
        [
            pltpu.VMEM(x.shape, BF16),
            room,
            pltpu.SemaphoreType.DMA((8,)),
        ],
        vmem=MIX_BYTES,
        hbm=(projected, weight),
    )
    own = step(mix_own_kernel, (x_own, w_own), mixed, [room])
    return far, [*own, w_own]


def local_call(mixes, rim, beta, other, after=()):
    outs = [shaped(HALF, DK, 2 * DK), shaped(HALF, DK, ROWS), shaped(HALF, ROWS, 2 * DK)]
    return step(
        functools.partial(local_kernel, other=other),
        (*mixes, rim, beta),
        outs,
        [pltpu.VMEM((2, HALF, 16, DK), F32)],
        after,
    )


def output_call(projected, rim, weight, keys_t, solved, other):
    outs = [shaped(HALF, ROWS, DK), shaped(HALF, ROWS, DK), shaped(8, DK)]
    return step(
        functools.partial(output_kernel, other=other),
        (projected, rim, weight, keys_t, solved),
        outs,
        [pltpu.VMEM((HALF, ROWS + 8, DK), F32)],
    )


def swap(block):
    return lax.ppermute(block, "core", [(0, 1), (1, 0)])


def shift(block, axis, distance):
    n = lax.axis_size(axis)
    return lax.ppermute(block, axis, [(i, (i + distance) % n) for i in range(n)])


def ring_of(blocks, axis):
    return [shift(block, axis, d + 1) for d, block in enumerate(blocks)]


def shards(projected, weight, beta, gain):
    gain = gain.reshape(1, DK)
    one, state = shaped(DK, 2 * DK), shaped(DK, DK)

    last = projected[ROWS - (KCONV - 1) :]
    count = lax.axis_size(ALL)
    rim = lax.ppermute(last, ALL, [(i, (i + 1) % count) for i in range(count)])
    mixes_far, mixes_own = mix_calls(projected, weight)
    sent, keys_far, solved_far = local_call(mixes_far, rim, beta, True, mixes_own[2:3])
    came = swap(sent)
    kept, keys_own, solved_own = local_call(mixes_own, rim, beta, False)
    chip = step(chip_kernel, (kept, came), [one] * 4)

    held = pltpu.VMEM((4, DK, 2 * DK), F32)
    b1, b2, b3 = ring_of(chip[1:], "y")
    q_far, o_far, far_done = output_call(projected, rim, weight, keys_far, solved_far, True)
    q_own, o_own, own_done = output_call(projected, rim, weight, keys_own, solved_own, False)
    trans, y_prefixes = step(
        y_kernel,
        (chip[0], b2, b1, b3),
        [one, shaped(3, DK, 2 * DK)],
        [held],
        (far_done, own_done),
    )
    b1, b2, b3 = ring_of([trans] * 3, "x")
    trans, x_prefix = step(x_kernel, (trans, b1, b3, b2), [one, one], [held])
    b1, b2, b3 = ring_of([trans] * 3, "z")

    states = step(
        z_kernel,
        (b1, b3, b2, x_prefix, y_prefixes),
        [state] * 4,
        [pltpu.VMEM((4, DK, DK), F32)],
    )
    s1, s2, s3 = ring_of(states[1:], "y")
    s_own, goes = step(core_kernel, (kept, came, states[0], s2, s1, s3), [shaped(HALF, DK, DK)] * 2)
    s_far = swap(goes)
    half = jax.ShapeDtypeStruct((ROWS, HALF * DK), BF16)
    (own,) = step(final_own_kernel, (q_own, o_own, s_own, gain), [half])
    out = jax.ShapeDtypeStruct((ROWS, H * DK), BF16)
    return step(final_kernel, (q_far, o_far, s_far, gain, own), [out])[0]


def solution(mesh):
    grid = Mesh(mesh.devices.reshape(4, 4, 4, 2), ALL)
    placed = (P(ALL, None), P(), P(None, ALL), P())
    return jax.shard_map(
        shards, mesh=grid, in_specs=placed, out_specs=P(ALL, None), check_vma=False
    )
```

time: 68.3 us -> 59.3 us (0.87)
  starting transfers between devices: 29.8 us -> 20 us
  waiting for transfers between devices: 14.4 us -> 22.2 us
  Pallas kernels: 21.9 us -> 15.1 us
    ppermute x12, starting transfers between devices: 20.3 us -> 9.84 us  [shift(): lax.ppermute(block, axis, [(i, (i + distance) % n) for i in range(n)])]
    ppermute x12, waiting for transfers between devices: 14.2 us -> 21.5 us  [shift(): lax.ppermute(block, axis, [(i, (i + distance) % n) for i in range(n)])]
    pallas_call x12 -> x13, Pallas kernels: 21.9 us -> 15.1 us  [step(): pl.pallas_call(body, in_specs=[pl.BlockSpec()] * len(args) + [anywhere] *...]
    ppermute x2, starting transfers between devices: 4.93 us -> 7.39 us  [swap(): return lax.ppermute(block, 'core', [(0, 1), (1, 0)])]
    ppermute x1, starting transfers between devices: 4.59 us -> 2.76 us  [shards(): rim = lax.ppermute(last, ALL, [(i, (i + 1) % count) for i in range(count)])]
  transfers between devices with their start and end apart: 15 -> 15, of which waited for: 10 -> 10; matrix products, arithmetic and copies ran while one was open for 0% -> 0% of each run, Pallas kernels for 17% -> 14%
where the time goes in v3:
time: 59.3 us; the launch traced here: 59.1 us
  waiting for transfers between devices  22.2 us (37%)
  starting transfers between devices  20 us (34%)
  Pallas kernels  15.1 us (25%)
  local copies, waits for them, and re-layouts  1.64 us (3%)
    ppermute x12, waiting for transfers between devices, shift(): lax.ppermute(block, axis, [(i, (i + distance) % n) for i in range(n)])  21.5 us
    pallas_call x13, Pallas kernels, step(): pl.pallas_call(body, in_specs=[pl.BlockSpec()] * len(args) + [anywhere] *...  15.1 us
    ppermute x12, starting transfers between devices, shift(): lax.ppermute(block, axis, [(i, (i + distance) % n) for i in range(n)])  9.84 us
    ppermute x2, starting transfers between devices, swap(): return lax.ppermute(block, 'core', [(0, 1), (1, 0)])  7.39 us
    ppermute x1, starting transfers between devices, shards(): rim = lax.ppermute(last, ALL, [(i, (i + 1) % count) for i in range(count)])  2.76 us
  transfers between devices with their start and end apart: 15, of which 10 were waited for; matrix products, arithmetic and copies ran while one was open for 0% of the time, Pallas kernels for 14%

profile of v3, /device:TPU:1, one launch (start us, length us, event | category | flops | bytes accessed | tf_op | source)
XLA Modules:
  0.0 59.1 jit_solution(3272398663250147671)
XLA Ops:
  0.0 0.0 copy-start.3
  0.0 0.8 %slice.3 = bf16[3,3072]{1,0:T(4,128)(2,1)S(1)} slice(bf16[256,3072]{1,0:T(8,128)(2,1)} %refs_0_.5), slice={[253:256], [0:3072]} | slice | bytes 36864 | tf_op jit(solution)/shard_map/slice | solution.py:409
  0.8 2.8 %collective-permute-start = (bf16[3,3072]{1,0:T(4,128)(2,1)S(1)}, bf16[3,3072]{1,0:T(4,128)(2,1)S(1)}, u32[]{:S(2)}, u32[]{:S(2)}) collective-permute-start(bf16[3,3072]{1,0:T(4,128)(2,1)S(1)} %slice.3), channel_id=1, source_target_pairs={{0,1},{1,2},{2,3},{3,4},{4,5},{5,6},{6,7},{7,8},{8,9},{9,10},{10,1... | collective-permute-start | bytes 55304 | tf_op jit(solution)/shard_map/ppermute | solution.py:411
  3.6 0.0 copy-start.1
  3.6 0.8 %copy-done.1 = f32[4,3072]{1,0:T(4,128)S(1)} copy-done((f32[4,3072]{1,0:T(4,128)S(1)}, f32[4,3072]{1,0:T(4,128)}, u32[]{:S(2)}) %copy-start.1) | copy-done | bytes 49176
  4.4 1.9 %shard_map.46 = (f32[4,256,128]{2,1,0:T(8,128)S(1)}, f32[4,256,128]{2,1,0:T(8,128)S(1)}, f32[2,8,512]{2,1,0:T(8,128)S(1)}, f32[2,4,512]{2,1,0:T(4,128)S(1)}, f32...) custom-call(bf16[256,3072]{1,0:T(8,128)(2,1)} %refs_0_.5, f32[4,3072]{1,0:T(4,128)S(1)} %copy-done.1), custom_call_target="tpu_custom_call" | custom-call | flops 1000000 | bytes 1024 | tf_op jit(solution)/shard_map/pallas_call | solution.py:337
  6.3 0.7 %shard_map.47 = (f32[4,256,128]{2,1,0:T(8,128)S(1)}, f32[4,256,128]{2,1,0:T(8,128)S(1)}, f32[2,8,512]{2,1,0:T(8,128)S(1)}) custom-call(bf16[2,256,512]{2,1,0:T(8,128)(2,1)S(1)} %get-tuple-element.44.refs_0_, f32[2,4,512]{2,1,0:T(4,128)S(1)} %get-tuple-element.45.refs_1_.refs_3_), custom_call_target="tpu_custom_call" | custom-call | flops 1000000 | bytes 1024 | tf_op jit(solution)/shard_map/pallas_call | solution.py:337
  7.0 0.0 collective-permute-done.refs_4_.refs_1_
  7.0 0.0 copy-done.3
  7.0 0.0 copy-start
  7.0 0.0 copy-start.2
  7.0 3.0 %shard_map.48 = (f32[4,128,256]{2,1,0:T(8,128)S(1)}, f32[4,128,256]{2,1,0:T(8,128)S(1)}, f32[4,256,256]{2,1,0:T(8,128)S(1)}) custom-call(f32[4,256,128]{2,1,0:T(8,128)S(1)} %get-tuple-element.40.refs_0_, f32[4,256,128]{2,1,0:T(8,128)S(1)} %get-tuple-element.41.refs_1_, f32[2,8,512]{2,1,0:T(8,128)S(1)} %get-tuple-element.42.refs_2_, ...), custom_call_target="tpu_custom_call" | custom-call | flops 1000000 | bytes 1024 | tf_op jit(solution)/shard_map/pallas_call | solution.py:337
  10.1 5.1 %collective-permute-start.1 = (f32[4,128,256]{2,1,0:T(8,128)S(1)}, f32[4,128,256]{2,1,0:T(8,128)S(1)}, u32[]{:S(2)}, u32[]{:S(2)}) collective-permute-start(f32[4,128,256]{2,1,0:T(8,128)S(1)} %get-tuple-element.54), channel_id=1, source_target_pairs={{0,1},{1,0},{2,3},{3,2},{4,5},{5,4},{6,7},{7,6},{8,9},{9,8},{10,11... | collective-permute-start | bytes 1572872 | tf_op jit(solution)/shard_map/ppermute | solution.py:393
  15.2 3.0 %shard_map.50 = (f32[4,128,256]{2,1,0:T(8,128)S(1)}, f32[4,128,256]{2,1,0:T(8,128)S(1)}, f32[4,256,256]{2,1,0:T(8,128)S(1)}) custom-call(f32[4,256,128]{2,1,0:T(8,128)S(1)} %get-tuple-element.51.refs_0_, f32[4,256,128]{2,1,0:T(8,128)S(1)} %get-tuple-element.52.refs_1_, f32[2,8,512]{2,1,0:T(8,128)S(1)} %get-tuple-element.46.refs_6_.refs_2_, ...), custom_call_target="tpu_custom_call" | custom-call | flops 1000000 | bytes 1024 | tf_op jit(solution)/shard_map/pallas_call | solution.py:337
  18.2 0.0 collective-permute-done.1.refs_1_
  18.2 0.3 shard_map.51
  18.6 0.1 collective-permute-start.2
  18.6 0.1 collective-permute-start.3
  18.7 2.7 %collective-permute-start.4 = (f32[128,256]{1,0:T(8,128)S(1)}, f32[128,256]{1,0:T(8,128)S(1)}, u32[]{:S(2)}, u32[]{:S(2)}) collective-permute-start(f32[128,256]{1,0:T(8,128)S(1)} %get-tuple-element.58), channel_id=1, source_target_pairs={{0,6},{2,0},{4,2},{6,4},{1,7},{3,1},{5,3},{7,5},{8,14},{10,8},{12,... | collective-permute-start | bytes 393224 | tf_op jit(solution)/shard_map/ppermute | solution.py:398
  21.4 0.0 copy-done
  21.4 0.0 copy-done.2
  21.4 1.2 %shard_map.49 = (f32[4,256,128]{2,1,0:T(8,128)S(1)}, f32[4,256,128]{2,1,0:T(8,128)S(1)}, f32[8,128]{1,0:T(8,128)S(1)}) custom-call(bf16[256,3072]{1,0:T(8,128)(2,1)S(1)} %copy-done, bf16[3,3072]{1,0:T(4,128)(2,1)S(1)} %collective-permute-done.refs_4_.refs_1_, f32[4,3072]{1,0:T(4,128)S(1)} %copy-done.2, f32[4,128,256]{2,1,0:T(8,128)S(1)} %get-tuple-element.47.refs_3_, ...), custom_call_target="tpu_custom_call" | custom-call | flops 1000000 | bytes 1024 | tf_op jit(solution)/shard_map/pallas_call | solution.py:337
  22.6 1.2 %shard_map.52 = (f32[4,256,128]{2,1,0:T(8,128)S(1)}, f32[4,256,128]{2,1,0:T(8,128)S(1)}, f32[8,128]{1,0:T(8,128)S(1)}) custom-call(bf16[256,3072]{1,0:T(8,128)(2,1)S(1)} %copy-done, bf16[3,3072]{1,0:T(4,128)(2,1)S(1)} %collective-permute-done.refs_4_.refs_1_, f32[4,3072]{1,0:T(4,128)S(1)} %copy-done.2, f32[4,128,256]{2,1,0:T(8,128)S(1)} %get-tuple-element.60.refs_3_, ...), custom_call_target="tpu_custom_call" | custom-call | flops 1000000 | bytes 1024 | tf_op jit(solution)/shard_map/pallas_call | solution.py:337
  23.9 1.4 %collective-permute-done.2.refs_1_ = f32[128,256]{1,0:T(8,128)S(1)} collective-permute-done((f32[128,256]{1,0:T(8,128)S(1)}, f32[128,256]{1,0:T(8,128)S(1)}, u32[]{:S(2)}, u32[]{:S(2)}) %collective-permute-start.2) | collective-permute-done | bytes 131104 | tf_op jit(solution)/shard_map/ppermute | solution.py:398
  25.3 2.7 %collective-permute-done.3.refs_2_ = f32[128,256]{1,0:T(8,128)S(1)} collective-permute-done((f32[128,256]{1,0:T(8,128)S(1)}, f32[128,256]{1,0:T(8,128)S(1)}, u32[]{:S(2)}, u32[]{:S(2)}) %collective-permute-start.3) | collective-permute-done | bytes 131104 | tf_op jit(solution)/shard_map/ppermute | solution.py:398
  27.9 0.0 collective-permute-done.4.refs_3_
  27.9 0.0 copy-start.4
  27.9 0.5 shard_map.53
  28.4 0.1 collective-permute-start.7
  28.5 0.1 collective-permute-start.6
  28.6 1.5 %collective-permute-start.5 = (f32[128,256]{1,0:T(8,128)S(1)}, f32[128,256]{1,0:T(8,128)S(1)}, u32[]{:S(2)}, u32[]{:S(2)}) collective-permute-start(f32[128,256]{1,0:T(8,128)S(1)} %get-tuple-element.63.refs_0_), channel_id=1, source_target_pairs={{0,8},{8,16},{16,24},{24,0},{1,9},{9,17},{17,25},{25,1},{2,10},{10... | collective-permute-start | bytes 393224 | tf_op jit(solution)/shard_map/ppermute | solution.py:398
  30.1 4.3 %collective-permute-done.7.refs_3_ = f32[128,256]{1,0:T(8,128)S(1)} collective-permute-done((f32[128,256]{1,0:T(8,128)S(1)}, f32[128,256]{1,0:T(8,128)S(1)}, u32[]{:S(2)}, u32[]{:S(2)}) %collective-permute-start.7) | collective-permute-done | bytes 131104 | tf_op jit(solution)/shard_map/ppermute | solution.py:398
  34.3 0.0 collective-permute-done.6.refs_2_
  34.3 3.9 %collective-permute-done.5.refs_1_ = f32[128,256]{1,0:T(8,128)S(1)} collective-permute-done((f32[128,256]{1,0:T(8,128)S(1)}, f32[128,256]{1,0:T(8,128)S(1)}, u32[]{:S(2)}, u32[]{:S(2)}) %collective-permute-start.5) | collective-permute-done | bytes 131104 | tf_op jit(solution)/shard_map/ppermute | solution.py:398
  38.2 0.5 shard_map.54
  38.7 0.8 %collective-permute-start.10 = (f32[128,256]{1,0:T(8,128)S(1)}, f32[128,256]{1,0:T(8,128)S(1)}, u32[]{:S(2)}, u32[]{:S(2)}) collective-permute-start(f32[128,256]{1,0:T(8,128)S(1)} %get-tuple-element.64), channel_id=1, source_target_pairs={{0,64},{32,96},{64,0},{96,32},{1,65},{33,97},{65,1},{97,33},{2,66}... | collective-permute-start | bytes 393224 | tf_op jit(solution)/shard_map/ppermute | solution.py:398
  39.5 0.4 collective-permute-start.9
  40.0 1.0 %collective-permute-start.8 = (f32[128,256]{1,0:T(8,128)S(1)}, f32[128,256]{1,0:T(8,128)S(1)}, u32[]{:S(2)}, u32[]{:S(2)}) collective-permute-start(f32[128,256]{1,0:T(8,128)S(1)} %get-tuple-element.64), channel_id=1, source_target_pairs={{0,32},{32,64},{64,96},{96,0},{1,33},{33,65},{65,97},{97,1},{2,34}... | collective-permute-start | bytes 393224 | tf_op jit(solution)/shard_map/ppermute | solution.py:398
  41.0 3.9 %collective-permute-done.10.refs_2_ = f32[128,256]{1,0:T(8,128)S(1)} collective-permute-done((f32[128,256]{1,0:T(8,128)S(1)}, f32[128,256]{1,0:T(8,128)S(1)}, u32[]{:S(2)}, u32[]{:S(2)}) %collective-permute-start.10) | collective-permute-done | bytes 131104 | tf_op jit(solution)/shard_map/ppermute | solution.py:398
  44.9 0.6 collective-permute-done.9.refs_1_
  45.5 2.5 %collective-permute-done.8.refs_0_ = f32[128,256]{1,0:T(8,128)S(1)} collective-permute-done((f32[128,256]{1,0:T(8,128)S(1)}, f32[128,256]{1,0:T(8,128)S(1)}, u32[]{:S(2)}, u32[]{:S(2)}) %collective-permute-start.8) | collective-permute-done | bytes 131104 | tf_op jit(solution)/shard_map/ppermute | solution.py:398
  48.0 0.8 %shard_map.55 = (f32[128,128]{1,0:T(8,128)S(1)}, f32[128,128]{1,0:T(8,128)S(1)}, f32[128,128]{1,0:T(8,128)S(1)}, f32[128,128]{1,0:T(8,128)S(1)}) custom-call(f32[128,256]{1,0:T(8,128)S(1)} %collective-permute-done.8.refs_0_, f32[128,256]{1,0:T(8,128)S(1)} %collective-permute-done.9.refs_1_, f32[128,256]{1,0:T(8,128)S(1)} %collective-permute-done.10.refs_2_, ...), custom_call_target="tpu_custom_call" | custom-call | flops 1000000 | bytes 1024 | tf_op jit(solution)/shard_map/pallas_call | solution.py:337
  48.7 0.5 collective-permute-start.11
  49.2 0.0 collective-permute-start.12
  49.2 2.7 %collective-permute-start.13 = (f32[128,128]{1,0:T(8,128)S(1)}, f32[128,128]{1,0:T(8,128)S(1)}, u32[]{:S(2)}, u32[]{:S(2)}) collective-permute-start(f32[128,128]{1,0:T(8,128)S(1)} %get-tuple-element.70), channel_id=1, source_target_pairs={{0,6},{2,0},{4,2},{6,4},{1,7},{3,1},{5,3},{7,5},{8,14},{10,8},{12,... | collective-permute-start | bytes 196616 | tf_op jit(solution)/shard_map/ppermute | solution.py:398
  51.9 1.6 %collective-permute-done.11.refs_3_ = f32[128,128]{1,0:T(8,128)S(1)} collective-permute-done((f32[128,128]{1,0:T(8,128)S(1)}, f32[128,128]{1,0:T(8,128)S(1)}, u32[]{:S(2)}, u32[]{:S(2)}) %collective-permute-start.11) | collective-permute-done | bytes 65568 | tf_op jit(solution)/shard_map/ppermute | solution.py:398
  53.5 0.6 %collective-permute-done.12.refs_4_ = f32[128,128]{1,0:T(8,128)S(1)} collective-permute-done((f32[128,128]{1,0:T(8,128)S(1)}, f32[128,128]{1,0:T(8,128)S(1)}, u32[]{:S(2)}, u32[]{:S(2)}) %collective-permute-start.12) | collective-permute-done | bytes 65568 | tf_op jit(solution)/shard_map/ppermute | solution.py:398
  54.2 0.0 collective-permute-done.13.refs_5_
  54.2 0.2 shard_map.56
  54.4 2.3 %collective-permute-start.14 = (f32[4,128,128]{2,1,0:T(8,128)S(1)}, f32[4,128,128]{2,1,0:T(8,128)S(1)}, u32[]{:S(2)}, u32[]{:S(2)}) collective-permute-start(f32[4,128,128]{2,1,0:T(8,128)S(1)} %get-tuple-element.71), channel_id=1, source_target_pairs={{0,1},{1,0},{2,3},{3,2},{4,5},{5,4},{6,7},{7,6},{8,9},{9,8},{10,11... | collective-permute-start | bytes 786440 | tf_op jit(solution)/shard_map/ppermute | solution.py:393
  56.7 0.0 copy-done.4
  56.7 0.4 shard_map.57.refs_4_
  57.1 0.7 %collective-permute-done.14.refs_2_ = f32[4,128,128]{2,1,0:T(8,128)S(1)} collective-permute-done((f32[4,128,128]{2,1,0:T(8,128)S(1)}, f32[4,128,128]{2,1,0:T(8,128)S(1)}, u32[]{:S(2)}, u32[]{:S(2)}) %collective-permute-start.14) | collective-permute-done | bytes 262176 | tf_op jit(solution)/shard_map/ppermute | solution.py:393
  57.9 1.2 %shard_map.58 = bf16[256,1024]{1,0:T(8,128)(2,1)} custom-call(f32[4,256,128]{2,1,0:T(8,128)S(1)} %get-tuple-element.49.refs_0_, f32[4,256,128]{2,1,0:T(8,128)S(1)} %get-tuple-element.50.refs_1_, f32[4,128,128]{2,1,0:T(8,128)S(1)} %collective-permute-done.14.refs_2_, f32[1,128]{1,0:T(1,128)S(1)} %bitcast.2, bf16[256,512]{1,0:T(8,128)(2,1)S(1)} %shard_map.57.refs_4_), custom_call_target="tpu_custom_call" | custom-call | flops 1000000 | bytes 1024 | tf_op jit(solution)/shard_map/pallas_call | solution.py:337
Async XLA Ops:
  0.0 7.0 %copy-start.3 = (f32[8,256]{1,0:T(8,128)S(1)}, f32[8,256]{1,0:T(8,128)}, u32[]{:S(2)}) copy-start(f32[8,256]{1,0:T(8,128)} %refs_5_.3) | copy-start | bytes 24580
  0.8 6.2 %collective-permute-start = (bf16[3,3072]{1,0:T(4,128)(2,1)S(1)}, bf16[3,3072]{1,0:T(4,128)(2,1)S(1)}, u32[]{:S(2)}, u32[]{:S(2)}) collective-permute-start(bf16[3,3072]{1,0:T(4,128)(2,1)S(1)} %slice.3), channel_id=1, source_target_pairs={{0,1},{1,2},{2,3},{3,4},{4,5},{5,6},{6,7},{7,8},{8,9},{9,10},{10,1... | collective-permute-start | bytes 55304 | tf_op jit(solution)/shard_map/ppermute | solution.py:411
  3.6 0.8 %copy-start.1 = (f32[4,3072]{1,0:T(4,128)S(1)}, f32[4,3072]{1,0:T(4,128)}, u32[]{:S(2)}) copy-start(f32[4,3072]{1,0:T(4,128)} %refs_2_.3) | copy-start | bytes 147460
  7.0 14.4 %copy-start = (bf16[256,3072]{1,0:T(8,128)(2,1)S(1)}, bf16[256,3072]{1,0:T(8,128)(2,1)}, u32[]{:S(2)}) copy-start(bf16[256,3072]{1,0:T(8,128)(2,1)} %refs_0_.5) | copy-start | bytes 4718596
  7.0 14.4 %copy-start.2 = (f32[4,3072]{1,0:T(4,128)S(1)}, f32[4,3072]{1,0:T(4,128)}, u32[]{:S(2)}) copy-start(f32[4,3072]{1,0:T(4,128)} %refs_2_.3) | copy-start | bytes 147460
  10.1 8.1 %collective-permute-start.1 = (f32[4,128,256]{2,1,0:T(8,128)S(1)}, f32[4,128,256]{2,1,0:T(8,128)S(1)}, u32[]{:S(2)}, u32[]{:S(2)}) collective-permute-start(f32[4,128,256]{2,1,0:T(8,128)S(1)} %get-tuple-element.54), channel_id=1, source_target_pairs={{0,1},{1,0},{2,3},{3,2},{4,5},{5,4},{6,7},{7,6},{8,9},{9,8},{10,11... | collective-permute-start | bytes 1572872 | tf_op jit(solution)/shard_map/ppermute | solution.py:393
  18.6 6.7 %collective-permute-start.2 = (f32[128,256]{1,0:T(8,128)S(1)}, f32[128,256]{1,0:T(8,128)S(1)}, u32[]{:S(2)}, u32[]{:S(2)}) collective-permute-start(f32[128,256]{1,0:T(8,128)S(1)} %get-tuple-element.56), channel_id=1, source_target_pairs={{0,4},{2,6},{4,0},{6,2},{1,5},{3,7},{5,1},{7,3},{8,12},{10,14},{12... | collective-permute-start | bytes 393224 | tf_op jit(solution)/shard_map/ppermute | solution.py:398
  18.6 9.3 %collective-permute-start.3 = (f32[128,256]{1,0:T(8,128)S(1)}, f32[128,256]{1,0:T(8,128)S(1)}, u32[]{:S(2)}, u32[]{:S(2)}) collective-permute-start(f32[128,256]{1,0:T(8,128)S(1)} %get-tuple-element.57), channel_id=1, source_target_pairs={{0,2},{2,4},{4,6},{6,0},{1,3},{3,5},{5,7},{7,1},{8,10},{10,12},{12... | collective-permute-start | bytes 393224 | tf_op jit(solution)/shard_map/ppermute | solution.py:398
  18.7 9.2 %collective-permute-start.4 = (f32[128,256]{1,0:T(8,128)S(1)}, f32[128,256]{1,0:T(8,128)S(1)}, u32[]{:S(2)}, u32[]{:S(2)}) collective-permute-start(f32[128,256]{1,0:T(8,128)S(1)} %get-tuple-element.58), channel_id=1, source_target_pairs={{0,6},{2,0},{4,2},{6,4},{1,7},{3,1},{5,3},{7,5},{8,14},{10,8},{12,... | collective-permute-start | bytes 393224 | tf_op jit(solution)/shard_map/ppermute | solution.py:398
  27.9 28.8 %copy-start.4 = (f32[128]{0:T(128)S(1)}, f32[128]{0:T(128)}, u32[]{:S(2)}) copy-start(f32[128]{0:T(128)} %param.7) | copy-start | bytes 1540
  28.4 5.9 %collective-permute-start.7 = (f32[128,256]{1,0:T(8,128)S(1)}, f32[128,256]{1,0:T(8,128)S(1)}, u32[]{:S(2)}, u32[]{:S(2)}) collective-permute-start(f32[128,256]{1,0:T(8,128)S(1)} %get-tuple-element.63.refs_0_), channel_id=1, source_target_pairs={{0,16},{8,24},{16,0},{24,8},{1,17},{9,25},{17,1},{25,9},{2,18},{10... | collective-permute-start | bytes 393224 | tf_op jit(solution)/shard_map/ppermute | solution.py:398
  28.5 5.8 %collective-permute-start.6 = (f32[128,256]{1,0:T(8,128)S(1)}, f32[128,256]{1,0:T(8,128)S(1)}, u32[]{:S(2)}, u32[]{:S(2)}) collective-permute-start(f32[128,256]{1,0:T(8,128)S(1)} %get-tuple-element.63.refs_0_), channel_id=1, source_target_pairs={{0,24},{8,0},{16,8},{24,16},{1,25},{9,1},{17,9},{25,17},{2,26},{10... | collective-permute-start | bytes 393224 | tf_op jit(solution)/shard_map/ppermute | solution.py:398
  28.6 9.6 %collective-permute-start.5 = (f32[128,256]{1,0:T(8,128)S(1)}, f32[128,256]{1,0:T(8,128)S(1)}, u32[]{:S(2)}, u32[]{:S(2)}) collective-permute-start(f32[128,256]{1,0:T(8,128)S(1)} %get-tuple-element.63.refs_0_), channel_id=1, source_target_pairs={{0,8},{8,16},{16,24},{24,0},{1,9},{9,17},{17,25},{25,1},{2,10},{10... | collective-permute-start | bytes 393224 | tf_op jit(solution)/shard_map/ppermute | solution.py:398
  38.7 6.2 %collective-permute-start.10 = (f32[128,256]{1,0:T(8,128)S(1)}, f32[128,256]{1,0:T(8,128)S(1)}, u32[]{:S(2)}, u32[]{:S(2)}) collective-permute-start(f32[128,256]{1,0:T(8,128)S(1)} %get-tuple-element.64), channel_id=1, source_target_pairs={{0,64},{32,96},{64,0},{96,32},{1,65},{33,97},{65,1},{97,33},{2,66}... | collective-permute-start | bytes 393224 | tf_op jit(solution)/shard_map/ppermute | solution.py:398
  39.5 5.9 %collective-permute-start.9 = (f32[128,256]{1,0:T(8,128)S(1)}, f32[128,256]{1,0:T(8,128)S(1)}, u32[]{:S(2)}, u32[]{:S(2)}) collective-permute-start(f32[128,256]{1,0:T(8,128)S(1)} %get-tuple-element.64), channel_id=1, source_target_pairs={{0,96},{32,0},{64,32},{96,64},{1,97},{33,1},{65,33},{97,65},{2,98}... | collective-permute-start | bytes 393224 | tf_op jit(solution)/shard_map/ppermute | solution.py:398
  40.0 8.0 %collective-permute-start.8 = (f32[128,256]{1,0:T(8,128)S(1)}, f32[128,256]{1,0:T(8,128)S(1)}, u32[]{:S(2)}, u32[]{:S(2)}) collective-permute-start(f32[128,256]{1,0:T(8,128)S(1)} %get-tuple-element.64), channel_id=1, source_target_pairs={{0,32},{32,64},{64,96},{96,0},{1,33},{33,65},{65,97},{97,1},{2,34}... | collective-permute-start | bytes 393224 | tf_op jit(solution)/shard_map/ppermute | solution.py:398
  48.7 4.8 %collective-permute-start.11 = (f32[128,128]{1,0:T(8,128)S(1)}, f32[128,128]{1,0:T(8,128)S(1)}, u32[]{:S(2)}, u32[]{:S(2)}) collective-permute-start(f32[128,128]{1,0:T(8,128)S(1)} %get-tuple-element.68), channel_id=1, source_target_pairs={{0,4},{2,6},{4,0},{6,2},{1,5},{3,7},{5,1},{7,3},{8,12},{10,14},{12... | collective-permute-start | bytes 196616 | tf_op jit(solution)/shard_map/ppermute | solution.py:398
  49.2 4.9 %collective-permute-start.12 = (f32[128,128]{1,0:T(8,128)S(1)}, f32[128,128]{1,0:T(8,128)S(1)}, u32[]{:S(2)}, u32[]{:S(2)}) collective-permute-start(f32[128,128]{1,0:T(8,128)S(1)} %get-tuple-element.69), channel_id=1, source_target_pairs={{0,2},{2,4},{4,6},{6,0},{1,3},{3,5},{5,7},{7,1},{8,10},{10,12},{12... | collective-permute-start | bytes 196616 | tf_op jit(solution)/shard_map/ppermute | solution.py:398
  49.2 4.9 %collective-permute-start.13 = (f32[128,128]{1,0:T(8,128)S(1)}, f32[128,128]{1,0:T(8,128)S(1)}, u32[]{:S(2)}, u32[]{:S(2)}) collective-permute-start(f32[128,128]{1,0:T(8,128)S(1)} %get-tuple-element.70), channel_id=1, source_target_pairs={{0,6},{2,0},{4,2},{6,4},{1,7},{3,1},{5,3},{7,5},{8,14},{10,8},{12,... | collective-permute-start | bytes 196616 | tf_op jit(solution)/shard_map/ppermute | solution.py:398
  54.4 3.5 %collective-permute-start.14 = (f32[4,128,128]{2,1,0:T(8,128)S(1)}, f32[4,128,128]{2,1,0:T(8,128)S(1)}, u32[]{:S(2)}, u32[]{:S(2)}) collective-permute-start(f32[4,128,128]{2,1,0:T(8,128)S(1)} %get-tuple-element.71), channel_id=1, source_target_pairs={{0,1},{1,0},{2,3},{3,2},{4,5},{5,4},{6,7},{7,6},{8,9},{9,8},{10,11... | collective-permute-start | bytes 786440 | tf_op jit(solution)/shard_map/ppermute | solution.py:393

commit v4 on v3

--- a/solution.py
+++ b/solution.py
@@ -16,7 +16,8 @@
 F32, BF16 = jnp.float32, jnp.bfloat16
 ALL = ("z", "x", "y", "core")
 VMEM_BYTES = 48 * 1024 * 1024
-MIX_BYTES = 103 * 512 * 1024
+FETCH_BYTES = 52 * 1024 * 1024
+FETCH_FLOPS = 10**9
 
 
 def split(a):
@@ -132,45 +133,37 @@
 HEADS = range(HALF)
 
 
-def mix_kernel(x_in, w_in, keys_out, values_out, x_out, scratch):
+def fetch_kernel(at, x_all, last_out, x_far, x_own, tail, sems):
+    copies = [pltpu.make_async_copy(x_all.at[pl.ds(ROWS - 16, 16), :], tail, sems.at[4])]
+    for g, to in enumerate((x_far, x_own)):
+        for p in range(2):
+            begin = ((p + 1) * H + half_of(at, g == 0) * HALF) * DK
+            cols = pl.ds(pl.multiple_of(begin, HALF * DK), HALF * DK)
+            copies.append(
+                pltpu.make_async_copy(x_all.at[:, cols], to.at[p], sems.at[2 * g + p])
+            )
+    for copy in copies:
+        copy.start()
+    for copy in copies:
+        copy.wait()
+    last_out[...] = tail[...].astype(F32)[16 - (KCONV - 1) :].astype(BF16)
+
+
+def mix_kernel(at, x, w, keys_out, values_out, x_out, scratch, *, other):
+    half = half_of(at, other)
     for p in range(2):
         for h in HEADS:
             held = scratch.at[p, h]
             held[0:8, :] = jnp.zeros((8, DK), F32)
-            held[8 : 8 + ROWS, :] = x_in[p, :, columns(h)].astype(F32)
+            held[8 : 8 + ROWS, :] = x[p, :, columns(h)].astype(F32)
             x_out[p, :, columns(h)] = held[8:16, :]
-            m = taps(w_in[p, :, columns(h)], ROWS, held, ROWS)
+            m = taps(w[:, head_columns(p + 1, half, h)], ROWS, held, ROWS)
             if p == 0:
                 keys_out[h] = unit(m)
             else:
                 values_out[h] = m
 
 
-def mix_own_kernel(at, x_in, w_in, *refs):
-    mix_kernel(x_in, w_in, *refs)
-
-
-def mix_far_kernel(at, x_all, w_all, *refs):
-    keys_out, values_out, x_out, w_far, w_own, x_own, x_far, scratch, sems = refs
-    copies = []
-    for i, (other, x_to, w_to) in enumerate(((True, x_far, w_far), (False, x_own, w_own))):
-        for p in range(2):
-            begin = pl.multiple_of(
-                ((p + 1) * H + half_of(at, other) * HALF) * DK, HALF * DK
-            )
-            cols = pl.ds(begin, HALF * DK)
-            k = 4 * i + 2 * p
-            copies.append(pltpu.make_async_copy(w_all.at[:, cols], w_to.at[p], sems.at[k]))
-            copies.append(pltpu.make_async_copy(x_all.at[:, cols], x_to.at[p], sems.at[k + 1]))
-    for copy in copies:
-        copy.start()
-    for copy in copies[:4]:
-        copy.wait()
-    mix_kernel(x_far, w_far, keys_out, values_out, x_out, scratch)
-    for copy in copies[4:]:
-        copy.wait()
-
-
 def rim_of(at, rim, cols):
     first = at[0] + at[1] + at[2] + at[3] == 0
     return jnp.where(first, 0.0, rim[:, cols].astype(F32))
@@ -191,7 +184,7 @@
         first = first_rows(
             rim_of(at, rim, head_columns(p + 1, half, h)),
             x[p, :, columns(h)],
-            w[p, :, columns(h)],
+            w[:, head_columns(p + 1, half, h)],
             scratch.at[p, h],
         )
         return jnp.concatenate([unit(first) if p == 0 else first, rest[h, 8:, :]], 0)
@@ -283,11 +276,18 @@
     total[...] = compose(upper, two)
 
 
-def z_kernel(at, b1, b3, b2, x_prefix, y_prefixes, s0, s1, s2, s3, states):
-    y, z = at[2], at[0]
-    state = jnp.where(z >= 3, b3[:, DK:], 0.0)
-    state = jnp.where(z >= 2, enter(b2[...], state), 0.0)
-    state = jnp.where(z >= 1, enter(b1[...], state), 0.0)
+def z1_kernel(at, own, got, second):
+    later, earlier = ordered(at[0] % 2 == 0, own[...], got[...])
+    second[...] = enter(later, earlier[:, DK:])
+
+
+def z2_kernel(at, got_z, got_second, x_prefix, y_prefixes, s0, s1, s2, s3, states):
+    z, y = at[0], at[2]
+    state = jnp.where(
+        z < 2,
+        jnp.where(z == 0, 0.0, got_z[:, DK:]),
+        jnp.where(z == 2, got_second[...], enter(got_z[...], got_second[...])),
+    )
     state = enter(x_prefix[...], state)
     states[0] = state
     for i in range(3):
@@ -327,7 +327,7 @@
         return lax.axis_index(ALL[i])
 
 
-def step(kernel, args, outs, scratch=(), after=(), vmem=VMEM_BYTES, hbm=()):
+def step(kernel, args, outs, scratch=(), after=(), vmem=VMEM_BYTES, hbm=(), flops=10**6):
     args, after, hbm = list(args), list(after), list(hbm)
 
     def body(*refs):
@@ -339,7 +339,7 @@
         in_specs=[pl.BlockSpec()] * len(args) + [anywhere] * (len(hbm) + len(after)),
         out_shape=list(outs),
         scratch_shapes=list(scratch),
-        cost_estimate=pl.CostEstimate(flops=10**6, bytes_accessed=2**10, transcendentals=0),
+        cost_estimate=pl.CostEstimate(flops=flops, bytes_accessed=2**10, transcendentals=0),
         compiler_params=pltpu.CompilerParams(vmem_limit_bytes=vmem),
     )(*args, *hbm, *after)
 
@@ -348,31 +348,33 @@
     return jax.ShapeDtypeStruct(shape, F32)
 
 
-def mix_calls(projected, weight):
-    mixed = [shaped(HALF, ROWS, DK)] * 2 + [shaped(2, 8, HALF * DK)]
-    w, x = shaped(2, KCONV, HALF * DK), jax.ShapeDtypeStruct((2, ROWS, HALF * DK), BF16)
-    room = pltpu.VMEM((2, HALF, ROWS + 8, DK), F32)
-    *far, w_own, x_own = step(
-        mix_far_kernel,
+def fetch_call(projected):
+    x = jax.ShapeDtypeStruct((2, ROWS, HALF * DK), BF16)
+    return step(
+        fetch_kernel,
         (),
-        [*mixed, w, w, x],
-        [
-            pltpu.VMEM(x.shape, BF16),
-            room,
-            pltpu.SemaphoreType.DMA((8,)),
-        ],
-        vmem=MIX_BYTES,
-        hbm=(projected, weight),
-    )
-    own = step(mix_own_kernel, (x_own, w_own), mixed, [room])
-    return far, [*own, w_own]
-
-
-def local_call(mixes, rim, beta, other, after=()):
+        [jax.ShapeDtypeStruct((KCONV - 1, 3 * H * DK), BF16), x, x],
+        [pltpu.VMEM((16, 3 * H * DK), BF16), pltpu.SemaphoreType.DMA((5,))],
+        vmem=FETCH_BYTES,
+        hbm=(projected,),
+        flops=FETCH_FLOPS,
+    )
+
+
+def mix_call(x, weight, other):
+    return step(
+        functools.partial(mix_kernel, other=other),
+        (x, weight),
+        [shaped(HALF, ROWS, DK)] * 2 + [shaped(2, 8, HALF * DK)],
+        [pltpu.VMEM((2, HALF, ROWS + 8, DK), F32)],
+    )
+
+
+def local_call(mixes, weight, rim, beta, other, after=()):
     outs = [shaped(HALF, DK, 2 * DK), shaped(HALF, DK, ROWS), shaped(HALF, ROWS, 2 * DK)]
     return step(
         functools.partial(local_kernel, other=other),
-        (*mixes, rim, beta),
+        (*mixes, weight, rim, beta),
         outs,
         [pltpu.VMEM((2, HALF, 16, DK), F32)],
         after,
@@ -389,8 +391,12 @@
     )
 
 
+def exchange(block, axis, partner):
+    return lax.ppermute(block, axis, [(i, partner(i)) for i in range(lax.axis_size(axis))])
+
+
 def swap(block):
-    return lax.ppermute(block, "core", [(0, 1), (1, 0)])
+    return exchange(block, "core", lambda i: 1 - i)
 
 
 def shift(block, axis, distance):
@@ -406,13 +412,16 @@
     gain = gain.reshape(1, DK)
     one, state = shaped(DK, 2 * DK), shaped(DK, DK)
 
-    last = projected[ROWS - (KCONV - 1) :]
+    last, x_far, x_own = fetch_call(projected)
     count = lax.axis_size(ALL)
     rim = lax.ppermute(last, ALL, [(i, (i + 1) % count) for i in range(count)])
-    mixes_far, mixes_own = mix_calls(projected, weight)
-    sent, keys_far, solved_far = local_call(mixes_far, rim, beta, True, mixes_own[2:3])
+    mixes_far = mix_call(x_far, weight, True)
+    mixes_own = mix_call(x_own, weight, False)
+    sent, keys_far, solved_far = local_call(
+        mixes_far, weight, rim, beta, True, mixes_own[2:]
+    )
     came = swap(sent)
-    kept, keys_own, solved_own = local_call(mixes_own, rim, beta, False)
+    kept, keys_own, solved_own = local_call(mixes_own, weight, rim, beta, False)
     chip = step(chip_kernel, (kept, came), [one] * 4)
 
     held = pltpu.VMEM((4, DK, 2 * DK), F32)
@@ -428,11 +437,13 @@
     )
     b1, b2, b3 = ring_of([trans] * 3, "x")
     trans, x_prefix = step(x_kernel, (trans, b1, b3, b2), [one, one], [held])
-    b1, b2, b3 = ring_of([trans] * 3, "z")
+    got_z = exchange(trans, "z", lambda i: i ^ 1)
+    (second,) = step(z1_kernel, (trans, got_z), [state])
+    got_second = exchange(second, "z", lambda i: 3 - i)
 
     states = step(
-        z_kernel,
-        (b1, b3, b2, x_prefix, y_prefixes),
+        z2_kernel,
+        (got_z, got_second, x_prefix, y_prefixes),
         [state] * 4,
         [pltpu.VMEM((4, DK, DK), F32)],
     )

time: 59.3 us -> 61.1 us (1.030)
  starting transfers between devices: 20 us -> 21.7 us
  waiting for transfers between devices: 22.2 us -> 23.9 us
  local copies, waits for them, and re-layouts: 1.64 us -> 0.02 us
    ppermute x2 -> x4, waiting for transfers between devices: 0.75 us -> 9.49 us  [exchange(): lax.ppermute(block, axis, [(i, partner(i)) for i in range(lax.axis_size(a...]
    ppermute x12 -> x9, waiting for transfers between devices: 21.5 us -> 14.4 us  [shift(): lax.ppermute(block, axis, [(i, (i + distance) % n) for i in range(n)])]
    ppermute x2 -> x4, starting transfers between devices: 7.39 us -> 11.2 us  [exchange(): lax.ppermute(block, axis, [(i, partner(i)) for i in range(lax.axis_size(a...]
    ppermute x12 -> x9, starting transfers between devices: 9.84 us -> 7.66 us  [shift(): lax.ppermute(block, axis, [(i, (i + distance) % n) for i in range(n)])]
    slice x1 -> x0, local copies, waits for them, and re-layouts: 0.83 us -> none  [shards(): last = projected[ROWS - (KCONV - 1):]]
    unnamed x10 -> x8, local copies, waits for them, and re-layouts: 0.82 us -> 0.02 us
    pallas_call x13 -> x15, Pallas kernels: 15.1 us -> 15.2 us  [step(): pl.pallas_call(body, in_specs=[pl.BlockSpec()] * len(args) + [anywhere] *...]
  transfers between devices with their start and end apart: 15 -> 14, of which waited for: 10 -> 9; matrix products, arithmetic and copies ran while one was open for 0% -> 0% of each run, Pallas kernels for 14% -> 12%
where the time goes in v4:
time: 61.1 us; the launch traced here: 61 us
  waiting for transfers between devices  23.9 us (39%)
  starting transfers between devices  21.7 us (36%)
  Pallas kernels  15.2 us (25%)
    pallas_call x15, Pallas kernels, step(): pl.pallas_call(body, in_specs=[pl.BlockSpec()] * len(args) + [anywhere] *...  15.2 us
    ppermute x9, waiting for transfers between devices, shift(): lax.ppermute(block, axis, [(i, (i + distance) % n) for i in range(n)])  14.4 us
    ppermute x4, starting transfers between devices, exchange(): lax.ppermute(block, axis, [(i, partner(i)) for i in range(lax.axis_size(a...  11.2 us
    ppermute x4, waiting for transfers between devices, exchange(): lax.ppermute(block, axis, [(i, partner(i)) for i in range(lax.axis_size(a...  9.49 us
    ppermute x9, starting transfers between devices, shift(): lax.ppermute(block, axis, [(i, (i + distance) % n) for i in range(n)])  7.66 us
    ppermute x1, starting transfers between devices, shards(): rim = lax.ppermute(last, ALL, [(i, (i + 1) % count) for i in range(count)])  2.76 us
  transfers between devices with their start and end apart: 14, of which 9 were waited for; matrix products, arithmetic and copies ran while one was open for 0% of the time, Pallas kernels for 12%

profile of v4, /device:TPU:1, one launch (start us, length us, event | category | flops | bytes accessed | tf_op | source)
XLA Modules:
  0.0 61.0 jit_solution(6903743402492014654)
XLA Ops:
  0.0 0.0 copy-start.1
  0.0 0.0 copy-start.2
  0.0 1.3 %shard_map.46 = (bf16[3,3072]{1,0:T(4,128)(2,1)S(1)}, bf16[2,256,512]{2,1,0:T(8,128)(2,1)S(1)}, bf16[2,256,512]{2,1,0:T(8,128)(2,1)S(1)}) custom-call(bf16[256,3072]{1,0:T(8,128)(2,1)} %refs_0_.5), custom_call_target="tpu_custom_call" | custom-call | flops 1000000000 | bytes 1024 | tf_op jit(solution)/shard_map/pallas_call | solution.py:337
  1.3 2.8 %collective-permute-start = (bf16[3,3072]{1,0:T(4,128)(2,1)S(1)}, bf16[3,3072]{1,0:T(4,128)(2,1)S(1)}, u32[]{:S(2)}, u32[]{:S(2)}) collective-permute-start(bf16[3,3072]{1,0:T(4,128)(2,1)S(1)} %get-tuple-element.40), channel_id=1, source_target_pairs={{0,1},{1,2},{2,3},{3,4},{4,5},{5,6},{6,7},{7,8},{8,9},{9,10},{10,1... | collective-permute-start | bytes 55304 | tf_op jit(solution)/shard_map/ppermute | solution.py:417
  4.1 0.0 copy-done.1
  4.1 0.7 %shard_map.47 = (f32[4,256,128]{2,1,0:T(8,128)S(1)}, f32[4,256,128]{2,1,0:T(8,128)S(1)}, f32[2,8,512]{2,1,0:T(8,128)S(1)}) custom-call(bf16[2,256,512]{2,1,0:T(8,128)(2,1)S(1)} %get-tuple-element.41.refs_0_, f32[4,3072]{1,0:T(4,128)S(1)} %copy-done.1), custom_call_target="tpu_custom_call" | custom-call | flops 1000000 | bytes 1024 | tf_op jit(solution)/shard_map/pallas_call | solution.py:337
  4.8 0.7 %shard_map.48 = (f32[4,256,128]{2,1,0:T(8,128)S(1)}, f32[4,256,128]{2,1,0:T(8,128)S(1)}, f32[2,8,512]{2,1,0:T(8,128)S(1)}) custom-call(bf16[2,256,512]{2,1,0:T(8,128)(2,1)S(1)} %get-tuple-element.45.refs_0_, f32[4,3072]{1,0:T(4,128)S(1)} %copy-done.1), custom_call_target="tpu_custom_call" | custom-call | flops 1000000 | bytes 1024 | tf_op jit(solution)/shard_map/pallas_call | solution.py:337
  5.5 0.0 collective-permute-done.refs_4_.refs_1_
  5.5 0.0 copy-done.2
  5.6 0.0 copy-start
  5.6 3.0 %shard_map.49 = (f32[4,128,256]{2,1,0:T(8,128)S(1)}, f32[4,128,256]{2,1,0:T(8,128)S(1)}, f32[4,256,256]{2,1,0:T(8,128)S(1)}) custom-call(f32[4,256,128]{2,1,0:T(8,128)S(1)} %get-tuple-element.42.refs_0_, f32[4,256,128]{2,1,0:T(8,128)S(1)} %get-tuple-element.43.refs_1_, f32[2,8,512]{2,1,0:T(8,128)S(1)} %get-tuple-element.44.refs_2_, f32[4,3072]{1,0:T(4,128)S(1)} %copy-done.1, ...), custom_call_target="tpu_custom_call" | custom-call | flops 1000000 | bytes 1024 | tf_op jit(solution)/shard_map/pallas_call | solution.py:337
  8.6 7.0 %collective-permute-start.1 = (f32[4,128,256]{2,1,0:T(8,128)S(1)}, f32[4,128,256]{2,1,0:T(8,128)S(1)}, u32[]{:S(2)}, u32[]{:S(2)}) collective-permute-start(f32[4,128,256]{2,1,0:T(8,128)S(1)} %get-tuple-element.54), channel_id=1, source_target_pairs={{0,1},{1,0},{2,3},{3,2},{4,5},{5,4},{6,7},{7,6},{8,9},{9,8},{10,11... | collective-permute-start | bytes 1572872 | tf_op jit(solution)/shard_map/ppermute | solution.py:395
  15.7 3.0 %shard_map.51 = (f32[4,128,256]{2,1,0:T(8,128)S(1)}, f32[4,128,256]{2,1,0:T(8,128)S(1)}, f32[4,256,256]{2,1,0:T(8,128)S(1)}) custom-call(f32[4,256,128]{2,1,0:T(8,128)S(1)} %get-tuple-element.51.refs_0_, f32[4,256,128]{2,1,0:T(8,128)S(1)} %get-tuple-element.52.refs_1_, f32[2,8,512]{2,1,0:T(8,128)S(1)} %get-tuple-element.46.refs_6_.refs_2_, ...), custom_call_target="tpu_custom_call" | custom-call | flops 1000000 | bytes 1024 | tf_op jit(solution)/shard_map/pallas_call | solution.py:337
  18.7 0.0 collective-permute-done.1.refs_1_
  18.7 0.3 shard_map.52
  19.0 0.1 collective-permute-start.2
  19.1 0.1 collective-permute-start.3
  19.2 2.7 %collective-permute-start.4 = (f32[128,256]{1,0:T(8,128)S(1)}, f32[128,256]{1,0:T(8,128)S(1)}, u32[]{:S(2)}, u32[]{:S(2)}) collective-permute-start(f32[128,256]{1,0:T(8,128)S(1)} %get-tuple-element.58), channel_id=1, source_target_pairs={{0,6},{2,0},{4,2},{6,4},{1,7},{3,1},{5,3},{7,5},{8,14},{10,8},{12,... | collective-permute-start | bytes 393224 | tf_op jit(solution)/shard_map/ppermute | solution.py:404
  21.9 0.0 copy-done
  21.9 1.2 %shard_map.50 = (f32[4,256,128]{2,1,0:T(8,128)S(1)}, f32[4,256,128]{2,1,0:T(8,128)S(1)}, f32[8,128]{1,0:T(8,128)S(1)}) custom-call(bf16[256,3072]{1,0:T(8,128)(2,1)S(1)} %copy-done, bf16[3,3072]{1,0:T(4,128)(2,1)S(1)} %collective-permute-done.refs_4_.refs_1_, f32[4,3072]{1,0:T(4,128)S(1)} %copy-done.1, f32[4,128,256]{2,1,0:T(8,128)S(1)} %get-tuple-element.47.refs_3_, ...), custom_call_target="tpu_custom_call" | custom-call | flops 1000000 | bytes 1024 | tf_op jit(solution)/shard_map/pallas_call | solution.py:337
  23.1 1.2 %shard_map.53 = (f32[4,256,128]{2,1,0:T(8,128)S(1)}, f32[4,256,128]{2,1,0:T(8,128)S(1)}, f32[8,128]{1,0:T(8,128)S(1)}) custom-call(bf16[256,3072]{1,0:T(8,128)(2,1)S(1)} %copy-done, bf16[3,3072]{1,0:T(4,128)(2,1)S(1)} %collective-permute-done.refs_4_.refs_1_, f32[4,3072]{1,0:T(4,128)S(1)} %copy-done.1, f32[4,128,256]{2,1,0:T(8,128)S(1)} %get-tuple-element.60.refs_3_, ...), custom_call_target="tpu_custom_call" | custom-call | flops 1000000 | bytes 1024 | tf_op jit(solution)/shard_map/pallas_call | solution.py:337
  24.4 1.4 %collective-permute-done.2.refs_1_ = f32[128,256]{1,0:T(8,128)S(1)} collective-permute-done((f32[128,256]{1,0:T(8,128)S(1)}, f32[128,256]{1,0:T(8,128)S(1)}, u32[]{:S(2)}, u32[]{:S(2)}) %collective-permute-start.2) | collective-permute-done | bytes 131104 | tf_op jit(solution)/shard_map/ppermute | solution.py:404
  25.8 2.7 %collective-permute-done.3.refs_2_ = f32[128,256]{1,0:T(8,128)S(1)} collective-permute-done((f32[128,256]{1,0:T(8,128)S(1)}, f32[128,256]{1,0:T(8,128)S(1)}, u32[]{:S(2)}, u32[]{:S(2)}) %collective-permute-start.3) | collective-permute-done | bytes 131104 | tf_op jit(solution)/shard_map/ppermute | solution.py:404
  28.4 0.0 collective-permute-done.4.refs_3_
  28.4 0.5 shard_map.54
  28.9 0.0 copy-start.3
  28.9 0.1 collective-permute-start.7
  29.0 0.1 collective-permute-start.6
  29.1 1.5 %collective-permute-start.5 = (f32[128,256]{1,0:T(8,128)S(1)}, f32[128,256]{1,0:T(8,128)S(1)}, u32[]{:S(2)}, u32[]{:S(2)}) collective-permute-start(f32[128,256]{1,0:T(8,128)S(1)} %get-tuple-element.63.refs_0_), channel_id=1, source_target_pairs={{0,8},{8,16},{16,24},{24,0},{1,9},{9,17},{17,25},{25,1},{2,10},{10... | collective-permute-start | bytes 393224 | tf_op jit(solution)/shard_map/ppermute | solution.py:404
  30.6 4.3 %collective-permute-done.7.refs_3_ = f32[128,256]{1,0:T(8,128)S(1)} collective-permute-done((f32[128,256]{1,0:T(8,128)S(1)}, f32[128,256]{1,0:T(8,128)S(1)}, u32[]{:S(2)}, u32[]{:S(2)}) %collective-permute-start.7) | collective-permute-done | bytes 131104 | tf_op jit(solution)/shard_map/ppermute | solution.py:404
  34.8 0.0 collective-permute-done.6.refs_2_
  34.8 3.9 %collective-permute-done.5.refs_1_ = f32[128,256]{1,0:T(8,128)S(1)} collective-permute-done((f32[128,256]{1,0:T(8,128)S(1)}, f32[128,256]{1,0:T(8,128)S(1)}, u32[]{:S(2)}, u32[]{:S(2)}) %collective-permute-start.5) | collective-permute-done | bytes 131104 | tf_op jit(solution)/shard_map/ppermute | solution.py:404
  38.7 0.5 shard_map.55
  39.2 0.3 collective-permute-start.8
  39.5 4.6 %collective-permute-done.8.refs_1_.refs_0_ = f32[128,256]{1,0:T(8,128)S(1)} collective-permute-done((f32[128,256]{1,0:T(8,128)S(1)}, f32[128,256]{1,0:T(8,128)S(1)}, u32[]{:S(2)}, u32[]{:S(2)}) %collective-permute-start.8) | collective-permute-done | bytes 131104 | tf_op jit(solution)/shard_map/ppermute | solution.py:395
  44.1 0.2 shard_map.56
  44.2 0.2 collective-permute-start.9
  44.5 4.2 %collective-permute-done.9.refs_1_ = f32[128,128]{1,0:T(8,128)S(1)} collective-permute-done((f32[128,128]{1,0:T(8,128)S(1)}, f32[128,128]{1,0:T(8,128)S(1)}, u32[]{:S(2)}, u32[]{:S(2)}) %collective-permute-start.9) | collective-permute-done | bytes 65568 | tf_op jit(solution)/shard_map/ppermute | solution.py:395
  48.7 0.6 shard_map.57
  49.2 0.5 collective-permute-start.10
  49.8 0.4 collective-permute-start.11
  50.2 2.3 %collective-permute-start.12 = (f32[128,128]{1,0:T(8,128)S(1)}, f32[128,128]{1,0:T(8,128)S(1)}, u32[]{:S(2)}, u32[]{:S(2)}) collective-permute-start(f32[128,128]{1,0:T(8,128)S(1)} %get-tuple-element.70), channel_id=1, source_target_pairs={{0,6},{2,0},{4,2},{6,4},{1,7},{3,1},{5,3},{7,5},{8,14},{10,8},{12,... | collective-permute-start | bytes 196616 | tf_op jit(solution)/shard_map/ppermute | solution.py:404
  52.5 1.5 %collective-permute-done.10.refs_3_ = f32[128,128]{1,0:T(8,128)S(1)} collective-permute-done((f32[128,128]{1,0:T(8,128)S(1)}, f32[128,128]{1,0:T(8,128)S(1)}, u32[]{:S(2)}, u32[]{:S(2)}) %collective-permute-start.10) | collective-permute-done | bytes 65568 | tf_op jit(solution)/shard_map/ppermute | solution.py:404
  54.0 0.6 %collective-permute-done.11.refs_4_ = f32[128,128]{1,0:T(8,128)S(1)} collective-permute-done((f32[128,128]{1,0:T(8,128)S(1)}, f32[128,128]{1,0:T(8,128)S(1)}, u32[]{:S(2)}, u32[]{:S(2)}) %collective-permute-start.11) | collective-permute-done | bytes 65568 | tf_op jit(solution)/shard_map/ppermute | solution.py:404
  54.6 0.0 collective-permute-done.12.refs_5_
  54.7 0.2 shard_map.58
  54.9 3.7 %collective-permute-start.13 = (f32[4,128,128]{2,1,0:T(8,128)S(1)}, f32[4,128,128]{2,1,0:T(8,128)S(1)}, u32[]{:S(2)}, u32[]{:S(2)}) collective-permute-start(f32[4,128,128]{2,1,0:T(8,128)S(1)} %get-tuple-element.71), channel_id=1, source_target_pairs={{0,1},{1,0},{2,3},{3,2},{4,5},{5,4},{6,7},{7,6},{8,9},{9,8},{10,11... | collective-permute-start | bytes 786440 | tf_op jit(solution)/shard_map/ppermute | solution.py:395
  58.6 0.0 copy-done.3
  58.6 0.4 shard_map.59.refs_4_
  59.0 0.7 %collective-permute-done.13.refs_2_ = f32[4,128,128]{2,1,0:T(8,128)S(1)} collective-permute-done((f32[4,128,128]{2,1,0:T(8,128)S(1)}, f32[4,128,128]{2,1,0:T(8,128)S(1)}, u32[]{:S(2)}, u32[]{:S(2)}) %collective-permute-start.13) | collective-permute-done | bytes 262176 | tf_op jit(solution)/shard_map/ppermute | solution.py:395
  59.8 1.2 %shard_map.60 = bf16[256,1024]{1,0:T(8,128)(2,1)} custom-call(f32[4,256,128]{2,1,0:T(8,128)S(1)} %get-tuple-element.49.refs_0_, f32[4,256,128]{2,1,0:T(8,128)S(1)} %get-tuple-element.50.refs_1_, f32[4,128,128]{2,1,0:T(8,128)S(1)} %collective-permute-done.13.refs_2_, f32[1,128]{1,0:T(1,128)S(1)} %bitcast.2, bf16[256,512]{1,0:T(8,128)(2,1)S(1)} %shard_map.59.refs_4_), custom_call_target="tpu_custom_call" | custom-call | flops 1000000 | bytes 1024 | tf_op jit(solution)/shard_map/pallas_call | solution.py:337
Async XLA Ops:
  0.0 4.1 %copy-start.1 = (f32[4,3072]{1,0:T(4,128)S(1)}, f32[4,3072]{1,0:T(4,128)}, u32[]{:S(2)}) copy-start(f32[4,3072]{1,0:T(4,128)} %refs_2_.3) | copy-start | bytes 147460
  0.0 5.5 %copy-start.2 = (f32[8,256]{1,0:T(8,128)S(1)}, f32[8,256]{1,0:T(8,128)}, u32[]{:S(2)}) copy-start(f32[8,256]{1,0:T(8,128)} %refs_5_.3) | copy-start | bytes 24580
  1.3 4.2 %collective-permute-start = (bf16[3,3072]{1,0:T(4,128)(2,1)S(1)}, bf16[3,3072]{1,0:T(4,128)(2,1)S(1)}, u32[]{:S(2)}, u32[]{:S(2)}) collective-permute-start(bf16[3,3072]{1,0:T(4,128)(2,1)S(1)} %get-tuple-element.40), channel_id=1, source_target_pairs={{0,1},{1,2},{2,3},{3,4},{4,5},{5,6},{6,7},{7,8},{8,9},{9,10},{10,1... | collective-permute-start | bytes 55304 | tf_op jit(solution)/shard_map/ppermute | solution.py:417
  5.6 16.3 %copy-start = (bf16[256,3072]{1,0:T(8,128)(2,1)S(1)}, bf16[256,3072]{1,0:T(8,128)(2,1)}, u32[]{:S(2)}) copy-start(bf16[256,3072]{1,0:T(8,128)(2,1)} %refs_0_.5) | copy-start | bytes 4718596
  8.6 10.1 %collective-permute-start.1 = (f32[4,128,256]{2,1,0:T(8,128)S(1)}, f32[4,128,256]{2,1,0:T(8,128)S(1)}, u32[]{:S(2)}, u32[]{:S(2)}) collective-permute-start(f32[4,128,256]{2,1,0:T(8,128)S(1)} %get-tuple-element.54), channel_id=1, source_target_pairs={{0,1},{1,0},{2,3},{3,2},{4,5},{5,4},{6,7},{7,6},{8,9},{9,8},{10,11... | collective-permute-start | bytes 1572872 | tf_op jit(solution)/shard_map/ppermute | solution.py:395
  19.0 6.7 %collective-permute-start.2 = (f32[128,256]{1,0:T(8,128)S(1)}, f32[128,256]{1,0:T(8,128)S(1)}, u32[]{:S(2)}, u32[]{:S(2)}) collective-permute-start(f32[128,256]{1,0:T(8,128)S(1)} %get-tuple-element.56), channel_id=1, source_target_pairs={{0,4},{2,6},{4,0},{6,2},{1,5},{3,7},{5,1},{7,3},{8,12},{10,14},{12... | collective-permute-start | bytes 393224 | tf_op jit(solution)/shard_map/ppermute | solution.py:404
  19.1 9.3 %collective-permute-start.3 = (f32[128,256]{1,0:T(8,128)S(1)}, f32[128,256]{1,0:T(8,128)S(1)}, u32[]{:S(2)}, u32[]{:S(2)}) collective-permute-start(f32[128,256]{1,0:T(8,128)S(1)} %get-tuple-element.57), channel_id=1, source_target_pairs={{0,2},{2,4},{4,6},{6,0},{1,3},{3,5},{5,7},{7,1},{8,10},{10,12},{12... | collective-permute-start | bytes 393224 | tf_op jit(solution)/shard_map/ppermute | solution.py:404
  19.2 9.2 %collective-permute-start.4 = (f32[128,256]{1,0:T(8,128)S(1)}, f32[128,256]{1,0:T(8,128)S(1)}, u32[]{:S(2)}, u32[]{:S(2)}) collective-permute-start(f32[128,256]{1,0:T(8,128)S(1)} %get-tuple-element.58), channel_id=1, source_target_pairs={{0,6},{2,0},{4,2},{6,4},{1,7},{3,1},{5,3},{7,5},{8,14},{10,8},{12,... | collective-permute-start | bytes 393224 | tf_op jit(solution)/shard_map/ppermute | solution.py:404
  28.9 29.7 %copy-start.3 = (f32[128]{0:T(128)S(1)}, f32[128]{0:T(128)}, u32[]{:S(2)}) copy-start(f32[128]{0:T(128)} %param.7) | copy-start | bytes 1540
  28.9 5.9 %collective-permute-start.7 = (f32[128,256]{1,0:T(8,128)S(1)}, f32[128,256]{1,0:T(8,128)S(1)}, u32[]{:S(2)}, u32[]{:S(2)}) collective-permute-start(f32[128,256]{1,0:T(8,128)S(1)} %get-tuple-element.63.refs_0_), channel_id=1, source_target_pairs={{0,16},{8,24},{16,0},{24,8},{1,17},{9,25},{17,1},{25,9},{2,18},{10... | collective-permute-start | bytes 393224 | tf_op jit(solution)/shard_map/ppermute | solution.py:404
  29.0 5.8 %collective-permute-start.6 = (f32[128,256]{1,0:T(8,128)S(1)}, f32[128,256]{1,0:T(8,128)S(1)}, u32[]{:S(2)}, u32[]{:S(2)}) collective-permute-start(f32[128,256]{1,0:T(8,128)S(1)} %get-tuple-element.63.refs_0_), channel_id=1, source_target_pairs={{0,24},{8,0},{16,8},{24,16},{1,25},{9,1},{17,9},{25,17},{2,26},{10... | collective-permute-start | bytes 393224 | tf_op jit(solution)/shard_map/ppermute | solution.py:404
  29.1 9.6 %collective-permute-start.5 = (f32[128,256]{1,0:T(8,128)S(1)}, f32[128,256]{1,0:T(8,128)S(1)}, u32[]{:S(2)}, u32[]{:S(2)}) collective-permute-start(f32[128,256]{1,0:T(8,128)S(1)} %get-tuple-element.63.refs_0_), channel_id=1, source_target_pairs={{0,8},{8,16},{16,24},{24,0},{1,9},{9,17},{17,25},{25,1},{2,10},{10... | collective-permute-start | bytes 393224 | tf_op jit(solution)/shard_map/ppermute | solution.py:404
  39.2 4.8 %collective-permute-start.8 = (f32[128,256]{1,0:T(8,128)S(1)}, f32[128,256]{1,0:T(8,128)S(1)}, u32[]{:S(2)}, u32[]{:S(2)}) collective-permute-start(f32[128,256]{1,0:T(8,128)S(1)} %get-tuple-element.64.refs_0_), channel_id=1, source_target_pairs={{0,32},{32,0},{64,96},{96,64},{1,33},{33,1},{65,97},{97,65},{2,34}... | collective-permute-start | bytes 393224 | tf_op jit(solution)/shard_map/ppermute | solution.py:395
  44.2 4.4 %collective-permute-start.9 = (f32[128,128]{1,0:T(8,128)S(1)}, f32[128,128]{1,0:T(8,128)S(1)}, u32[]{:S(2)}, u32[]{:S(2)}) collective-permute-start(f32[128,128]{1,0:T(8,128)S(1)} %shard_map.56), channel_id=1, source_target_pairs={{0,96},{32,64},{64,32},{96,0},{1,97},{33,65},{65,33},{97,1},{2,98}... | collective-permute-start | bytes 196616 | tf_op jit(solution)/shard_map/ppermute | solution.py:395
  49.2 4.8 %collective-permute-start.10 = (f32[128,128]{1,0:T(8,128)S(1)}, f32[128,128]{1,0:T(8,128)S(1)}, u32[]{:S(2)}, u32[]{:S(2)}) collective-permute-start(f32[128,128]{1,0:T(8,128)S(1)} %get-tuple-element.68), channel_id=1, source_target_pairs={{0,4},{2,6},{4,0},{6,2},{1,5},{3,7},{5,1},{7,3},{8,12},{10,14},{12... | collective-permute-start | bytes 196616 | tf_op jit(solution)/shard_map/ppermute | solution.py:404
  49.8 4.9 %collective-permute-start.11 = (f32[128,128]{1,0:T(8,128)S(1)}, f32[128,128]{1,0:T(8,128)S(1)}, u32[]{:S(2)}, u32[]{:S(2)}) collective-permute-start(f32[128,128]{1,0:T(8,128)S(1)} %get-tuple-element.69), channel_id=1, source_target_pairs={{0,2},{2,4},{4,6},{6,0},{1,3},{3,5},{5,7},{7,1},{8,10},{10,12},{12... | collective-permute-start | bytes 196616 | tf_op jit(solution)/shard_map/ppermute | solution.py:404
  50.2 4.5 %collective-permute-start.12 = (f32[128,128]{1,0:T(8,128)S(1)}, f32[128,128]{1,0:T(8,128)S(1)}, u32[]{:S(2)}, u32[]{:S(2)}) collective-permute-start(f32[128,128]{1,0:T(8,128)S(1)} %get-tuple-element.70), channel_id=1, source_target_pairs={{0,6},{2,0},{4,2},{6,4},{1,7},{3,1},{5,3},{7,5},{8,14},{10,8},{12,... | collective-permute-start | bytes 196616 | tf_op jit(solution)/shard_map/ppermute | solution.py:404
  54.9 4.9 %collective-permute-start.13 = (f32[4,128,128]{2,1,0:T(8,128)S(1)}, f32[4,128,128]{2,1,0:T(8,128)S(1)}, u32[]{:S(2)}, u32[]{:S(2)}) collective-permute-start(f32[4,128,128]{2,1,0:T(8,128)S(1)} %get-tuple-element.71), channel_id=1, source_target_pairs={{0,1},{1,0},{2,3},{3,2},{4,5},{5,4},{6,7},{7,6},{8,9},{9,8},{10,11... | collective-permute-start | bytes 786440 | tf_op jit(solution)/shard_map/ppermute | solution.py:395

commit v5 on v4

--- a/solution.py
+++ b/solution.py
@@ -131,10 +131,12 @@
 
 
 HEADS = range(HALF)
-
-
-def fetch_kernel(at, x_all, last_out, x_far, x_own, tail, sems):
-    copies = [pltpu.make_async_copy(x_all.at[pl.ds(ROWS - 16, 16), :], tail, sems.at[4])]
+FIRST, SECOND = (2, 0), (1, 3)
+OWN = FIRST + SECOND
+
+
+def fetch_kernel(at, x_all, x_far, x_own, sems):
+    copies = []
     for g, to in enumerate((x_far, x_own)):
         for p in range(2):
             begin = ((p + 1) * H + half_of(at, g == 0) * HALF) * DK
@@ -146,7 +148,6 @@
         copy.start()
     for copy in copies:
         copy.wait()
-    last_out[...] = tail[...].astype(F32)[16 - (KCONV - 1) :].astype(BF16)
 
 
 def mix_kernel(at, x, w, keys_out, values_out, x_out, scratch, *, other):
@@ -164,6 +165,16 @@
                 values_out[h] = m
 
 
+def at_head(h):
+    return pl.ds(pl.multiple_of(h * DK, DK), DK)
+
+
+def picked(at, which):
+    if which is None:
+        return list(HEADS)
+    return [lax.rem(at[2] + d, 4) for d in which]
+
+
 def rim_of(at, rim, cols):
     first = at[0] + at[1] + at[2] + at[3] == 0
     return jnp.where(first, 0.0, rim[:, cols].astype(F32))
@@ -176,22 +187,24 @@
 
 
 def local_kernel(
-    at, keys_in, values_in, x, w, rim, beta, trans_out, keys_out, solved_out, scratch, *, other
+    at, keys_in, values_in, x, w, rim, beta, trans_out, keys_out, solved_out, scratch, *, other, which
 ):
     half = half_of(at, other)
-
-    def with_rim(p, h, rest):
+    heads = picked(at, which)
+    n = len(heads)
+
+    def with_rim(p, i, h, rest):
         first = first_rows(
             rim_of(at, rim, head_columns(p + 1, half, h)),
-            x[p, :, columns(h)],
+            x[p, :, at_head(h)],
             w[:, head_columns(p + 1, half, h)],
-            scratch.at[p, h],
+            scratch.at[p, i],
         )
         return jnp.concatenate([unit(first) if p == 0 else first, rest[h, 8:, :]], 0)
 
-    keys = [with_rim(0, h, keys_in) for h in HEADS]
-    values = [with_rim(1, h, values_in) for h in HEADS]
-    keys_t = [k.T * beta[pl.ds(half * HALF + h, 1), :] for h, k in zip(HEADS, keys)]
+    keys = [with_rim(0, i, h, keys_in) for i, h in enumerate(heads)]
+    values = [with_rim(1, i, h, values_in) for i, h in enumerate(heads)]
+    keys_t = [k.T * beta[pl.ds(half * HALF + h, 1), :] for h, k in zip(heads, keys)]
     r, c = places(128)
     strict = r > c
     top = [jnp.where(strict, mm(k[:128], kt[:, :128]), 0.0) for k, kt in zip(keys, keys_t)]
@@ -199,30 +212,34 @@
     inner = top + [jnp.where(strict, a[:, 128:], 0.0) for a in below]
     right = [jnp.concatenate([k, v], 1) for k, v in zip(keys, values)]
     inv = unit_lower_inverses(inner)
-    first = [mmw(d, x[:128]) for d, x in zip(inv[:HALF], right)]
+    first = [mmw(d, x[:128]) for d, x in zip(inv[:n], right)]
     rest = [x[128:] - mmw(a[:, :128], y) for x, a, y in zip(right, below, first)]
-    second = [mmw(d, z) for d, z in zip(inv[HALF:], rest)]
+    second = [mmw(d, z) for d, z in zip(inv[n:], rest)]
     solved = [jnp.concatenate([a, b], 0) for a, b in zip(first, second)]
     trans = [mmw(kt, y) for kt, y in zip(keys_t, solved)]
-    for h in HEADS:
+    for h in range(n):
         trans_out[h, :, :DK] = jnp.where(r == c, 1.0, 0.0) - trans[h][:, :DK]
         trans_out[h, :, DK:] = trans[h][:, DK:]
         keys_out[h] = keys_t[h]
         solved_out[h] = solved[h]
 
 
-def output_kernel(at, x, rim, w, keys_t, solved, q_out, o_out, token, scratch, *, other):
+def output_kernel(at, x, rim, w, *refs, other, which):
+    blocks, (q_out, o_out, token, scratch) = refs[:-4], refs[-4:]
     token[...] = jnp.zeros_like(token)
     half = half_of(at, other)
+    size = HALF * 2 // len(blocks)
+    keys_t = [blocks[2 * (i // size)].at[i % size] for i in HEADS]
+    solved = [blocks[2 * (i // size) + 1].at[i % size] for i in HEADS]
     queries = []
-    for h in HEADS:
-        held, cols = scratch.at[h], head_columns(0, half, h)
+    for i, h in enumerate(picked(at, which)):
+        held, cols = scratch.at[i], head_columns(0, half, h)
         held[5:8, :] = rim_of(at, rim, cols)
         held[8 : 8 + ROWS, :] = x[:, cols].astype(F32)
         queries.append(unit(taps(w[:, cols], ROWS, held, ROWS)))
     r, c = places(ROWS)
-    scores = [jnp.where(r >= c, mmw(q, keys_t[h]), 0.0) for h, q in zip(HEADS, queries)]
-    out = [mmw(s, solved[h]) for h, s in zip(HEADS, scores)]
+    scores = [jnp.where(r >= c, mmw(q, keys_t[h][...]), 0.0) for h, q in zip(HEADS, queries)]
+    out = [mmw(s, solved[h][...]) for h, s in zip(HEADS, scores)]
     for h in HEADS:
         q_out[h] = queries[h] - out[h][:, :DK]
         o_out[h] = out[h][:, DK:]
@@ -241,10 +258,9 @@
     return jnp.where(own_first, other, own), jnp.where(own_first, own, other)
 
 
-def chip_kernel(at, kept, came, *outs):
-    for d in range(4):
-        j = lax.rem(at[2] + d, 4)
-        outs[d][...] = compose(*ordered(at[3] == 0, kept[j], came[j]))
+def chip_kernel(at, kept, came, *outs, which):
+    for i, (out, j) in enumerate(zip(outs, picked(at, which))):
+        out[...] = compose(*ordered(at[3] == 0, kept[i], came[j]))
 
 
 def y_kernel(at, b0, b2, b1, b3, total, prefixes, held):
@@ -276,50 +292,48 @@
     total[...] = compose(upper, two)
 
 
-def z1_kernel(at, own, got, second):
-    later, earlier = ordered(at[0] % 2 == 0, own[...], got[...])
-    second[...] = enter(later, earlier[:, DK:])
-
-
-def z2_kernel(at, got_z, got_second, x_prefix, y_prefixes, s0, s1, s2, s3, states):
-    z, y = at[0], at[2]
-    state = jnp.where(
-        z < 2,
-        jnp.where(z == 0, 0.0, got_z[:, DK:]),
-        jnp.where(z == 2, got_second[...], enter(got_z[...], got_second[...])),
-    )
-    state = enter(x_prefix[...], state)
-    states[0] = state
+def prefix_kernel(at, x_prefix, y_prefixes, out):
+    out[0] = x_prefix[...]
     for i in range(3):
-        states[i + 1] = enter(y_prefixes[i], state)
+        out[i + 1] = compose(y_prefixes[i], x_prefix[...])
+
+
+def z_kernel(at, b1, b3, b2, prefixes, s0, s1, s2, s3, states):
+    y, z = at[2], at[0]
+    state = jnp.where(z >= 3, b3[:, DK:], 0.0)
+    state = jnp.where(z >= 2, enter(b2[...], state), 0.0)
+    state = jnp.where(z >= 1, enter(b1[...], state), 0.0)
+    for i in range(4):
+        states[i] = enter(prefixes[i], state)
     for d, out in enumerate((s0, s1, s2, s3)):
         out[...] = states[lax.rem(y + d, 4)]
 
 
-def core_kernel(at, kept, came, s0, s2, s1, s3, stays, goes):
+def core_kernel(at, kept_a, kept_b, came, s0, s2, s1, s3, stays, goes):
     y, low = at[2], at[3] == 0
+    own = kept_a[1], kept_b[1], kept_a[0], kept_b[0]
     for d, state in enumerate((s0, s1, s2, s3)):
         j = lax.rem(y + 4 - d, 4)
         first = state[...]
-        second = enter(jnp.where(low, kept[j], came[j]), first)
+        second = enter(jnp.where(low, own[d], came[j]), first)
         stays[j] = jnp.where(low, first, second)
         goes[j] = jnp.where(low, second, first)
 
 
-def finished(q, o, s, gain, h):
-    r = mm(q[h], s[h]) + o[h]
+def finished(q, o, s, gain, i, h):
+    r = mm(q[i], s[h]) + o[i]
     return (r * lax.rsqrt(jnp.mean(r * r, -1, keepdims=True) + 1e-06) * gain[...]).astype(BF16)
 
 
 def final_own_kernel(at, q, o, s, gain, out):
-    for h in HEADS:
-        out[:, columns(h)] = finished(q, o, s, gain, h)
+    for i, h in enumerate(picked(at, OWN)):
+        out[:, at_head(h)] = finished(q, o, s, gain, i, h)
 
 
 def final_kernel(at, q, o, s, gain, own, out):
     for h in HEADS:
         out[:, head_columns(0, at[3], h)] = own[:, columns(h)]
-        out[:, head_columns(0, 1 - at[3], h)] = finished(q, o, s, gain, h)
+        out[:, head_columns(0, 1 - at[3], h)] = finished(q, o, s, gain, h, h)
 
 
 class Place:
@@ -353,8 +367,8 @@
     return step(
         fetch_kernel,
         (),
-        [jax.ShapeDtypeStruct((KCONV - 1, 3 * H * DK), BF16), x, x],
-        [pltpu.VMEM((16, 3 * H * DK), BF16), pltpu.SemaphoreType.DMA((5,))],
+        [x, x],
+        [pltpu.SemaphoreType.DMA((4,))],
         vmem=FETCH_BYTES,
         hbm=(projected,),
         flops=FETCH_FLOPS,
@@ -370,33 +384,30 @@
     )
 
 
-def local_call(mixes, weight, rim, beta, other, after=()):
-    outs = [shaped(HALF, DK, 2 * DK), shaped(HALF, DK, ROWS), shaped(HALF, ROWS, 2 * DK)]
+def local_call(mixes, weight, rim, beta, other, which=None, after=()):
+    n = HALF if which is None else len(which)
+    outs = [shaped(n, DK, 2 * DK), shaped(n, DK, ROWS), shaped(n, ROWS, 2 * DK)]
     return step(
-        functools.partial(local_kernel, other=other),
+        functools.partial(local_kernel, other=other, which=which),
         (*mixes, weight, rim, beta),
         outs,
-        [pltpu.VMEM((2, HALF, 16, DK), F32)],
+        [pltpu.VMEM((2, n, 16, DK), F32)],
         after,
     )
 
 
-def output_call(projected, rim, weight, keys_t, solved, other):
+def output_call(projected, rim, weight, blocks, other, which=None):
     outs = [shaped(HALF, ROWS, DK), shaped(HALF, ROWS, DK), shaped(8, DK)]
     return step(
-        functools.partial(output_kernel, other=other),
-        (projected, rim, weight, keys_t, solved),
+        functools.partial(output_kernel, other=other, which=which),
+        (projected, rim, weight, *blocks),
         outs,
         [pltpu.VMEM((HALF, ROWS + 8, DK), F32)],
     )
 
 
-def exchange(block, axis, partner):
-    return lax.ppermute(block, axis, [(i, partner(i)) for i in range(lax.axis_size(axis))])
-
-
 def swap(block):
-    return exchange(block, "core", lambda i: 1 - i)
+    return lax.ppermute(block, "core", [(0, 1), (1, 0)])
 
 
 def shift(block, axis, distance):
@@ -412,43 +423,46 @@
     gain = gain.reshape(1, DK)
     one, state = shaped(DK, 2 * DK), shaped(DK, DK)
 
-    last, x_far, x_own = fetch_call(projected)
+    x_far, x_own = fetch_call(projected)
+    last = projected[ROWS - (KCONV - 1) :]
     count = lax.axis_size(ALL)
     rim = lax.ppermute(last, ALL, [(i, (i + 1) % count) for i in range(count)])
     mixes_far = mix_call(x_far, weight, True)
     mixes_own = mix_call(x_own, weight, False)
-    sent, keys_far, solved_far = local_call(
-        mixes_far, weight, rim, beta, True, mixes_own[2:]
-    )
+    sent, *far = local_call(mixes_far, weight, rim, beta, True, after=mixes_own[2:])
     came = swap(sent)
-    kept, keys_own, solved_own = local_call(mixes_own, weight, rim, beta, False)
-    chip = step(chip_kernel, (kept, came), [one] * 4)
+    kept_a, *own_a = local_call(mixes_own, weight, rim, beta, False, FIRST)
+    chip_a = functools.partial(chip_kernel, which=FIRST)
+    across, own = step(chip_a, (kept_a, came), [one, one])
+    first, across = across, shift(across, "y", 2)
+    kept_b, *own_b = local_call(mixes_own, weight, rim, beta, False, SECOND, (first,))
+    chip_b = functools.partial(chip_kernel, which=SECOND)
+    after, before = step(chip_b, (kept_b, came), [one, one])
 
     held = pltpu.VMEM((4, DK, 2 * DK), F32)
-    b1, b2, b3 = ring_of(chip[1:], "y")
-    q_far, o_far, far_done = output_call(projected, rim, weight, keys_far, solved_far, True)
-    q_own, o_own, own_done = output_call(projected, rim, weight, keys_own, solved_own, False)
+    b1, b2, b3 = shift(after, "y", 1), across, shift(before, "y", 3)
+    q_far, o_far, far_done = output_call(projected, rim, weight, far, True)
+    q_own, o_own, own_done = output_call(projected, rim, weight, own_a + own_b, False, OWN)
     trans, y_prefixes = step(
         y_kernel,
-        (chip[0], b2, b1, b3),
+        (own, b2, b1, b3),
         [one, shaped(3, DK, 2 * DK)],
         [held],
         (far_done, own_done),
     )
     b1, b2, b3 = ring_of([trans] * 3, "x")
     trans, x_prefix = step(x_kernel, (trans, b1, b3, b2), [one, one], [held])
-    got_z = exchange(trans, "z", lambda i: i ^ 1)
-    (second,) = step(z1_kernel, (trans, got_z), [state])
-    got_second = exchange(second, "z", lambda i: 3 - i)
+    b1, b2, b3 = ring_of([trans] * 3, "z")
+    (prefixes,) = step(prefix_kernel, (x_prefix, y_prefixes), [shaped(4, DK, 2 * DK)])
 
     states = step(
-        z2_kernel,
-        (got_z, got_second, x_prefix, y_prefixes),
+        z_kernel,
+        (b1, b3, b2, prefixes),
         [state] * 4,
         [pltpu.VMEM((4, DK, DK), F32)],
     )
     s1, s2, s3 = ring_of(states[1:], "y")
-    s_own, goes = step(core_kernel, (kept, came, states[0], s2, s1, s3), [shaped(HALF, DK, DK)] * 2)
+    s_own, goes = step(core_kernel, (kept_a, kept_b, came, states[0], s2, s1, s3), [shaped(HALF, DK, DK)] * 2)
     s_far = swap(goes)
     half = jax.ShapeDtypeStruct((ROWS, HALF * DK), BF16)
     (own,) = step(final_own_kernel, (q_own, o_own, s_own, gain), [half])

time: 61.1 us -> 59 us (0.966)
  waiting for transfers between devices: 23.9 us -> 19.8 us
  Pallas kernels: 15.2 us -> 17.4 us
  starting transfers between devices: 21.7 us -> 20.6 us
  local copies, waits for them, and re-layouts: 0.02 us -> 0.84 us
    ppermute x4 -> x2, waiting for transfers between devices: 9.49 us -> 0.73 us  [swap(): return lax.ppermute(block, 'core', [(0, 1), (1, 0)])]
    ppermute x9 -> x12, waiting for transfers between devices: 14.4 us -> 19 us  [shift(): lax.ppermute(block, axis, [(i, (i + distance) % n) for i in range(n)])]
    ppermute x4 -> x2, starting transfers between devices: 11.2 us -> 8.5 us  [swap(): return lax.ppermute(block, 'core', [(0, 1), (1, 0)])]
    pallas_call x15 -> x17, Pallas kernels: 15.2 us -> 17.4 us  [step(): pl.pallas_call(body, in_specs=[pl.BlockSpec()] * len(args) + [anywhere] *...]
    ppermute x9 -> x12, starting transfers between devices: 7.66 us -> 9.38 us  [shift(): lax.ppermute(block, axis, [(i, (i + distance) % n) for i in range(n)])]
    slice x0 -> x1, local copies, waits for them, and re-layouts: none -> 0.81 us  [shards(): last = projected[ROWS - (KCONV - 1):]]
  transfers between devices with their start and end apart: 14 -> 15, of which waited for: 9 -> 8; matrix products, arithmetic and copies ran while one was open for 0% -> 0% of each run, Pallas kernels for 12% -> 19%
where the time goes in v5:
time: 59 us; the launch traced here: 58.9 us
  starting transfers between devices  20.6 us (35%)
  waiting for transfers between devices  19.8 us (34%)
  Pallas kernels  17.4 us (29%)
  local copies, waits for them, and re-layouts  0.84 us (1%)
    ppermute x12, waiting for transfers between devices, shift(): lax.ppermute(block, axis, [(i, (i + distance) % n) for i in range(n)])  19 us
    pallas_call x17, Pallas kernels, step(): pl.pallas_call(body, in_specs=[pl.BlockSpec()] * len(args) + [anywhere] *...  17.4 us
    ppermute x12, starting transfers between devices, shift(): lax.ppermute(block, axis, [(i, (i + distance) % n) for i in range(n)])  9.38 us
    ppermute x2, starting transfers between devices, swap(): return lax.ppermute(block, 'core', [(0, 1), (1, 0)])  8.5 us
    ppermute x1, starting transfers between devices, shards(): rim = lax.ppermute(last, ALL, [(i, (i + 1) % count) for i in range(count)])  2.76 us
  transfers between devices with their start and end apart: 15, of which 8 were waited for; matrix products, arithmetic and copies ran while one was open for 0% of the time, Pallas kernels for 19%

profile of v5, /device:TPU:1, one launch (start us, length us, event | category | flops | bytes accessed | tf_op | source)
XLA Modules:
  0.0 58.9 jit_solution(3668267996037086360)
XLA Ops:
  0.0 0.8 %slice.3 = bf16[3,3072]{1,0:T(4,128)(2,1)S(1)} slice(bf16[256,3072]{1,0:T(8,128)(2,1)} %refs_0_.5), slice={[253:256], [0:3072]} | slice | bytes 36864 | tf_op jit(solution)/shard_map/slice | solution.py:427
  0.8 0.0 copy-start.1
  0.8 0.0 copy-start.2
  0.8 2.8 %collective-permute-start = (bf16[3,3072]{1,0:T(4,128)(2,1)S(1)}, bf16[3,3072]{1,0:T(4,128)(2,1)S(1)}, u32[]{:S(2)}, u32[]{:S(2)}) collective-permute-start(bf16[3,3072]{1,0:T(4,128)(2,1)S(1)} %slice.3), channel_id=1, source_target_pairs={{0,1},{1,2},{2,3},{3,4},{4,5},{5,6},{6,7},{7,8},{8,9},{9,10},{10,1... | collective-permute-start | bytes 55304 | tf_op jit(solution)/shard_map/ppermute | solution.py:429
  3.6 1.2 %shard_map.46 = (bf16[2,256,512]{2,1,0:T(8,128)(2,1)S(1)}, bf16[2,256,512]{2,1,0:T(8,128)(2,1)S(1)}) custom-call(bf16[256,3072]{1,0:T(8,128)(2,1)} %refs_0_.5), custom_call_target="tpu_custom_call" | custom-call | flops 1000000000 | bytes 1024 | tf_op jit(solution)/shard_map/pallas_call | solution.py:351
  4.8 0.0 copy-done.1
  4.8 0.7 %shard_map.47 = (f32[4,256,128]{2,1,0:T(8,128)S(1)}, f32[4,256,128]{2,1,0:T(8,128)S(1)}, f32[2,8,512]{2,1,0:T(8,128)S(1)}) custom-call(bf16[2,256,512]{2,1,0:T(8,128)(2,1)S(1)} %get-tuple-element.42.refs_0_, f32[4,3072]{1,0:T(4,128)S(1)} %copy-done.1), custom_call_target="tpu_custom_call" | custom-call | flops 1000000 | bytes 1024 | tf_op jit(solution)/shard_map/pallas_call | solution.py:351
  5.6 0.7 %shard_map.48 = (f32[4,256,128]{2,1,0:T(8,128)S(1)}, f32[4,256,128]{2,1,0:T(8,128)S(1)}, f32[2,8,512]{2,1,0:T(8,128)S(1)}) custom-call(bf16[2,256,512]{2,1,0:T(8,128)(2,1)S(1)} %get-tuple-element.46.refs_0_, f32[4,3072]{1,0:T(4,128)S(1)} %copy-done.1), custom_call_target="tpu_custom_call" | custom-call | flops 1000000 | bytes 1024 | tf_op jit(solution)/shard_map/pallas_call | solution.py:351
  6.3 0.0 collective-permute-done.refs_4_.refs_1_
  6.3 0.0 copy-done.2
  6.3 3.0 %shard_map.49 = (f32[4,128,256]{2,1,0:T(8,128)S(1)}, f32[4,128,256]{2,1,0:T(8,128)S(1)}, f32[4,256,256]{2,1,0:T(8,128)S(1)}) custom-call(f32[4,256,128]{2,1,0:T(8,128)S(1)} %get-tuple-element.43.refs_0_, f32[4,256,128]{2,1,0:T(8,128)S(1)} %get-tuple-element.44.refs_1_, f32[2,8,512]{2,1,0:T(8,128)S(1)} %get-tuple-element.45.refs_2_, f32[4,3072]{1,0:T(4,128)S(1)} %copy-done.1, ...), custom_call_target="tpu_custom_call" | custom-call | flops 1000000 | bytes 1024 | tf_op jit(solution)/shard_map/pallas_call | solution.py:351
  9.4 5.8 %collective-permute-start.1 = (f32[4,128,256]{2,1,0:T(8,128)S(1)}, f32[4,128,256]{2,1,0:T(8,128)S(1)}, u32[]{:S(2)}, u32[]{:S(2)}) collective-permute-start(f32[4,128,256]{2,1,0:T(8,128)S(1)} %get-tuple-element.55), channel_id=1, source_target_pairs={{0,1},{1,0},{2,3},{3,2},{4,5},{5,4},{6,7},{7,6},{8,9},{9,8},{10,11... | collective-permute-start | bytes 1572872 | tf_op jit(solution)/shard_map/ppermute | solution.py:410
  15.2 2.5 %shard_map.51 = (f32[2,128,256]{2,1,0:T(8,128)S(1)}, f32[2,128,256]{2,1,0:T(8,128)S(1)}, f32[2,256,256]{2,1,0:T(8,128)S(1)}) custom-call(f32[4,256,128]{2,1,0:T(8,128)S(1)} %get-tuple-element.52.refs_0_, f32[4,256,128]{2,1,0:T(8,128)S(1)} %get-tuple-element.53.refs_1_, f32[2,8,512]{2,1,0:T(8,128)S(1)} %get-tuple-element.47.refs_6_.refs_2_, ...), custom_call_target="tpu_custom_call" | custom-call | flops 1000000 | bytes 1024 | tf_op jit(solution)/shard_map/pallas_call | solution.py:351
  17.7 0.0 copy-start
  17.7 0.0 collective-permute-done.1.refs_1_.refs_2_
  17.7 0.3 shard_map.52
  18.0 0.1 collective-permute-start.2
  18.1 2.5 %shard_map.53 = (f32[2,128,256]{2,1,0:T(8,128)S(1)}, f32[2,128,256]{2,1,0:T(8,128)S(1)}, f32[2,256,256]{2,1,0:T(8,128)S(1)}) custom-call(f32[4,256,128]{2,1,0:T(8,128)S(1)} %get-tuple-element.52.refs_0_, f32[4,256,128]{2,1,0:T(8,128)S(1)} %get-tuple-element.53.refs_1_, f32[2,8,512]{2,1,0:T(8,128)S(1)} %get-tuple-element.47.refs_6_.refs_2_, ...), custom_call_target="tpu_custom_call" | custom-call | flops 1000000 | bytes 1024 | tf_op jit(solution)/shard_map/pallas_call | solution.py:351
  20.6 0.3 shard_map.54
  20.8 0.1 collective-permute-start.3
  20.9 2.7 %collective-permute-start.4 = (f32[128,256]{1,0:T(8,128)S(1)}, f32[128,256]{1,0:T(8,128)S(1)}, u32[]{:S(2)}, u32[]{:S(2)}) collective-permute-start(f32[128,256]{1,0:T(8,128)S(1)} %get-tuple-element.60), channel_id=1, source_target_pairs={{0,6},{2,0},{4,2},{6,4},{1,7},{3,1},{5,3},{7,5},{8,14},{10,8},{12,... | collective-permute-start | bytes 393224 | tf_op jit(solution)/shard_map/ppermute | solution.py:415
  23.6 0.0 copy-done
  23.6 1.2 %shard_map.50 = (f32[4,256,128]{2,1,0:T(8,128)S(1)}, f32[4,256,128]{2,1,0:T(8,128)S(1)}, f32[8,128]{1,0:T(8,128)S(1)}) custom-call(bf16[256,3072]{1,0:T(8,128)(2,1)S(1)} %copy-done, bf16[3,3072]{1,0:T(4,128)(2,1)S(1)} %collective-permute-done.refs_4_.refs_1_, f32[4,3072]{1,0:T(4,128)S(1)} %copy-done.1, f32[4,128,256]{2,1,0:T(8,128)S(1)} %get-tuple-element.48.refs_3_, ...), custom_call_target="tpu_custom_call" | custom-call | flops 1000000 | bytes 1024 | tf_op jit(solution)/shard_map/pallas_call | solution.py:351
  24.8 1.2 %shard_map.55 = (f32[4,256,128]{2,1,0:T(8,128)S(1)}, f32[4,256,128]{2,1,0:T(8,128)S(1)}, f32[8,128]{1,0:T(8,128)S(1)}) custom-call(bf16[256,3072]{1,0:T(8,128)(2,1)S(1)} %copy-done, bf16[3,3072]{1,0:T(4,128)(2,1)S(1)} %collective-permute-done.refs_4_.refs_1_, f32[4,3072]{1,0:T(4,128)S(1)} %copy-done.1, f32[2,128,256]{2,1,0:T(8,128)S(1)} %get-tuple-element.62.refs_3_, ...), custom_call_target="tpu_custom_call" | custom-call | flops 1000000 | bytes 1024 | tf_op jit(solution)/shard_map/pallas_call | solution.py:351
  26.0 0.0 collective-permute-done.2.refs_1_
  26.1 1.6 %collective-permute-done.3.refs_2_ = f32[128,256]{1,0:T(8,128)S(1)} collective-permute-done((f32[128,256]{1,0:T(8,128)S(1)}, f32[128,256]{1,0:T(8,128)S(1)}, u32[]{:S(2)}, u32[]{:S(2)}) %collective-permute-start.3) | collective-permute-done | bytes 131104 | tf_op jit(solution)/shard_map/ppermute | solution.py:415
  27.6 0.0 collective-permute-done.4.refs_3_
  27.6 0.5 shard_map.56
  28.1 0.1 collective-permute-start.7
  28.2 0.1 collective-permute-start.6
  28.3 1.5 %collective-permute-start.5 = (f32[128,256]{1,0:T(8,128)S(1)}, f32[128,256]{1,0:T(8,128)S(1)}, u32[]{:S(2)}, u32[]{:S(2)}) collective-permute-start(f32[128,256]{1,0:T(8,128)S(1)} %get-tuple-element.67.refs_0_), channel_id=1, source_target_pairs={{0,8},{8,16},{16,24},{24,0},{1,9},{9,17},{17,25},{25,1},{2,10},{10... | collective-permute-start | bytes 393224 | tf_op jit(solution)/shard_map/ppermute | solution.py:415
  29.7 4.4 %collective-permute-done.7.refs_3_ = f32[128,256]{1,0:T(8,128)S(1)} collective-permute-done((f32[128,256]{1,0:T(8,128)S(1)}, f32[128,256]{1,0:T(8,128)S(1)}, u32[]{:S(2)}, u32[]{:S(2)}) %collective-permute-start.7) | collective-permute-done | bytes 131104 | tf_op jit(solution)/shard_map/ppermute | solution.py:415
  34.1 0.0 collective-permute-done.6.refs_2_
  34.1 3.8 %collective-permute-done.5.refs_1_ = f32[128,256]{1,0:T(8,128)S(1)} collective-permute-done((f32[128,256]{1,0:T(8,128)S(1)}, f32[128,256]{1,0:T(8,128)S(1)}, u32[]{:S(2)}, u32[]{:S(2)}) %collective-permute-start.5) | collective-permute-done | bytes 131104 | tf_op jit(solution)/shard_map/ppermute | solution.py:415
  37.9 0.5 shard_map.57
  38.4 0.5 collective-permute-start.10
  38.9 0.4 collective-permute-start.9
  39.4 1.1 %collective-permute-start.8 = (f32[128,256]{1,0:T(8,128)S(1)}, f32[128,256]{1,0:T(8,128)S(1)}, u32[]{:S(2)}, u32[]{:S(2)}) collective-permute-start(f32[128,256]{1,0:T(8,128)S(1)} %get-tuple-element.68), channel_id=1, source_target_pairs={{0,32},{32,64},{64,96},{96,0},{1,33},{33,65},{65,97},{97,1},{2,34}... | collective-permute-start | bytes 393224 | tf_op jit(solution)/shard_map/ppermute | solution.py:415
  40.4 0.0 copy-start.3
  40.4 0.3 shard_map.58.refs_3_
  40.7 3.9 %collective-permute-done.10.refs_2_ = f32[128,256]{1,0:T(8,128)S(1)} collective-permute-done((f32[128,256]{1,0:T(8,128)S(1)}, f32[128,256]{1,0:T(8,128)S(1)}, u32[]{:S(2)}, u32[]{:S(2)}) %collective-permute-start.10) | collective-permute-done | bytes 131104 | tf_op jit(solution)/shard_map/ppermute | solution.py:415
  44.5 0.0 collective-permute-done.9.refs_1_
  44.6 3.0 %collective-permute-done.8.refs_0_ = f32[128,256]{1,0:T(8,128)S(1)} collective-permute-done((f32[128,256]{1,0:T(8,128)S(1)}, f32[128,256]{1,0:T(8,128)S(1)}, u32[]{:S(2)}, u32[]{:S(2)}) %collective-permute-start.8) | collective-permute-done | bytes 131104 | tf_op jit(solution)/shard_map/ppermute | solution.py:415
  47.6 0.6 %shard_map.59 = (f32[128,128]{1,0:T(8,128)S(1)}, f32[128,128]{1,0:T(8,128)S(1)}, f32[128,128]{1,0:T(8,128)S(1)}, f32[128,128]{1,0:T(8,128)S(1)}) custom-call(f32[128,256]{1,0:T(8,128)S(1)} %collective-permute-done.8.refs_0_, f32[128,256]{1,0:T(8,128)S(1)} %collective-permute-done.9.refs_1_, f32[128,256]{1,0:T(8,128)S(1)} %collective-permute-done.10.refs_2_, ...), custom_call_target="tpu_custom_call" | custom-call | flops 1000000 | bytes 1024 | tf_op jit(solution)/shard_map/pallas_call | solution.py:351
  48.2 0.3 collective-permute-start.11
  48.5 0.8 %collective-permute-start.12 = (f32[128,128]{1,0:T(8,128)S(1)}, f32[128,128]{1,0:T(8,128)S(1)}, u32[]{:S(2)}, u32[]{:S(2)}) collective-permute-start(f32[128,128]{1,0:T(8,128)S(1)} %get-tuple-element.73), channel_id=1, source_target_pairs={{0,2},{2,4},{4,6},{6,0},{1,3},{3,5},{5,7},{7,1},{8,10},{10,12},{12... | collective-permute-start | bytes 196616 | tf_op jit(solution)/shard_map/ppermute | solution.py:415
  49.3 1.9 %collective-permute-start.13 = (f32[128,128]{1,0:T(8,128)S(1)}, f32[128,128]{1,0:T(8,128)S(1)}, u32[]{:S(2)}, u32[]{:S(2)}) collective-permute-start(f32[128,128]{1,0:T(8,128)S(1)} %get-tuple-element.74), channel_id=1, source_target_pairs={{0,6},{2,0},{4,2},{6,4},{1,7},{3,1},{5,3},{7,5},{8,14},{10,8},{12,... | collective-permute-start | bytes 196616 | tf_op jit(solution)/shard_map/ppermute | solution.py:415
  51.2 1.9 %collective-permute-done.11.refs_4_ = f32[128,128]{1,0:T(8,128)S(1)} collective-permute-done((f32[128,128]{1,0:T(8,128)S(1)}, f32[128,128]{1,0:T(8,128)S(1)}, u32[]{:S(2)}, u32[]{:S(2)}) %collective-permute-start.11) | collective-permute-done | bytes 65568 | tf_op jit(solution)/shard_map/ppermute | solution.py:415
  53.1 0.5 collective-permute-done.12.refs_5_
  53.5 0.0 collective-permute-done.13.refs_6_
  53.5 0.2 shard_map.60
  53.8 2.7 %collective-permute-start.14 = (f32[4,128,128]{2,1,0:T(8,128)S(1)}, f32[4,128,128]{2,1,0:T(8,128)S(1)}, u32[]{:S(2)}, u32[]{:S(2)}) collective-permute-start(f32[4,128,128]{2,1,0:T(8,128)S(1)} %get-tuple-element.75), channel_id=1, source_target_pairs={{0,1},{1,0},{2,3},{3,2},{4,5},{5,4},{6,7},{7,6},{8,9},{9,8},{10,11... | collective-permute-start | bytes 786440 | tf_op jit(solution)/shard_map/ppermute | solution.py:410
  56.5 0.0 copy-done.3
  56.5 0.4 shard_map.61.refs_4_
  56.9 0.7 %collective-permute-done.14.refs_2_ = f32[4,128,128]{2,1,0:T(8,128)S(1)} collective-permute-done((f32[4,128,128]{2,1,0:T(8,128)S(1)}, f32[4,128,128]{2,1,0:T(8,128)S(1)}, u32[]{:S(2)}, u32[]{:S(2)}) %collective-permute-start.14) | collective-permute-done | bytes 262176 | tf_op jit(solution)/shard_map/ppermute | solution.py:410
  57.7 1.2 %shard_map.62 = bf16[256,1024]{1,0:T(8,128)(2,1)} custom-call(f32[4,256,128]{2,1,0:T(8,128)S(1)} %get-tuple-element.50.refs_0_, f32[4,256,128]{2,1,0:T(8,128)S(1)} %get-tuple-element.51.refs_1_, f32[4,128,128]{2,1,0:T(8,128)S(1)} %collective-permute-done.14.refs_2_, f32[1,128]{1,0:T(1,128)S(1)} %bitcast.2, bf16[256,512]{1,0:T(8,128)(2,1)S(1)} %shard_map.61.refs_4_), custom_call_target="tpu_custom_call" | custom-call | flops 1000000 | bytes 1024 | tf_op jit(solution)/shard_map/pallas_call | solution.py:351
Async XLA Ops:
  0.8 4.0 %copy-start.1 = (f32[4,3072]{1,0:T(4,128)S(1)}, f32[4,3072]{1,0:T(4,128)}, u32[]{:S(2)}) copy-start(f32[4,3072]{1,0:T(4,128)} %refs_2_.3) | copy-start | bytes 147460
  0.8 5.5 %copy-start.2 = (f32[8,256]{1,0:T(8,128)S(1)}, f32[8,256]{1,0:T(8,128)}, u32[]{:S(2)}) copy-start(f32[8,256]{1,0:T(8,128)} %refs_5_.5) | copy-start | bytes 24580
  0.8 5.5 %collective-permute-start = (bf16[3,3072]{1,0:T(4,128)(2,1)S(1)}, bf16[3,3072]{1,0:T(4,128)(2,1)S(1)}, u32[]{:S(2)}, u32[]{:S(2)}) collective-permute-start(bf16[3,3072]{1,0:T(4,128)(2,1)S(1)} %slice.3), channel_id=1, source_target_pairs={{0,1},{1,2},{2,3},{3,4},{4,5},{5,6},{6,7},{7,8},{8,9},{9,10},{10,1... | collective-permute-start | bytes 55304 | tf_op jit(solution)/shard_map/ppermute | solution.py:429
  9.4 8.3 %collective-permute-start.1 = (f32[4,128,256]{2,1,0:T(8,128)S(1)}, f32[4,128,256]{2,1,0:T(8,128)S(1)}, u32[]{:S(2)}, u32[]{:S(2)}) collective-permute-start(f32[4,128,256]{2,1,0:T(8,128)S(1)} %get-tuple-element.55), channel_id=1, source_target_pairs={{0,1},{1,0},{2,3},{3,2},{4,5},{5,4},{6,7},{7,6},{8,9},{9,8},{10,11... | collective-permute-start | bytes 1572872 | tf_op jit(solution)/shard_map/ppermute | solution.py:410
  17.7 5.9 %copy-start = (bf16[256,3072]{1,0:T(8,128)(2,1)S(1)}, bf16[256,3072]{1,0:T(8,128)(2,1)}, u32[]{:S(2)}) copy-start(bf16[256,3072]{1,0:T(8,128)(2,1)} %refs_0_.5) | copy-start | bytes 4718596
  18.0 8.1 %collective-permute-start.2 = (f32[128,256]{1,0:T(8,128)S(1)}, f32[128,256]{1,0:T(8,128)S(1)}, u32[]{:S(2)}, u32[]{:S(2)}) collective-permute-start(f32[128,256]{1,0:T(8,128)S(1)} %get-tuple-element.56.refs_6_), channel_id=1, source_target_pairs={{0,4},{2,6},{4,0},{6,2},{1,5},{3,7},{5,1},{7,3},{8,12},{10,14},{12... | collective-permute-start | bytes 393224 | tf_op jit(solution)/shard_map/ppermute | solution.py:415
  20.8 6.8 %collective-permute-start.3 = (f32[128,256]{1,0:T(8,128)S(1)}, f32[128,256]{1,0:T(8,128)S(1)}, u32[]{:S(2)}, u32[]{:S(2)}) collective-permute-start(f32[128,256]{1,0:T(8,128)S(1)} %get-tuple-element.59), channel_id=1, source_target_pairs={{0,2},{2,4},{4,6},{6,0},{1,3},{3,5},{5,7},{7,1},{8,10},{10,12},{12... | collective-permute-start | bytes 393224 | tf_op jit(solution)/shard_map/ppermute | solution.py:415
  20.9 6.7 %collective-permute-start.4 = (f32[128,256]{1,0:T(8,128)S(1)}, f32[128,256]{1,0:T(8,128)S(1)}, u32[]{:S(2)}, u32[]{:S(2)}) collective-permute-start(f32[128,256]{1,0:T(8,128)S(1)} %get-tuple-element.60), channel_id=1, source_target_pairs={{0,6},{2,0},{4,2},{6,4},{1,7},{3,1},{5,3},{7,5},{8,14},{10,8},{12,... | collective-permute-start | bytes 393224 | tf_op jit(solution)/shard_map/ppermute | solution.py:415
  28.1 6.0 %collective-permute-start.7 = (f32[128,256]{1,0:T(8,128)S(1)}, f32[128,256]{1,0:T(8,128)S(1)}, u32[]{:S(2)}, u32[]{:S(2)}) collective-permute-start(f32[128,256]{1,0:T(8,128)S(1)} %get-tuple-element.67.refs_0_), channel_id=1, source_target_pairs={{0,16},{8,24},{16,0},{24,8},{1,17},{9,25},{17,1},{25,9},{2,18},{10... | collective-permute-start | bytes 393224 | tf_op jit(solution)/shard_map/ppermute | solution.py:415
  28.2 5.9 %collective-permute-start.6 = (f32[128,256]{1,0:T(8,128)S(1)}, f32[128,256]{1,0:T(8,128)S(1)}, u32[]{:S(2)}, u32[]{:S(2)}) collective-permute-start(f32[128,256]{1,0:T(8,128)S(1)} %get-tuple-element.67.refs_0_), channel_id=1, source_target_pairs={{0,24},{8,0},{16,8},{24,16},{1,25},{9,1},{17,9},{25,17},{2,26},{10... | collective-permute-start | bytes 393224 | tf_op jit(solution)/shard_map/ppermute | solution.py:415
  28.3 9.6 %collective-permute-start.5 = (f32[128,256]{1,0:T(8,128)S(1)}, f32[128,256]{1,0:T(8,128)S(1)}, u32[]{:S(2)}, u32[]{:S(2)}) collective-permute-start(f32[128,256]{1,0:T(8,128)S(1)} %get-tuple-element.67.refs_0_), channel_id=1, source_target_pairs={{0,8},{8,16},{16,24},{24,0},{1,9},{9,17},{17,25},{25,1},{2,10},{10... | collective-permute-start | bytes 393224 | tf_op jit(solution)/shard_map/ppermute | solution.py:415
  38.4 6.2 %collective-permute-start.10 = (f32[128,256]{1,0:T(8,128)S(1)}, f32[128,256]{1,0:T(8,128)S(1)}, u32[]{:S(2)}, u32[]{:S(2)}) collective-permute-start(f32[128,256]{1,0:T(8,128)S(1)} %get-tuple-element.68), channel_id=1, source_target_pairs={{0,64},{32,96},{64,0},{96,32},{1,65},{33,97},{65,1},{97,33},{2,66}... | collective-permute-start | bytes 393224 | tf_op jit(solution)/shard_map/ppermute | solution.py:415
  38.9 5.6 %collective-permute-start.9 = (f32[128,256]{1,0:T(8,128)S(1)}, f32[128,256]{1,0:T(8,128)S(1)}, u32[]{:S(2)}, u32[]{:S(2)}) collective-permute-start(f32[128,256]{1,0:T(8,128)S(1)} %get-tuple-element.68), channel_id=1, source_target_pairs={{0,96},{32,0},{64,32},{96,64},{1,97},{33,1},{65,33},{97,65},{2,98}... | collective-permute-start | bytes 393224 | tf_op jit(solution)/shard_map/ppermute | solution.py:415
  39.4 8.3 %collective-permute-start.8 = (f32[128,256]{1,0:T(8,128)S(1)}, f32[128,256]{1,0:T(8,128)S(1)}, u32[]{:S(2)}, u32[]{:S(2)}) collective-permute-start(f32[128,256]{1,0:T(8,128)S(1)} %get-tuple-element.68), channel_id=1, source_target_pairs={{0,32},{32,64},{64,96},{96,0},{1,33},{33,65},{65,97},{97,1},{2,34}... | collective-permute-start | bytes 393224 | tf_op jit(solution)/shard_map/ppermute | solution.py:415
  40.4 16.1 %copy-start.3 = (f32[128]{0:T(128)S(1)}, f32[128]{0:T(128)}, u32[]{:S(2)}) copy-start(f32[128]{0:T(128)} %param.7) | copy-start | bytes 1540
  48.2 4.8 %collective-permute-start.11 = (f32[128,128]{1,0:T(8,128)S(1)}, f32[128,128]{1,0:T(8,128)S(1)}, u32[]{:S(2)}, u32[]{:S(2)}) collective-permute-start(f32[128,128]{1,0:T(8,128)S(1)} %get-tuple-element.72), channel_id=1, source_target_pairs={{0,4},{2,6},{4,0},{6,2},{1,5},{3,7},{5,1},{7,3},{8,12},{10,14},{12... | collective-permute-start | bytes 196616 | tf_op jit(solution)/shard_map/ppermute | solution.py:415
  48.5 5.0 %collective-permute-start.12 = (f32[128,128]{1,0:T(8,128)S(1)}, f32[128,128]{1,0:T(8,128)S(1)}, u32[]{:S(2)}, u32[]{:S(2)}) collective-permute-start(f32[128,128]{1,0:T(8,128)S(1)} %get-tuple-element.73), channel_id=1, source_target_pairs={{0,2},{2,4},{4,6},{6,0},{1,3},{3,5},{5,7},{7,1},{8,10},{10,12},{12... | collective-permute-start | bytes 196616 | tf_op jit(solution)/shard_map/ppermute | solution.py:415
  49.3 4.2 %collective-permute-start.13 = (f32[128,128]{1,0:T(8,128)S(1)}, f32[128,128]{1,0:T(8,128)S(1)}, u32[]{:S(2)}, u32[]{:S(2)}) collective-permute-start(f32[128,128]{1,0:T(8,128)S(1)} %get-tuple-element.74), channel_id=1, source_target_pairs={{0,6},{2,0},{4,2},{6,4},{1,7},{3,1},{5,3},{7,5},{8,14},{10,8},{12,... | collective-permute-start | bytes 196616 | tf_op jit(solution)/shard_map/ppermute | solution.py:415
  53.8 3.9 %collective-permute-start.14 = (f32[4,128,128]{2,1,0:T(8,128)S(1)}, f32[4,128,128]{2,1,0:T(8,128)S(1)}, u32[]{:S(2)}, u32[]{:S(2)}) collective-permute-start(f32[4,128,128]{2,1,0:T(8,128)S(1)} %get-tuple-element.75), channel_id=1, source_target_pairs={{0,1},{1,0},{2,3},{3,2},{4,5},{5,4},{6,7},{7,6},{8,9},{9,8},{10,11... | collective-permute-start | bytes 786440 | tf_op jit(solution)/shard_map/ppermute | solution.py:410

commit v6 on v5

--- a/solution.py
+++ b/solution.py
@@ -330,10 +330,20 @@
         out[:, at_head(h)] = finished(q, o, s, gain, i, h)
 
 
-def final_kernel(at, q, o, s, gain, own, out):
-    for h in HEADS:
-        out[:, head_columns(0, at[3], h)] = own[:, columns(h)]
-        out[:, head_columns(0, 1 - at[3], h)] = finished(q, o, s, gain, h, h)
+def final_kernel(at, q, o, s, gain, own, out, far, sems):
+    def copy(part, half, h, count, i):
+        cols = pl.ds(pl.multiple_of((half * HALF + h) * DK, count * DK), count * DK)
+        return pltpu.make_async_copy(part, out.at[:, cols], sems.at[i])
+
+    copies = [copy(own, at[3], 0, HALF, 0)]
+    copies[0].start()
+    for i in range(2):
+        for h in (2 * i, 2 * i + 1):
+            far[i, :, columns(h - 2 * i)] = finished(q, o, s, gain, h, h)
+        copies.append(copy(far.at[i], 1 - at[3], 2 * i, 2, 1 + i))
+        copies[-1].start()
+    for c in copies:
+        c.wait()
 
 
 class Place:
@@ -341,7 +351,7 @@
         return lax.axis_index(ALL[i])
 
 
-def step(kernel, args, outs, scratch=(), after=(), vmem=VMEM_BYTES, hbm=(), flops=10**6):
+def step(kernel, args, outs, scratch=(), after=(), vmem=VMEM_BYTES, hbm=(), flops=10**6, out=None):
     args, after, hbm = list(args), list(after), list(hbm)
 
     def body(*refs):
@@ -351,6 +361,7 @@
     return pl.pallas_call(
         body,
         in_specs=[pl.BlockSpec()] * len(args) + [anywhere] * (len(hbm) + len(after)),
+        out_specs=[pl.BlockSpec() if out is None else out] * len(outs),
         out_shape=list(outs),
         scratch_shapes=list(scratch),
         cost_estimate=pl.CostEstimate(flops=flops, bytes_accessed=2**10, transcendentals=0),
@@ -448,10 +459,10 @@
         (own, b2, b1, b3),
         [one, shaped(3, DK, 2 * DK)],
         [held],
-        (far_done, own_done),
+        (far_done,),
     )
     b1, b2, b3 = ring_of([trans] * 3, "x")
-    trans, x_prefix = step(x_kernel, (trans, b1, b3, b2), [one, one], [held])
+    trans, x_prefix = step(x_kernel, (trans, b1, b3, b2), [one, one], [held], (own_done,))
     b1, b2, b3 = ring_of([trans] * 3, "z")
     (prefixes,) = step(prefix_kernel, (x_prefix, y_prefixes), [shaped(4, DK, 2 * DK)])
 
@@ -467,7 +478,14 @@
     half = jax.ShapeDtypeStruct((ROWS, HALF * DK), BF16)
     (own,) = step(final_own_kernel, (q_own, o_own, s_own, gain), [half])
     out = jax.ShapeDtypeStruct((ROWS, H * DK), BF16)
-    return step(final_kernel, (q_far, o_far, s_far, gain, own), [out])[0]
+    (out,) = step(
+        final_kernel,
+        (q_far, o_far, s_far, gain, own),
+        [out],
+        [pltpu.VMEM((2, ROWS, 2 * DK), BF16), pltpu.SemaphoreType.DMA((3,))],
+        out=pl.BlockSpec(memory_space=pl.ANY),
+    )
+    return out
 
 
 def solution(mesh):

time: 59 us -> 59.1 us (level)
  no operation moved by 1% of the time
where the time goes in v6:
time: 59.1 us; the launch traced here: 58.9 us
  starting transfers between devices  20.6 us (35%)
  waiting for transfers between devices  19.8 us (34%)
  Pallas kernels  17.3 us (29%)
  local copies, waits for them, and re-layouts  0.84 us (1%)
    ppermute x12, waiting for transfers between devices, shift(): lax.ppermute(block, axis, [(i, (i + distance) % n) for i in range(n)])  19 us
    pallas_call x17, Pallas kernels, step(): pl.pallas_call(body, in_specs=[pl.BlockSpec()] * len(args) + [anywhere] *...  17.3 us
    ppermute x12, starting transfers between devices, shift(): lax.ppermute(block, axis, [(i, (i + distance) % n) for i in range(n)])  9.38 us
    ppermute x2, starting transfers between devices, swap(): return lax.ppermute(block, 'core', [(0, 1), (1, 0)])  8.5 us
    ppermute x1, starting transfers between devices, shards(): rim = lax.ppermute(last, ALL, [(i, (i + 1) % count) for i in range(count)])  2.76 us
  transfers between devices with their start and end apart: 15, of which 8 were waited for; matrix products, arithmetic and copies ran while one was open for 0% of the time, Pallas kernels for 19%

profile of v6, /device:TPU:1, one launch (start us, length us, event | category | flops | bytes accessed | tf_op | source)
XLA Modules:
  0.0 58.9 jit_solution(9337874737721545400)
XLA Ops:
  0.0 0.8 %slice.3 = bf16[3,3072]{1,0:T(4,128)(2,1)S(1)} slice(bf16[256,3072]{1,0:T(8,128)(2,1)} %refs_0_.5), slice={[253:256], [0:3072]} | slice | bytes 36864 | tf_op jit(solution)/shard_map/slice | solution.py:438
  0.8 0.0 copy-start.1
  0.8 0.0 copy-start.2
  0.8 2.8 %collective-permute-start = (bf16[3,3072]{1,0:T(4,128)(2,1)S(1)}, bf16[3,3072]{1,0:T(4,128)(2,1)S(1)}, u32[]{:S(2)}, u32[]{:S(2)}) collective-permute-start(bf16[3,3072]{1,0:T(4,128)(2,1)S(1)} %slice.3), channel_id=1, source_target_pairs={{0,1},{1,2},{2,3},{3,4},{4,5},{5,6},{6,7},{7,8},{8,9},{9,10},{10,1... | collective-permute-start | bytes 55304 | tf_op jit(solution)/shard_map/ppermute | solution.py:440
  3.6 1.2 %shard_map.46 = (bf16[2,256,512]{2,1,0:T(8,128)(2,1)S(1)}, bf16[2,256,512]{2,1,0:T(8,128)(2,1)S(1)}) custom-call(bf16[256,3072]{1,0:T(8,128)(2,1)} %refs_0_.5), custom_call_target="tpu_custom_call" | custom-call | flops 1000000000 | bytes 1024 | tf_op jit(solution)/shard_map/pallas_call | solution.py:361
  4.8 0.0 copy-done.1
  4.8 0.7 %shard_map.47 = (f32[4,256,128]{2,1,0:T(8,128)S(1)}, f32[4,256,128]{2,1,0:T(8,128)S(1)}, f32[2,8,512]{2,1,0:T(8,128)S(1)}) custom-call(bf16[2,256,512]{2,1,0:T(8,128)(2,1)S(1)} %get-tuple-element.42.refs_0_, f32[4,3072]{1,0:T(4,128)S(1)} %copy-done.1), custom_call_target="tpu_custom_call" | custom-call | flops 1000000 | bytes 1024 | tf_op jit(solution)/shard_map/pallas_call | solution.py:361
  5.6 0.7 %shard_map.48 = (f32[4,256,128]{2,1,0:T(8,128)S(1)}, f32[4,256,128]{2,1,0:T(8,128)S(1)}, f32[2,8,512]{2,1,0:T(8,128)S(1)}) custom-call(bf16[2,256,512]{2,1,0:T(8,128)(2,1)S(1)} %get-tuple-element.46.refs_0_, f32[4,3072]{1,0:T(4,128)S(1)} %copy-done.1), custom_call_target="tpu_custom_call" | custom-call | flops 1000000 | bytes 1024 | tf_op jit(solution)/shard_map/pallas_call | solution.py:361
  6.3 0.0 collective-permute-done.refs_4_.refs_1_
  6.3 0.0 copy-done.2
  6.3 3.0 %shard_map.49 = (f32[4,128,256]{2,1,0:T(8,128)S(1)}, f32[4,128,256]{2,1,0:T(8,128)S(1)}, f32[4,256,256]{2,1,0:T(8,128)S(1)}) custom-call(f32[4,256,128]{2,1,0:T(8,128)S(1)} %get-tuple-element.43.refs_0_, f32[4,256,128]{2,1,0:T(8,128)S(1)} %get-tuple-element.44.refs_1_, f32[2,8,512]{2,1,0:T(8,128)S(1)} %get-tuple-element.45.refs_2_, f32[4,3072]{1,0:T(4,128)S(1)} %copy-done.1, ...), custom_call_target="tpu_custom_call" | custom-call | flops 1000000 | bytes 1024 | tf_op jit(solution)/shard_map/pallas_call | solution.py:361
  9.4 5.8 %collective-permute-start.1 = (f32[4,128,256]{2,1,0:T(8,128)S(1)}, f32[4,128,256]{2,1,0:T(8,128)S(1)}, u32[]{:S(2)}, u32[]{:S(2)}) collective-permute-start(f32[4,128,256]{2,1,0:T(8,128)S(1)} %get-tuple-element.55), channel_id=1, source_target_pairs={{0,1},{1,0},{2,3},{3,2},{4,5},{5,4},{6,7},{7,6},{8,9},{9,8},{10,11... | collective-permute-start | bytes 1572872 | tf_op jit(solution)/shard_map/ppermute | solution.py:421
  15.2 2.5 %shard_map.51 = (f32[2,128,256]{2,1,0:T(8,128)S(1)}, f32[2,128,256]{2,1,0:T(8,128)S(1)}, f32[2,256,256]{2,1,0:T(8,128)S(1)}) custom-call(f32[4,256,128]{2,1,0:T(8,128)S(1)} %get-tuple-element.52.refs_0_, f32[4,256,128]{2,1,0:T(8,128)S(1)} %get-tuple-element.53.refs_1_, f32[2,8,512]{2,1,0:T(8,128)S(1)} %get-tuple-element.47.refs_6_.refs_2_, ...), custom_call_target="tpu_custom_call" | custom-call | flops 1000000 | bytes 1024 | tf_op jit(solution)/shard_map/pallas_call | solution.py:361
  17.7 0.0 copy-start
  17.7 0.0 collective-permute-done.1.refs_1_.refs_2_
  17.7 0.3 shard_map.52
  18.0 0.1 collective-permute-start.2
  18.1 2.5 %shard_map.53 = (f32[2,128,256]{2,1,0:T(8,128)S(1)}, f32[2,128,256]{2,1,0:T(8,128)S(1)}, f32[2,256,256]{2,1,0:T(8,128)S(1)}) custom-call(f32[4,256,128]{2,1,0:T(8,128)S(1)} %get-tuple-element.52.refs_0_, f32[4,256,128]{2,1,0:T(8,128)S(1)} %get-tuple-element.53.refs_1_, f32[2,8,512]{2,1,0:T(8,128)S(1)} %get-tuple-element.47.refs_6_.refs_2_, ...), custom_call_target="tpu_custom_call" | custom-call | flops 1000000 | bytes 1024 | tf_op jit(solution)/shard_map/pallas_call | solution.py:361
  20.6 0.3 shard_map.54
  20.8 0.1 collective-permute-start.3
  20.9 2.7 %collective-permute-start.4 = (f32[128,256]{1,0:T(8,128)S(1)}, f32[128,256]{1,0:T(8,128)S(1)}, u32[]{:S(2)}, u32[]{:S(2)}) collective-permute-start(f32[128,256]{1,0:T(8,128)S(1)} %get-tuple-element.60), channel_id=1, source_target_pairs={{0,6},{2,0},{4,2},{6,4},{1,7},{3,1},{5,3},{7,5},{8,14},{10,8},{12,... | collective-permute-start | bytes 393224 | tf_op jit(solution)/shard_map/ppermute | solution.py:426
  23.6 0.0 copy-done
  23.6 1.2 %shard_map.50 = (f32[4,256,128]{2,1,0:T(8,128)S(1)}, f32[4,256,128]{2,1,0:T(8,128)S(1)}, f32[8,128]{1,0:T(8,128)S(1)}) custom-call(bf16[256,3072]{1,0:T(8,128)(2,1)S(1)} %copy-done, bf16[3,3072]{1,0:T(4,128)(2,1)S(1)} %collective-permute-done.refs_4_.refs_1_, f32[4,3072]{1,0:T(4,128)S(1)} %copy-done.1, f32[4,128,256]{2,1,0:T(8,128)S(1)} %get-tuple-element.48.refs_3_, ...), custom_call_target="tpu_custom_call" | custom-call | flops 1000000 | bytes 1024 | tf_op jit(solution)/shard_map/pallas_call | solution.py:361
  24.8 0.0 collective-permute-done.2.refs_1_
  24.8 2.8 %collective-permute-done.3.refs_2_ = f32[128,256]{1,0:T(8,128)S(1)} collective-permute-done((f32[128,256]{1,0:T(8,128)S(1)}, f32[128,256]{1,0:T(8,128)S(1)}, u32[]{:S(2)}, u32[]{:S(2)}) %collective-permute-start.3) | collective-permute-done | bytes 131104 | tf_op jit(solution)/shard_map/ppermute | solution.py:426
  27.6 0.0 collective-permute-done.4.refs_3_
  27.6 0.5 shard_map.55
  28.1 0.1 collective-permute-start.7
  28.2 0.1 collective-permute-start.6
  28.3 1.5 %collective-permute-start.5 = (f32[128,256]{1,0:T(8,128)S(1)}, f32[128,256]{1,0:T(8,128)S(1)}, u32[]{:S(2)}, u32[]{:S(2)}) collective-permute-start(f32[128,256]{1,0:T(8,128)S(1)} %get-tuple-element.62.refs_0_), channel_id=1, source_target_pairs={{0,8},{8,16},{16,24},{24,0},{1,9},{9,17},{17,25},{25,1},{2,10},{10... | collective-permute-start | bytes 393224 | tf_op jit(solution)/shard_map/ppermute | solution.py:426
  29.7 1.2 %shard_map.56 = (f32[4,256,128]{2,1,0:T(8,128)S(1)}, f32[4,256,128]{2,1,0:T(8,128)S(1)}, f32[8,128]{1,0:T(8,128)S(1)}) custom-call(bf16[256,3072]{1,0:T(8,128)(2,1)S(1)} %copy-done, bf16[3,3072]{1,0:T(4,128)(2,1)S(1)} %collective-permute-done.refs_4_.refs_1_, f32[4,3072]{1,0:T(4,128)S(1)} %copy-done.1, f32[2,128,256]{2,1,0:T(8,128)S(1)} %get-tuple-element.63.refs_3_, ...), custom_call_target="tpu_custom_call" | custom-call | flops 1000000 | bytes 1024 | tf_op jit(solution)/shard_map/pallas_call | solution.py:361
  31.0 3.1 %collective-permute-done.7.refs_3_ = f32[128,256]{1,0:T(8,128)S(1)} collective-permute-done((f32[128,256]{1,0:T(8,128)S(1)}, f32[128,256]{1,0:T(8,128)S(1)}, u32[]{:S(2)}, u32[]{:S(2)}) %collective-permute-start.7) | collective-permute-done | bytes 131104 | tf_op jit(solution)/shard_map/ppermute | solution.py:426
  34.1 0.0 collective-permute-done.6.refs_2_
  34.1 3.8 %collective-permute-done.5.refs_1_ = f32[128,256]{1,0:T(8,128)S(1)} collective-permute-done((f32[128,256]{1,0:T(8,128)S(1)}, f32[128,256]{1,0:T(8,128)S(1)}, u32[]{:S(2)}, u32[]{:S(2)}) %collective-permute-start.5) | collective-permute-done | bytes 131104 | tf_op jit(solution)/shard_map/ppermute | solution.py:426
  37.9 0.5 shard_map.57
  38.4 0.5 collective-permute-start.10
  38.9 0.4 collective-permute-start.9
  39.4 1.0 %collective-permute-start.8 = (f32[128,256]{1,0:T(8,128)S(1)}, f32[128,256]{1,0:T(8,128)S(1)}, u32[]{:S(2)}, u32[]{:S(2)}) collective-permute-start(f32[128,256]{1,0:T(8,128)S(1)} %get-tuple-element.68), channel_id=1, source_target_pairs={{0,32},{32,64},{64,96},{96,0},{1,33},{33,65},{65,97},{97,1},{2,34}... | collective-permute-start | bytes 393224 | tf_op jit(solution)/shard_map/ppermute | solution.py:426
  40.4 0.0 copy-start.3
  40.4 0.3 shard_map.58.refs_3_
  40.7 3.9 %collective-permute-done.10.refs_2_ = f32[128,256]{1,0:T(8,128)S(1)} collective-permute-done((f32[128,256]{1,0:T(8,128)S(1)}, f32[128,256]{1,0:T(8,128)S(1)}, u32[]{:S(2)}, u32[]{:S(2)}) %collective-permute-start.10) | collective-permute-done | bytes 131104 | tf_op jit(solution)/shard_map/ppermute | solution.py:426
  44.6 0.0 collective-permute-done.9.refs_1_
  44.6 3.0 %collective-permute-done.8.refs_0_ = f32[128,256]{1,0:T(8,128)S(1)} collective-permute-done((f32[128,256]{1,0:T(8,128)S(1)}, f32[128,256]{1,0:T(8,128)S(1)}, u32[]{:S(2)}, u32[]{:S(2)}) %collective-permute-start.8) | collective-permute-done | bytes 131104 | tf_op jit(solution)/shard_map/ppermute | solution.py:426
  47.6 0.6 %shard_map.59 = (f32[128,128]{1,0:T(8,128)S(1)}, f32[128,128]{1,0:T(8,128)S(1)}, f32[128,128]{1,0:T(8,128)S(1)}, f32[128,128]{1,0:T(8,128)S(1)}) custom-call(f32[128,256]{1,0:T(8,128)S(1)} %collective-permute-done.8.refs_0_, f32[128,256]{1,0:T(8,128)S(1)} %collective-permute-done.9.refs_1_, f32[128,256]{1,0:T(8,128)S(1)} %collective-permute-done.10.refs_2_, ...), custom_call_target="tpu_custom_call" | custom-call | flops 1000000 | bytes 1024 | tf_op jit(solution)/shard_map/pallas_call | solution.py:361
  48.3 0.3 collective-permute-start.11
  48.5 0.8 %collective-permute-start.12 = (f32[128,128]{1,0:T(8,128)S(1)}, f32[128,128]{1,0:T(8,128)S(1)}, u32[]{:S(2)}, u32[]{:S(2)}) collective-permute-start(f32[128,128]{1,0:T(8,128)S(1)} %get-tuple-element.73), channel_id=1, source_target_pairs={{0,2},{2,4},{4,6},{6,0},{1,3},{3,5},{5,7},{7,1},{8,10},{10,12},{12... | collective-permute-start | bytes 196616 | tf_op jit(solution)/shard_map/ppermute | solution.py:426
  49.3 1.9 %collective-permute-start.13 = (f32[128,128]{1,0:T(8,128)S(1)}, f32[128,128]{1,0:T(8,128)S(1)}, u32[]{:S(2)}, u32[]{:S(2)}) collective-permute-start(f32[128,128]{1,0:T(8,128)S(1)} %get-tuple-element.74), channel_id=1, source_target_pairs={{0,6},{2,0},{4,2},{6,4},{1,7},{3,1},{5,3},{7,5},{8,14},{10,8},{12,... | collective-permute-start | bytes 196616 | tf_op jit(solution)/shard_map/ppermute | solution.py:426
  51.2 1.9 %collective-permute-done.11.refs_4_ = f32[128,128]{1,0:T(8,128)S(1)} collective-permute-done((f32[128,128]{1,0:T(8,128)S(1)}, f32[128,128]{1,0:T(8,128)S(1)}, u32[]{:S(2)}, u32[]{:S(2)}) %collective-permute-start.11) | collective-permute-done | bytes 65568 | tf_op jit(solution)/shard_map/ppermute | solution.py:426
  53.1 0.5 collective-permute-done.12.refs_5_
  53.5 0.0 collective-permute-done.13.refs_6_
  53.5 0.2 shard_map.60
  53.8 2.7 %collective-permute-start.14 = (f32[4,128,128]{2,1,0:T(8,128)S(1)}, f32[4,128,128]{2,1,0:T(8,128)S(1)}, u32[]{:S(2)}, u32[]{:S(2)}) collective-permute-start(f32[4,128,128]{2,1,0:T(8,128)S(1)} %get-tuple-element.75), channel_id=1, source_target_pairs={{0,1},{1,0},{2,3},{3,2},{4,5},{5,4},{6,7},{7,6},{8,9},{9,8},{10,11... | collective-permute-start | bytes 786440 | tf_op jit(solution)/shard_map/ppermute | solution.py:421
  56.5 0.0 copy-done.3
  56.5 0.4 shard_map.61.refs_4_
  56.9 0.7 %collective-permute-done.14.refs_2_ = f32[4,128,128]{2,1,0:T(8,128)S(1)} collective-permute-done((f32[4,128,128]{2,1,0:T(8,128)S(1)}, f32[4,128,128]{2,1,0:T(8,128)S(1)}, u32[]{:S(2)}, u32[]{:S(2)}) %collective-permute-start.14) | collective-permute-done | bytes 262176 | tf_op jit(solution)/shard_map/ppermute | solution.py:421
  57.7 1.1 %shard_map.62 = bf16[256,1024]{1,0:T(8,128)(2,1)} custom-call(f32[4,256,128]{2,1,0:T(8,128)S(1)} %get-tuple-element.50.refs_0_, f32[4,256,128]{2,1,0:T(8,128)S(1)} %get-tuple-element.51.refs_1_, f32[4,128,128]{2,1,0:T(8,128)S(1)} %collective-permute-done.14.refs_2_, f32[1,128]{1,0:T(1,128)S(1)} %bitcast.2, bf16[256,512]{1,0:T(8,128)(2,1)S(1)} %shard_map.61.refs_4_), custom_call_target="tpu_custom_call" | custom-call | flops 1000000 | bytes 1024 | tf_op jit(solution)/shard_map/pallas_call | solution.py:361
Async XLA Ops:
  0.8 4.0 %copy-start.1 = (f32[4,3072]{1,0:T(4,128)S(1)}, f32[4,3072]{1,0:T(4,128)}, u32[]{:S(2)}) copy-start(f32[4,3072]{1,0:T(4,128)} %refs_2_.3) | copy-start | bytes 147460
  0.8 5.5 %copy-start.2 = (f32[8,256]{1,0:T(8,128)S(1)}, f32[8,256]{1,0:T(8,128)}, u32[]{:S(2)}) copy-start(f32[8,256]{1,0:T(8,128)} %refs_5_.5) | copy-start | bytes 24580
  0.8 5.5 %collective-permute-start = (bf16[3,3072]{1,0:T(4,128)(2,1)S(1)}, bf16[3,3072]{1,0:T(4,128)(2,1)S(1)}, u32[]{:S(2)}, u32[]{:S(2)}) collective-permute-start(bf16[3,3072]{1,0:T(4,128)(2,1)S(1)} %slice.3), channel_id=1, source_target_pairs={{0,1},{1,2},{2,3},{3,4},{4,5},{5,6},{6,7},{7,8},{8,9},{9,10},{10,1... | collective-permute-start | bytes 55304 | tf_op jit(solution)/shard_map/ppermute | solution.py:440
  9.4 8.3 %collective-permute-start.1 = (f32[4,128,256]{2,1,0:T(8,128)S(1)}, f32[4,128,256]{2,1,0:T(8,128)S(1)}, u32[]{:S(2)}, u32[]{:S(2)}) collective-permute-start(f32[4,128,256]{2,1,0:T(8,128)S(1)} %get-tuple-element.55), channel_id=1, source_target_pairs={{0,1},{1,0},{2,3},{3,2},{4,5},{5,4},{6,7},{7,6},{8,9},{9,8},{10,11... | collective-permute-start | bytes 1572872 | tf_op jit(solution)/shard_map/ppermute | solution.py:421
  17.7 5.9 %copy-start = (bf16[256,3072]{1,0:T(8,128)(2,1)S(1)}, bf16[256,3072]{1,0:T(8,128)(2,1)}, u32[]{:S(2)}) copy-start(bf16[256,3072]{1,0:T(8,128)(2,1)} %refs_0_.5) | copy-start | bytes 4718596
  18.0 6.9 %collective-permute-start.2 = (f32[128,256]{1,0:T(8,128)S(1)}, f32[128,256]{1,0:T(8,128)S(1)}, u32[]{:S(2)}, u32[]{:S(2)}) collective-permute-start(f32[128,256]{1,0:T(8,128)S(1)} %get-tuple-element.56.refs_6_), channel_id=1, source_target_pairs={{0,4},{2,6},{4,0},{6,2},{1,5},{3,7},{5,1},{7,3},{8,12},{10,14},{12... | collective-permute-start | bytes 393224 | tf_op jit(solution)/shard_map/ppermute | solution.py:426
  20.8 6.8 %collective-permute-start.3 = (f32[128,256]{1,0:T(8,128)S(1)}, f32[128,256]{1,0:T(8,128)S(1)}, u32[]{:S(2)}, u32[]{:S(2)}) collective-permute-start(f32[128,256]{1,0:T(8,128)S(1)} %get-tuple-element.59), channel_id=1, source_target_pairs={{0,2},{2,4},{4,6},{6,0},{1,3},{3,5},{5,7},{7,1},{8,10},{10,12},{12... | collective-permute-start | bytes 393224 | tf_op jit(solution)/shard_map/ppermute | solution.py:426
  20.9 6.7 %collective-permute-start.4 = (f32[128,256]{1,0:T(8,128)S(1)}, f32[128,256]{1,0:T(8,128)S(1)}, u32[]{:S(2)}, u32[]{:S(2)}) collective-permute-start(f32[128,256]{1,0:T(8,128)S(1)} %get-tuple-element.60), channel_id=1, source_target_pairs={{0,6},{2,0},{4,2},{6,4},{1,7},{3,1},{5,3},{7,5},{8,14},{10,8},{12,... | collective-permute-start | bytes 393224 | tf_op jit(solution)/shard_map/ppermute | solution.py:426
  28.1 6.0 %collective-permute-start.7 = (f32[128,256]{1,0:T(8,128)S(1)}, f32[128,256]{1,0:T(8,128)S(1)}, u32[]{:S(2)}, u32[]{:S(2)}) collective-permute-start(f32[128,256]{1,0:T(8,128)S(1)} %get-tuple-element.62.refs_0_), channel_id=1, source_target_pairs={{0,16},{8,24},{16,0},{24,8},{1,17},{9,25},{17,1},{25,9},{2,18},{10... | collective-permute-start | bytes 393224 | tf_op jit(solution)/shard_map/ppermute | solution.py:426
  28.2 5.9 %collective-permute-start.6 = (f32[128,256]{1,0:T(8,128)S(1)}, f32[128,256]{1,0:T(8,128)S(1)}, u32[]{:S(2)}, u32[]{:S(2)}) collective-permute-start(f32[128,256]{1,0:T(8,128)S(1)} %get-tuple-element.62.refs_0_), channel_id=1, source_target_pairs={{0,24},{8,0},{16,8},{24,16},{1,25},{9,1},{17,9},{25,17},{2,26},{10... | collective-permute-start | bytes 393224 | tf_op jit(solution)/shard_map/ppermute | solution.py:426
  28.3 9.6 %collective-permute-start.5 = (f32[128,256]{1,0:T(8,128)S(1)}, f32[128,256]{1,0:T(8,128)S(1)}, u32[]{:S(2)}, u32[]{:S(2)}) collective-permute-start(f32[128,256]{1,0:T(8,128)S(1)} %get-tuple-element.62.refs_0_), channel_id=1, source_target_pairs={{0,8},{8,16},{16,24},{24,0},{1,9},{9,17},{17,25},{25,1},{2,10},{10... | collective-permute-start | bytes 393224 | tf_op jit(solution)/shard_map/ppermute | solution.py:426
  38.4 6.2 %collective-permute-start.10 = (f32[128,256]{1,0:T(8,128)S(1)}, f32[128,256]{1,0:T(8,128)S(1)}, u32[]{:S(2)}, u32[]{:S(2)}) collective-permute-start(f32[128,256]{1,0:T(8,128)S(1)} %get-tuple-element.68), channel_id=1, source_target_pairs={{0,64},{32,96},{64,0},{96,32},{1,65},{33,97},{65,1},{97,33},{2,66}... | collective-permute-start | bytes 393224 | tf_op jit(solution)/shard_map/ppermute | solution.py:426
  38.9 5.7 %collective-permute-start.9 = (f32[128,256]{1,0:T(8,128)S(1)}, f32[128,256]{1,0:T(8,128)S(1)}, u32[]{:S(2)}, u32[]{:S(2)}) collective-permute-start(f32[128,256]{1,0:T(8,128)S(1)} %get-tuple-element.68), channel_id=1, source_target_pairs={{0,96},{32,0},{64,32},{96,64},{1,97},{33,1},{65,33},{97,65},{2,98}... | collective-permute-start | bytes 393224 | tf_op jit(solution)/shard_map/ppermute | solution.py:426
  39.4 8.3 %collective-permute-start.8 = (f32[128,256]{1,0:T(8,128)S(1)}, f32[128,256]{1,0:T(8,128)S(1)}, u32[]{:S(2)}, u32[]{:S(2)}) collective-permute-start(f32[128,256]{1,0:T(8,128)S(1)} %get-tuple-element.68), channel_id=1, source_target_pairs={{0,32},{32,64},{64,96},{96,0},{1,33},{33,65},{65,97},{97,1},{2,34}... | collective-permute-start | bytes 393224 | tf_op jit(solution)/shard_map/ppermute | solution.py:426
  40.4 16.1 %copy-start.3 = (f32[128]{0:T(128)S(1)}, f32[128]{0:T(128)}, u32[]{:S(2)}) copy-start(f32[128]{0:T(128)} %param.7) | copy-start | bytes 1540
  48.3 4.8 %collective-permute-start.11 = (f32[128,128]{1,0:T(8,128)S(1)}, f32[128,128]{1,0:T(8,128)S(1)}, u32[]{:S(2)}, u32[]{:S(2)}) collective-permute-start(f32[128,128]{1,0:T(8,128)S(1)} %get-tuple-element.72), channel_id=1, source_target_pairs={{0,4},{2,6},{4,0},{6,2},{1,5},{3,7},{5,1},{7,3},{8,12},{10,14},{12... | collective-permute-start | bytes 196616 | tf_op jit(solution)/shard_map/ppermute | solution.py:426
  48.5 5.0 %collective-permute-start.12 = (f32[128,128]{1,0:T(8,128)S(1)}, f32[128,128]{1,0:T(8,128)S(1)}, u32[]{:S(2)}, u32[]{:S(2)}) collective-permute-start(f32[128,128]{1,0:T(8,128)S(1)} %get-tuple-element.73), channel_id=1, source_target_pairs={{0,2},{2,4},{4,6},{6,0},{1,3},{3,5},{5,7},{7,1},{8,10},{10,12},{12... | collective-permute-start | bytes 196616 | tf_op jit(solution)/shard_map/ppermute | solution.py:426
  49.3 4.2 %collective-permute-start.13 = (f32[128,128]{1,0:T(8,128)S(1)}, f32[128,128]{1,0:T(8,128)S(1)}, u32[]{:S(2)}, u32[]{:S(2)}) collective-permute-start(f32[128,128]{1,0:T(8,128)S(1)} %get-tuple-element.74), channel_id=1, source_target_pairs={{0,6},{2,0},{4,2},{6,4},{1,7},{3,1},{5,3},{7,5},{8,14},{10,8},{12,... | collective-permute-start | bytes 196616 | tf_op jit(solution)/shard_map/ppermute | solution.py:426
  53.8 3.9 %collective-permute-start.14 = (f32[4,128,128]{2,1,0:T(8,128)S(1)}, f32[4,128,128]{2,1,0:T(8,128)S(1)}, u32[]{:S(2)}, u32[]{:S(2)}) collective-permute-start(f32[4,128,128]{2,1,0:T(8,128)S(1)} %get-tuple-element.75), channel_id=1, source_target_pairs={{0,1},{1,0},{2,3},{3,2},{4,5},{5,4},{6,7},{7,6},{8,9},{9,8},{10,11... | collective-permute-start | bytes 786440 | tf_op jit(solution)/shard_map/ppermute | solution.py:421

commit v7 on v5

--- a/solution.py
+++ b/solution.py
@@ -78,11 +78,7 @@
     for j in range(15):
         spread = (lane // 16) * 16 + j
         inv = [
-            x
-            - jnp.where(
-                row > j, jnp.take_along_axis(f, spread, axis=1, mode="promise_in_bounds"), 0.0
-            )
-            * x[j : j + 1]
+            x - jnp.take_along_axis(f, spread, axis=1, mode="promise_in_bounds") * x[j : j + 1]
             for f, x in zip(folded, inv)
         ]
     inv = [jnp.where(r // 16 == c // 16, jnp.concatenate([x] * 8, 0), 0.0) for x in inv]

time: 59 us -> 59.4 us (level)
  no operation moved by 1% of the time
where the time goes in v7:
time: 59.4 us; the launch traced here: 59.2 us
  starting transfers between devices  20.9 us (35%)
  waiting for transfers between devices  19.6 us (33%)
  Pallas kernels  17.7 us (30%)
  local copies, waits for them, and re-layouts  0.84 us (1%)
    ppermute x12, waiting for transfers between devices, shift(): lax.ppermute(block, axis, [(i, (i + distance) % n) for i in range(n)])  18.8 us
    pallas_call x17, Pallas kernels, step(): pl.pallas_call(body, in_specs=[pl.BlockSpec()] * len(args) + [anywhere] *...  17.7 us
    ppermute x12, starting transfers between devices, shift(): lax.ppermute(block, axis, [(i, (i + distance) % n) for i in range(n)])  9.57 us
    ppermute x2, starting transfers between devices, swap(): return lax.ppermute(block, 'core', [(0, 1), (1, 0)])  8.53 us
    ppermute x1, starting transfers between devices, shards(): rim = lax.ppermute(last, ALL, [(i, (i + 1) % count) for i in range(count)])  2.76 us
  transfers between devices with their start and end apart: 15, of which 8 were waited for; matrix products, arithmetic and copies ran while one was open for 0% of the time, Pallas kernels for 19%

profile of v7, /device:TPU:1, one launch (start us, length us, event | category | flops | bytes accessed | tf_op | source)
XLA Modules:
  0.0 59.2 jit_solution(13397484273530544363)
XLA Ops:
  0.0 0.8 %slice.3 = bf16[3,3072]{1,0:T(4,128)(2,1)S(1)} slice(bf16[256,3072]{1,0:T(8,128)(2,1)} %refs_0_.5), slice={[253:256], [0:3072]} | slice | bytes 36864 | tf_op jit(solution)/shard_map/slice | solution.py:423
  0.8 0.0 copy-start.1
  0.8 0.0 copy-start.2
  0.8 2.8 %collective-permute-start = (bf16[3,3072]{1,0:T(4,128)(2,1)S(1)}, bf16[3,3072]{1,0:T(4,128)(2,1)S(1)}, u32[]{:S(2)}, u32[]{:S(2)}) collective-permute-start(bf16[3,3072]{1,0:T(4,128)(2,1)S(1)} %slice.3), channel_id=1, source_target_pairs={{0,1},{1,2},{2,3},{3,4},{4,5},{5,6},{6,7},{7,8},{8,9},{9,10},{10,1... | collective-permute-start | bytes 55304 | tf_op jit(solution)/shard_map/ppermute | solution.py:425
  3.6 1.2 %shard_map.46 = (bf16[2,256,512]{2,1,0:T(8,128)(2,1)S(1)}, bf16[2,256,512]{2,1,0:T(8,128)(2,1)S(1)}) custom-call(bf16[256,3072]{1,0:T(8,128)(2,1)} %refs_0_.5), custom_call_target="tpu_custom_call" | custom-call | flops 1000000000 | bytes 1024 | tf_op jit(solution)/shard_map/pallas_call | solution.py:347
  4.8 0.0 copy-done.1
  4.8 0.7 %shard_map.47 = (f32[4,256,128]{2,1,0:T(8,128)S(1)}, f32[4,256,128]{2,1,0:T(8,128)S(1)}, f32[2,8,512]{2,1,0:T(8,128)S(1)}) custom-call(bf16[2,256,512]{2,1,0:T(8,128)(2,1)S(1)} %get-tuple-element.42.refs_0_, f32[4,3072]{1,0:T(4,128)S(1)} %copy-done.1), custom_call_target="tpu_custom_call" | custom-call | flops 1000000 | bytes 1024 | tf_op jit(solution)/shard_map/pallas_call | solution.py:347
  5.6 0.7 %shard_map.48 = (f32[4,256,128]{2,1,0:T(8,128)S(1)}, f32[4,256,128]{2,1,0:T(8,128)S(1)}, f32[2,8,512]{2,1,0:T(8,128)S(1)}) custom-call(bf16[2,256,512]{2,1,0:T(8,128)(2,1)S(1)} %get-tuple-element.46.refs_0_, f32[4,3072]{1,0:T(4,128)S(1)} %copy-done.1), custom_call_target="tpu_custom_call" | custom-call | flops 1000000 | bytes 1024 | tf_op jit(solution)/shard_map/pallas_call | solution.py:347
  6.3 0.0 collective-permute-done.refs_4_.refs_1_
  6.3 0.0 copy-done.2
  6.3 3.2 %shard_map.49 = (f32[4,128,256]{2,1,0:T(8,128)S(1)}, f32[4,128,256]{2,1,0:T(8,128)S(1)}, f32[4,256,256]{2,1,0:T(8,128)S(1)}) custom-call(f32[4,256,128]{2,1,0:T(8,128)S(1)} %get-tuple-element.43.refs_0_, f32[4,256,128]{2,1,0:T(8,128)S(1)} %get-tuple-element.44.refs_1_, f32[2,8,512]{2,1,0:T(8,128)S(1)} %get-tuple-element.45.refs_2_, f32[4,3072]{1,0:T(4,128)S(1)} %copy-done.1, ...), custom_call_target="tpu_custom_call" | custom-call | flops 1000000 | bytes 1024 | tf_op jit(solution)/shard_map/pallas_call | solution.py:347
  9.5 5.8 %collective-permute-start.1 = (f32[4,128,256]{2,1,0:T(8,128)S(1)}, f32[4,128,256]{2,1,0:T(8,128)S(1)}, u32[]{:S(2)}, u32[]{:S(2)}) collective-permute-start(f32[4,128,256]{2,1,0:T(8,128)S(1)} %get-tuple-element.55), channel_id=1, source_target_pairs={{0,1},{1,0},{2,3},{3,2},{4,5},{5,4},{6,7},{7,6},{8,9},{9,8},{10,11... | collective-permute-start | bytes 1572872 | tf_op jit(solution)/shard_map/ppermute | solution.py:406
  15.3 2.6 %shard_map.51 = (f32[2,128,256]{2,1,0:T(8,128)S(1)}, f32[2,128,256]{2,1,0:T(8,128)S(1)}, f32[2,256,256]{2,1,0:T(8,128)S(1)}) custom-call(f32[4,256,128]{2,1,0:T(8,128)S(1)} %get-tuple-element.52.refs_0_, f32[4,256,128]{2,1,0:T(8,128)S(1)} %get-tuple-element.53.refs_1_, f32[2,8,512]{2,1,0:T(8,128)S(1)} %get-tuple-element.47.refs_6_.refs_2_, ...), custom_call_target="tpu_custom_call" | custom-call | flops 1000000 | bytes 1024 | tf_op jit(solution)/shard_map/pallas_call | solution.py:347
  17.9 0.0 copy-start
  17.9 0.0 collective-permute-done.1.refs_1_.refs_2_
  18.0 0.3 shard_map.52
  18.2 0.1 collective-permute-start.2
  18.3 2.6 %shard_map.53 = (f32[2,128,256]{2,1,0:T(8,128)S(1)}, f32[2,128,256]{2,1,0:T(8,128)S(1)}, f32[2,256,256]{2,1,0:T(8,128)S(1)}) custom-call(f32[4,256,128]{2,1,0:T(8,128)S(1)} %get-tuple-element.52.refs_0_, f32[4,256,128]{2,1,0:T(8,128)S(1)} %get-tuple-element.53.refs_1_, f32[2,8,512]{2,1,0:T(8,128)S(1)} %get-tuple-element.47.refs_6_.refs_2_, ...), custom_call_target="tpu_custom_call" | custom-call | flops 1000000 | bytes 1024 | tf_op jit(solution)/shard_map/pallas_call | solution.py:347
  20.9 0.3 shard_map.54
  21.2 0.1 collective-permute-start.3
  21.2 2.7 %collective-permute-start.4 = (f32[128,256]{1,0:T(8,128)S(1)}, f32[128,256]{1,0:T(8,128)S(1)}, u32[]{:S(2)}, u32[]{:S(2)}) collective-permute-start(f32[128,256]{1,0:T(8,128)S(1)} %get-tuple-element.60), channel_id=1, source_target_pairs={{0,6},{2,0},{4,2},{6,4},{1,7},{3,1},{5,3},{7,5},{8,14},{10,8},{12,... | collective-permute-start | bytes 393224 | tf_op jit(solution)/shard_map/ppermute | solution.py:411
  23.9 0.0 copy-done
  23.9 1.2 %shard_map.50 = (f32[4,256,128]{2,1,0:T(8,128)S(1)}, f32[4,256,128]{2,1,0:T(8,128)S(1)}, f32[8,128]{1,0:T(8,128)S(1)}) custom-call(bf16[256,3072]{1,0:T(8,128)(2,1)S(1)} %copy-done, bf16[3,3072]{1,0:T(4,128)(2,1)S(1)} %collective-permute-done.refs_4_.refs_1_, f32[4,3072]{1,0:T(4,128)S(1)} %copy-done.1, f32[4,128,256]{2,1,0:T(8,128)S(1)} %get-tuple-element.48.refs_3_, ...), custom_call_target="tpu_custom_call" | custom-call | flops 1000000 | bytes 1024 | tf_op jit(solution)/shard_map/pallas_call | solution.py:347
  25.1 1.2 %shard_map.55 = (f32[4,256,128]{2,1,0:T(8,128)S(1)}, f32[4,256,128]{2,1,0:T(8,128)S(1)}, f32[8,128]{1,0:T(8,128)S(1)}) custom-call(bf16[256,3072]{1,0:T(8,128)(2,1)S(1)} %copy-done, bf16[3,3072]{1,0:T(4,128)(2,1)S(1)} %collective-permute-done.refs_4_.refs_1_, f32[4,3072]{1,0:T(4,128)S(1)} %copy-done.1, f32[2,128,256]{2,1,0:T(8,128)S(1)} %get-tuple-element.62.refs_3_, ...), custom_call_target="tpu_custom_call" | custom-call | flops 1000000 | bytes 1024 | tf_op jit(solution)/shard_map/pallas_call | solution.py:347
  26.4 0.0 collective-permute-done.2.refs_1_
  26.4 1.4 %collective-permute-done.3.refs_2_ = f32[128,256]{1,0:T(8,128)S(1)} collective-permute-done((f32[128,256]{1,0:T(8,128)S(1)}, f32[128,256]{1,0:T(8,128)S(1)}, u32[]{:S(2)}, u32[]{:S(2)}) %collective-permute-start.3) | collective-permute-done | bytes 131104 | tf_op jit(solution)/shard_map/ppermute | solution.py:411
  27.8 0.0 collective-permute-done.4.refs_3_
  27.8 0.5 shard_map.56
  28.3 0.1 collective-permute-start.7
  28.4 0.3 collective-permute-start.6
  28.7 1.5 %collective-permute-start.5 = (f32[128,256]{1,0:T(8,128)S(1)}, f32[128,256]{1,0:T(8,128)S(1)}, u32[]{:S(2)}, u32[]{:S(2)}) collective-permute-start(f32[128,256]{1,0:T(8,128)S(1)} %get-tuple-element.67.refs_0_), channel_id=1, source_target_pairs={{0,8},{8,16},{16,24},{24,0},{1,9},{9,17},{17,25},{25,1},{2,10},{10... | collective-permute-start | bytes 393224 | tf_op jit(solution)/shard_map/ppermute | solution.py:411
  30.1 4.1 %collective-permute-done.7.refs_3_ = f32[128,256]{1,0:T(8,128)S(1)} collective-permute-done((f32[128,256]{1,0:T(8,128)S(1)}, f32[128,256]{1,0:T(8,128)S(1)}, u32[]{:S(2)}, u32[]{:S(2)}) %collective-permute-start.7) | collective-permute-done | bytes 131104 | tf_op jit(solution)/shard_map/ppermute | solution.py:411
  34.2 0.0 collective-permute-done.6.refs_2_
  34.2 3.9 %collective-permute-done.5.refs_1_ = f32[128,256]{1,0:T(8,128)S(1)} collective-permute-done((f32[128,256]{1,0:T(8,128)S(1)}, f32[128,256]{1,0:T(8,128)S(1)}, u32[]{:S(2)}, u32[]{:S(2)}) %collective-permute-start.5) | collective-permute-done | bytes 131104 | tf_op jit(solution)/shard_map/ppermute | solution.py:411
  38.1 0.5 shard_map.57
  38.6 0.4 collective-permute-start.10
  39.0 0.5 collective-permute-start.9
  39.5 1.0 %collective-permute-start.8 = (f32[128,256]{1,0:T(8,128)S(1)}, f32[128,256]{1,0:T(8,128)S(1)}, u32[]{:S(2)}, u32[]{:S(2)}) collective-permute-start(f32[128,256]{1,0:T(8,128)S(1)} %get-tuple-element.68), channel_id=1, source_target_pairs={{0,32},{32,64},{64,96},{96,0},{1,33},{33,65},{65,97},{97,1},{2,34}... | collective-permute-start | bytes 393224 | tf_op jit(solution)/shard_map/ppermute | solution.py:411
  40.5 0.0 copy-start.3
  40.5 0.3 shard_map.58.refs_3_
  40.7 4.0 %collective-permute-done.10.refs_2_ = f32[128,256]{1,0:T(8,128)S(1)} collective-permute-done((f32[128,256]{1,0:T(8,128)S(1)}, f32[128,256]{1,0:T(8,128)S(1)}, u32[]{:S(2)}, u32[]{:S(2)}) %collective-permute-start.10) | collective-permute-done | bytes 131104 | tf_op jit(solution)/shard_map/ppermute | solution.py:411
  44.8 0.0 collective-permute-done.9.refs_1_
  44.8 3.1 %collective-permute-done.8.refs_0_ = f32[128,256]{1,0:T(8,128)S(1)} collective-permute-done((f32[128,256]{1,0:T(8,128)S(1)}, f32[128,256]{1,0:T(8,128)S(1)}, u32[]{:S(2)}, u32[]{:S(2)}) %collective-permute-start.8) | collective-permute-done | bytes 131104 | tf_op jit(solution)/shard_map/ppermute | solution.py:411
  47.8 0.6 %shard_map.59 = (f32[128,128]{1,0:T(8,128)S(1)}, f32[128,128]{1,0:T(8,128)S(1)}, f32[128,128]{1,0:T(8,128)S(1)}, f32[128,128]{1,0:T(8,128)S(1)}) custom-call(f32[128,256]{1,0:T(8,128)S(1)} %collective-permute-done.8.refs_0_, f32[128,256]{1,0:T(8,128)S(1)} %collective-permute-done.9.refs_1_, f32[128,256]{1,0:T(8,128)S(1)} %collective-permute-done.10.refs_2_, ...), custom_call_target="tpu_custom_call" | custom-call | flops 1000000 | bytes 1024 | tf_op jit(solution)/shard_map/pallas_call | solution.py:347
  48.4 0.4 collective-permute-start.11
  48.9 0.9 %collective-permute-start.12 = (f32[128,128]{1,0:T(8,128)S(1)}, f32[128,128]{1,0:T(8,128)S(1)}, u32[]{:S(2)}, u32[]{:S(2)}) collective-permute-start(f32[128,128]{1,0:T(8,128)S(1)} %get-tuple-element.73), channel_id=1, source_target_pairs={{0,2},{2,4},{4,6},{6,0},{1,3},{3,5},{5,7},{7,1},{8,10},{10,12},{12... | collective-permute-start | bytes 196616 | tf_op jit(solution)/shard_map/ppermute | solution.py:411
  49.7 1.8 %collective-permute-start.13 = (f32[128,128]{1,0:T(8,128)S(1)}, f32[128,128]{1,0:T(8,128)S(1)}, u32[]{:S(2)}, u32[]{:S(2)}) collective-permute-start(f32[128,128]{1,0:T(8,128)S(1)} %get-tuple-element.74), channel_id=1, source_target_pairs={{0,6},{2,0},{4,2},{6,4},{1,7},{3,1},{5,3},{7,5},{8,14},{10,8},{12,... | collective-permute-start | bytes 196616 | tf_op jit(solution)/shard_map/ppermute | solution.py:411
  51.5 1.7 %collective-permute-done.11.refs_4_ = f32[128,128]{1,0:T(8,128)S(1)} collective-permute-done((f32[128,128]{1,0:T(8,128)S(1)}, f32[128,128]{1,0:T(8,128)S(1)}, u32[]{:S(2)}, u32[]{:S(2)}) %collective-permute-start.11) | collective-permute-done | bytes 65568 | tf_op jit(solution)/shard_map/ppermute | solution.py:411
  53.2 0.6 %collective-permute-done.12.refs_5_ = f32[128,128]{1,0:T(8,128)S(1)} collective-permute-done((f32[128,128]{1,0:T(8,128)S(1)}, f32[128,128]{1,0:T(8,128)S(1)}, u32[]{:S(2)}, u32[]{:S(2)}) %collective-permute-start.12) | collective-permute-done | bytes 65568 | tf_op jit(solution)/shard_map/ppermute | solution.py:411
  53.8 0.0 collective-permute-done.13.refs_6_
  53.9 0.2 shard_map.60
  54.1 2.7 %collective-permute-start.14 = (f32[4,128,128]{2,1,0:T(8,128)S(1)}, f32[4,128,128]{2,1,0:T(8,128)S(1)}, u32[]{:S(2)}, u32[]{:S(2)}) collective-permute-start(f32[4,128,128]{2,1,0:T(8,128)S(1)} %get-tuple-element.75), channel_id=1, source_target_pairs={{0,1},{1,0},{2,3},{3,2},{4,5},{5,4},{6,7},{7,6},{8,9},{9,8},{10,11... | collective-permute-start | bytes 786440 | tf_op jit(solution)/shard_map/ppermute | solution.py:406
  56.8 0.0 copy-done.3
  56.8 0.4 shard_map.61.refs_4_
  57.3 0.7 %collective-permute-done.14.refs_2_ = f32[4,128,128]{2,1,0:T(8,128)S(1)} collective-permute-done((f32[4,128,128]{2,1,0:T(8,128)S(1)}, f32[4,128,128]{2,1,0:T(8,128)S(1)}, u32[]{:S(2)}, u32[]{:S(2)}) %collective-permute-start.14) | collective-permute-done | bytes 262176 | tf_op jit(solution)/shard_map/ppermute | solution.py:406
  58.0 1.2 %shard_map.62 = bf16[256,1024]{1,0:T(8,128)(2,1)} custom-call(f32[4,256,128]{2,1,0:T(8,128)S(1)} %get-tuple-element.50.refs_0_, f32[4,256,128]{2,1,0:T(8,128)S(1)} %get-tuple-element.51.refs_1_, f32[4,128,128]{2,1,0:T(8,128)S(1)} %collective-permute-done.14.refs_2_, f32[1,128]{1,0:T(1,128)S(1)} %bitcast.2, bf16[256,512]{1,0:T(8,128)(2,1)S(1)} %shard_map.61.refs_4_), custom_call_target="tpu_custom_call" | custom-call | flops 1000000 | bytes 1024 | tf_op jit(solution)/shard_map/pallas_call | solution.py:347
Async XLA Ops:
  0.8 4.0 %copy-start.1 = (f32[4,3072]{1,0:T(4,128)S(1)}, f32[4,3072]{1,0:T(4,128)}, u32[]{:S(2)}) copy-start(f32[4,3072]{1,0:T(4,128)} %refs_2_.3) | copy-start | bytes 147460
  0.8 5.5 %copy-start.2 = (f32[8,256]{1,0:T(8,128)S(1)}, f32[8,256]{1,0:T(8,128)}, u32[]{:S(2)}) copy-start(f32[8,256]{1,0:T(8,128)} %refs_5_.5) | copy-start | bytes 24580
  0.8 5.5 %collective-permute-start = (bf16[3,3072]{1,0:T(4,128)(2,1)S(1)}, bf16[3,3072]{1,0:T(4,128)(2,1)S(1)}, u32[]{:S(2)}, u32[]{:S(2)}) collective-permute-start(bf16[3,3072]{1,0:T(4,128)(2,1)S(1)} %slice.3), channel_id=1, source_target_pairs={{0,1},{1,2},{2,3},{3,4},{4,5},{5,6},{6,7},{7,8},{8,9},{9,10},{10,1... | collective-permute-start | bytes 55304 | tf_op jit(solution)/shard_map/ppermute | solution.py:425
  9.5 8.4 %collective-permute-start.1 = (f32[4,128,256]{2,1,0:T(8,128)S(1)}, f32[4,128,256]{2,1,0:T(8,128)S(1)}, u32[]{:S(2)}, u32[]{:S(2)}) collective-permute-start(f32[4,128,256]{2,1,0:T(8,128)S(1)} %get-tuple-element.55), channel_id=1, source_target_pairs={{0,1},{1,0},{2,3},{3,2},{4,5},{5,4},{6,7},{7,6},{8,9},{9,8},{10,11... | collective-permute-start | bytes 1572872 | tf_op jit(solution)/shard_map/ppermute | solution.py:406
  17.9 6.0 %copy-start = (bf16[256,3072]{1,0:T(8,128)(2,1)S(1)}, bf16[256,3072]{1,0:T(8,128)(2,1)}, u32[]{:S(2)}) copy-start(bf16[256,3072]{1,0:T(8,128)(2,1)} %refs_0_.5) | copy-start | bytes 4718596
  18.2 8.2 %collective-permute-start.2 = (f32[128,256]{1,0:T(8,128)S(1)}, f32[128,256]{1,0:T(8,128)S(1)}, u32[]{:S(2)}, u32[]{:S(2)}) collective-permute-start(f32[128,256]{1,0:T(8,128)S(1)} %get-tuple-element.56.refs_6_), channel_id=1, source_target_pairs={{0,4},{2,6},{4,0},{6,2},{1,5},{3,7},{5,1},{7,3},{8,12},{10,14},{12... | collective-permute-start | bytes 393224 | tf_op jit(solution)/shard_map/ppermute | solution.py:411
  21.2 6.7 %collective-permute-start.3 = (f32[128,256]{1,0:T(8,128)S(1)}, f32[128,256]{1,0:T(8,128)S(1)}, u32[]{:S(2)}, u32[]{:S(2)}) collective-permute-start(f32[128,256]{1,0:T(8,128)S(1)} %get-tuple-element.59), channel_id=1, source_target_pairs={{0,2},{2,4},{4,6},{6,0},{1,3},{3,5},{5,7},{7,1},{8,10},{10,12},{12... | collective-permute-start | bytes 393224 | tf_op jit(solution)/shard_map/ppermute | solution.py:411
  21.2 6.6 %collective-permute-start.4 = (f32[128,256]{1,0:T(8,128)S(1)}, f32[128,256]{1,0:T(8,128)S(1)}, u32[]{:S(2)}, u32[]{:S(2)}) collective-permute-start(f32[128,256]{1,0:T(8,128)S(1)} %get-tuple-element.60), channel_id=1, source_target_pairs={{0,6},{2,0},{4,2},{6,4},{1,7},{3,1},{5,3},{7,5},{8,14},{10,8},{12,... | collective-permute-start | bytes 393224 | tf_op jit(solution)/shard_map/ppermute | solution.py:411
  28.3 5.9 %collective-permute-start.7 = (f32[128,256]{1,0:T(8,128)S(1)}, f32[128,256]{1,0:T(8,128)S(1)}, u32[]{:S(2)}, u32[]{:S(2)}) collective-permute-start(f32[128,256]{1,0:T(8,128)S(1)} %get-tuple-element.67.refs_0_), channel_id=1, source_target_pairs={{0,16},{8,24},{16,0},{24,8},{1,17},{9,25},{17,1},{25,9},{2,18},{10... | collective-permute-start | bytes 393224 | tf_op jit(solution)/shard_map/ppermute | solution.py:411
  28.4 5.8 %collective-permute-start.6 = (f32[128,256]{1,0:T(8,128)S(1)}, f32[128,256]{1,0:T(8,128)S(1)}, u32[]{:S(2)}, u32[]{:S(2)}) collective-permute-start(f32[128,256]{1,0:T(8,128)S(1)} %get-tuple-element.67.refs_0_), channel_id=1, source_target_pairs={{0,24},{8,0},{16,8},{24,16},{1,25},{9,1},{17,9},{25,17},{2,26},{10... | collective-permute-start | bytes 393224 | tf_op jit(solution)/shard_map/ppermute | solution.py:411
  28.7 9.5 %collective-permute-start.5 = (f32[128,256]{1,0:T(8,128)S(1)}, f32[128,256]{1,0:T(8,128)S(1)}, u32[]{:S(2)}, u32[]{:S(2)}) collective-permute-start(f32[128,256]{1,0:T(8,128)S(1)} %get-tuple-element.67.refs_0_), channel_id=1, source_target_pairs={{0,8},{8,16},{16,24},{24,0},{1,9},{9,17},{17,25},{25,1},{2,10},{10... | collective-permute-start | bytes 393224 | tf_op jit(solution)/shard_map/ppermute | solution.py:411
  38.6 6.2 %collective-permute-start.10 = (f32[128,256]{1,0:T(8,128)S(1)}, f32[128,256]{1,0:T(8,128)S(1)}, u32[]{:S(2)}, u32[]{:S(2)}) collective-permute-start(f32[128,256]{1,0:T(8,128)S(1)} %get-tuple-element.68), channel_id=1, source_target_pairs={{0,64},{32,96},{64,0},{96,32},{1,65},{33,97},{65,1},{97,33},{2,66}... | collective-permute-start | bytes 393224 | tf_op jit(solution)/shard_map/ppermute | solution.py:411
  39.0 5.8 %collective-permute-start.9 = (f32[128,256]{1,0:T(8,128)S(1)}, f32[128,256]{1,0:T(8,128)S(1)}, u32[]{:S(2)}, u32[]{:S(2)}) collective-permute-start(f32[128,256]{1,0:T(8,128)S(1)} %get-tuple-element.68), channel_id=1, source_target_pairs={{0,96},{32,0},{64,32},{96,64},{1,97},{33,1},{65,33},{97,65},{2,98}... | collective-permute-start | bytes 393224 | tf_op jit(solution)/shard_map/ppermute | solution.py:411
  39.5 8.4 %collective-permute-start.8 = (f32[128,256]{1,0:T(8,128)S(1)}, f32[128,256]{1,0:T(8,128)S(1)}, u32[]{:S(2)}, u32[]{:S(2)}) collective-permute-start(f32[128,256]{1,0:T(8,128)S(1)} %get-tuple-element.68), channel_id=1, source_target_pairs={{0,32},{32,64},{64,96},{96,0},{1,33},{33,65},{65,97},{97,1},{2,34}... | collective-permute-start | bytes 393224 | tf_op jit(solution)/shard_map/ppermute | solution.py:411
  40.5 16.4 %copy-start.3 = (f32[128]{0:T(128)S(1)}, f32[128]{0:T(128)}, u32[]{:S(2)}) copy-start(f32[128]{0:T(128)} %param.7) | copy-start | bytes 1540
  48.4 4.8 %collective-permute-start.11 = (f32[128,128]{1,0:T(8,128)S(1)}, f32[128,128]{1,0:T(8,128)S(1)}, u32[]{:S(2)}, u32[]{:S(2)}) collective-permute-start(f32[128,128]{1,0:T(8,128)S(1)} %get-tuple-element.72), channel_id=1, source_target_pairs={{0,4},{2,6},{4,0},{6,2},{1,5},{3,7},{5,1},{7,3},{8,12},{10,14},{12... | collective-permute-start | bytes 196616 | tf_op jit(solution)/shard_map/ppermute | solution.py:411
  48.9 5.0 %collective-permute-start.12 = (f32[128,128]{1,0:T(8,128)S(1)}, f32[128,128]{1,0:T(8,128)S(1)}, u32[]{:S(2)}, u32[]{:S(2)}) collective-permute-start(f32[128,128]{1,0:T(8,128)S(1)} %get-tuple-element.73), channel_id=1, source_target_pairs={{0,2},{2,4},{4,6},{6,0},{1,3},{3,5},{5,7},{7,1},{8,10},{10,12},{12... | collective-permute-start | bytes 196616 | tf_op jit(solution)/shard_map/ppermute | solution.py:411
  49.7 4.1 %collective-permute-start.13 = (f32[128,128]{1,0:T(8,128)S(1)}, f32[128,128]{1,0:T(8,128)S(1)}, u32[]{:S(2)}, u32[]{:S(2)}) collective-permute-start(f32[128,128]{1,0:T(8,128)S(1)} %get-tuple-element.74), channel_id=1, source_target_pairs={{0,6},{2,0},{4,2},{6,4},{1,7},{3,1},{5,3},{7,5},{8,14},{10,8},{12,... | collective-permute-start | bytes 196616 | tf_op jit(solution)/shard_map/ppermute | solution.py:411
  54.1 3.9 %collective-permute-start.14 = (f32[4,128,128]{2,1,0:T(8,128)S(1)}, f32[4,128,128]{2,1,0:T(8,128)S(1)}, u32[]{:S(2)}, u32[]{:S(2)}) collective-permute-start(f32[4,128,128]{2,1,0:T(8,128)S(1)} %get-tuple-element.75), channel_id=1, source_target_pairs={{0,1},{1,0},{2,3},{3,2},{4,5},{5,4},{6,7},{7,6},{8,9},{9,8},{10,11... | collective-permute-start | bytes 786440 | tf_op jit(solution)/shard_map/ppermute | solution.py:406

commit v8 on v5

--- a/solution.py
+++ b/solution.py
@@ -448,10 +448,10 @@
         (own, b2, b1, b3),
         [one, shaped(3, DK, 2 * DK)],
         [held],
-        (far_done, own_done),
+        (far_done,),
     )
     b1, b2, b3 = ring_of([trans] * 3, "x")
-    trans, x_prefix = step(x_kernel, (trans, b1, b3, b2), [one, one], [held])
+    trans, x_prefix = step(x_kernel, (trans, b1, b3, b2), [one, one], [held], (own_done,))
     b1, b2, b3 = ring_of([trans] * 3, "z")
     (prefixes,) = step(prefix_kernel, (x_prefix, y_prefixes), [shaped(4, DK, 2 * DK)])
 

time: 59 us -> 59 us (level)
  no operation moved by 1% of the time
where the time goes in v8:
time: 59 us; the launch traced here: 58.9 us
  starting transfers between devices  20.6 us (35%)
  waiting for transfers between devices  19.8 us (34%)
  Pallas kernels  17.4 us (29%)
  local copies, waits for them, and re-layouts  0.84 us (1%)
    ppermute x12, waiting for transfers between devices, shift(): lax.ppermute(block, axis, [(i, (i + distance) % n) for i in range(n)])  19 us
    pallas_call x17, Pallas kernels, step(): pl.pallas_call(body, in_specs=[pl.BlockSpec()] * len(args) + [anywhere] *...  17.4 us
    ppermute x12, starting transfers between devices, shift(): lax.ppermute(block, axis, [(i, (i + distance) % n) for i in range(n)])  9.38 us
    ppermute x2, starting transfers between devices, swap(): return lax.ppermute(block, 'core', [(0, 1), (1, 0)])  8.5 us
    ppermute x1, starting transfers between devices, shards(): rim = lax.ppermute(last, ALL, [(i, (i + 1) % count) for i in range(count)])  2.76 us
  transfers between devices with their start and end apart: 15, of which 8 were waited for; matrix products, arithmetic and copies ran while one was open for 0% of the time, Pallas kernels for 19%

profile of v8, /device:TPU:1, one launch (start us, length us, event | category | flops | bytes accessed | tf_op | source)
XLA Modules:
  0.0 58.9 jit_solution(10037912998554357962)
XLA Ops:
  0.0 0.8 %slice.3 = bf16[3,3072]{1,0:T(4,128)(2,1)S(1)} slice(bf16[256,3072]{1,0:T(8,128)(2,1)} %refs_0_.5), slice={[253:256], [0:3072]} | slice | bytes 36864 | tf_op jit(solution)/shard_map/slice | solution.py:427
  0.8 0.0 copy-start.1
  0.8 0.0 copy-start.2
  0.8 2.8 %collective-permute-start = (bf16[3,3072]{1,0:T(4,128)(2,1)S(1)}, bf16[3,3072]{1,0:T(4,128)(2,1)S(1)}, u32[]{:S(2)}, u32[]{:S(2)}) collective-permute-start(bf16[3,3072]{1,0:T(4,128)(2,1)S(1)} %slice.3), channel_id=1, source_target_pairs={{0,1},{1,2},{2,3},{3,4},{4,5},{5,6},{6,7},{7,8},{8,9},{9,10},{10,1... | collective-permute-start | bytes 55304 | tf_op jit(solution)/shard_map/ppermute | solution.py:429
  3.6 1.2 %shard_map.46 = (bf16[2,256,512]{2,1,0:T(8,128)(2,1)S(1)}, bf16[2,256,512]{2,1,0:T(8,128)(2,1)S(1)}) custom-call(bf16[256,3072]{1,0:T(8,128)(2,1)} %refs_0_.5), custom_call_target="tpu_custom_call" | custom-call | flops 1000000000 | bytes 1024 | tf_op jit(solution)/shard_map/pallas_call | solution.py:351
  4.8 0.0 copy-done.1
  4.8 0.7 %shard_map.47 = (f32[4,256,128]{2,1,0:T(8,128)S(1)}, f32[4,256,128]{2,1,0:T(8,128)S(1)}, f32[2,8,512]{2,1,0:T(8,128)S(1)}) custom-call(bf16[2,256,512]{2,1,0:T(8,128)(2,1)S(1)} %get-tuple-element.42.refs_0_, f32[4,3072]{1,0:T(4,128)S(1)} %copy-done.1), custom_call_target="tpu_custom_call" | custom-call | flops 1000000 | bytes 1024 | tf_op jit(solution)/shard_map/pallas_call | solution.py:351
  5.6 0.7 %shard_map.48 = (f32[4,256,128]{2,1,0:T(8,128)S(1)}, f32[4,256,128]{2,1,0:T(8,128)S(1)}, f32[2,8,512]{2,1,0:T(8,128)S(1)}) custom-call(bf16[2,256,512]{2,1,0:T(8,128)(2,1)S(1)} %get-tuple-element.46.refs_0_, f32[4,3072]{1,0:T(4,128)S(1)} %copy-done.1), custom_call_target="tpu_custom_call" | custom-call | flops 1000000 | bytes 1024 | tf_op jit(solution)/shard_map/pallas_call | solution.py:351
  6.3 0.0 collective-permute-done.refs_4_.refs_1_
  6.3 0.0 copy-done.2
  6.3 3.0 %shard_map.49 = (f32[4,128,256]{2,1,0:T(8,128)S(1)}, f32[4,128,256]{2,1,0:T(8,128)S(1)}, f32[4,256,256]{2,1,0:T(8,128)S(1)}) custom-call(f32[4,256,128]{2,1,0:T(8,128)S(1)} %get-tuple-element.43.refs_0_, f32[4,256,128]{2,1,0:T(8,128)S(1)} %get-tuple-element.44.refs_1_, f32[2,8,512]{2,1,0:T(8,128)S(1)} %get-tuple-element.45.refs_2_, f32[4,3072]{1,0:T(4,128)S(1)} %copy-done.1, ...), custom_call_target="tpu_custom_call" | custom-call | flops 1000000 | bytes 1024 | tf_op jit(solution)/shard_map/pallas_call | solution.py:351
  9.4 5.8 %collective-permute-start.1 = (f32[4,128,256]{2,1,0:T(8,128)S(1)}, f32[4,128,256]{2,1,0:T(8,128)S(1)}, u32[]{:S(2)}, u32[]{:S(2)}) collective-permute-start(f32[4,128,256]{2,1,0:T(8,128)S(1)} %get-tuple-element.55), channel_id=1, source_target_pairs={{0,1},{1,0},{2,3},{3,2},{4,5},{5,4},{6,7},{7,6},{8,9},{9,8},{10,11... | collective-permute-start | bytes 1572872 | tf_op jit(solution)/shard_map/ppermute | solution.py:410
  15.2 2.5 %shard_map.51 = (f32[2,128,256]{2,1,0:T(8,128)S(1)}, f32[2,128,256]{2,1,0:T(8,128)S(1)}, f32[2,256,256]{2,1,0:T(8,128)S(1)}) custom-call(f32[4,256,128]{2,1,0:T(8,128)S(1)} %get-tuple-element.52.refs_0_, f32[4,256,128]{2,1,0:T(8,128)S(1)} %get-tuple-element.53.refs_1_, f32[2,8,512]{2,1,0:T(8,128)S(1)} %get-tuple-element.47.refs_6_.refs_2_, ...), custom_call_target="tpu_custom_call" | custom-call | flops 1000000 | bytes 1024 | tf_op jit(solution)/shard_map/pallas_call | solution.py:351
  17.7 0.0 copy-start
  17.7 0.0 collective-permute-done.1.refs_1_.refs_2_
  17.7 0.3 shard_map.52
  18.0 0.1 collective-permute-start.2
  18.1 2.5 %shard_map.53 = (f32[2,128,256]{2,1,0:T(8,128)S(1)}, f32[2,128,256]{2,1,0:T(8,128)S(1)}, f32[2,256,256]{2,1,0:T(8,128)S(1)}) custom-call(f32[4,256,128]{2,1,0:T(8,128)S(1)} %get-tuple-element.52.refs_0_, f32[4,256,128]{2,1,0:T(8,128)S(1)} %get-tuple-element.53.refs_1_, f32[2,8,512]{2,1,0:T(8,128)S(1)} %get-tuple-element.47.refs_6_.refs_2_, ...), custom_call_target="tpu_custom_call" | custom-call | flops 1000000 | bytes 1024 | tf_op jit(solution)/shard_map/pallas_call | solution.py:351
  20.6 0.3 shard_map.54
  20.8 0.1 collective-permute-start.3
  20.9 2.7 %collective-permute-start.4 = (f32[128,256]{1,0:T(8,128)S(1)}, f32[128,256]{1,0:T(8,128)S(1)}, u32[]{:S(2)}, u32[]{:S(2)}) collective-permute-start(f32[128,256]{1,0:T(8,128)S(1)} %get-tuple-element.60), channel_id=1, source_target_pairs={{0,6},{2,0},{4,2},{6,4},{1,7},{3,1},{5,3},{7,5},{8,14},{10,8},{12,... | collective-permute-start | bytes 393224 | tf_op jit(solution)/shard_map/ppermute | solution.py:415
  23.6 0.0 copy-done
  23.6 1.2 %shard_map.50 = (f32[4,256,128]{2,1,0:T(8,128)S(1)}, f32[4,256,128]{2,1,0:T(8,128)S(1)}, f32[8,128]{1,0:T(8,128)S(1)}) custom-call(bf16[256,3072]{1,0:T(8,128)(2,1)S(1)} %copy-done, bf16[3,3072]{1,0:T(4,128)(2,1)S(1)} %collective-permute-done.refs_4_.refs_1_, f32[4,3072]{1,0:T(4,128)S(1)} %copy-done.1, f32[4,128,256]{2,1,0:T(8,128)S(1)} %get-tuple-element.48.refs_3_, ...), custom_call_target="tpu_custom_call" | custom-call | flops 1000000 | bytes 1024 | tf_op jit(solution)/shard_map/pallas_call | solution.py:351
  24.8 0.0 collective-permute-done.2.refs_1_
  24.8 2.8 %collective-permute-done.3.refs_2_ = f32[128,256]{1,0:T(8,128)S(1)} collective-permute-done((f32[128,256]{1,0:T(8,128)S(1)}, f32[128,256]{1,0:T(8,128)S(1)}, u32[]{:S(2)}, u32[]{:S(2)}) %collective-permute-start.3) | collective-permute-done | bytes 131104 | tf_op jit(solution)/shard_map/ppermute | solution.py:415
  27.6 0.0 collective-permute-done.4.refs_3_
  27.6 0.5 shard_map.55
  28.1 0.1 collective-permute-start.7
  28.2 0.1 collective-permute-start.6
  28.3 1.5 %collective-permute-start.5 = (f32[128,256]{1,0:T(8,128)S(1)}, f32[128,256]{1,0:T(8,128)S(1)}, u32[]{:S(2)}, u32[]{:S(2)}) collective-permute-start(f32[128,256]{1,0:T(8,128)S(1)} %get-tuple-element.62.refs_0_), channel_id=1, source_target_pairs={{0,8},{8,16},{16,24},{24,0},{1,9},{9,17},{17,25},{25,1},{2,10},{10... | collective-permute-start | bytes 393224 | tf_op jit(solution)/shard_map/ppermute | solution.py:415
  29.7 1.2 %shard_map.56 = (f32[4,256,128]{2,1,0:T(8,128)S(1)}, f32[4,256,128]{2,1,0:T(8,128)S(1)}, f32[8,128]{1,0:T(8,128)S(1)}) custom-call(bf16[256,3072]{1,0:T(8,128)(2,1)S(1)} %copy-done, bf16[3,3072]{1,0:T(4,128)(2,1)S(1)} %collective-permute-done.refs_4_.refs_1_, f32[4,3072]{1,0:T(4,128)S(1)} %copy-done.1, f32[2,128,256]{2,1,0:T(8,128)S(1)} %get-tuple-element.63.refs_3_, ...), custom_call_target="tpu_custom_call" | custom-call | flops 1000000 | bytes 1024 | tf_op jit(solution)/shard_map/pallas_call | solution.py:351
  31.0 3.1 %collective-permute-done.7.refs_3_ = f32[128,256]{1,0:T(8,128)S(1)} collective-permute-done((f32[128,256]{1,0:T(8,128)S(1)}, f32[128,256]{1,0:T(8,128)S(1)}, u32[]{:S(2)}, u32[]{:S(2)}) %collective-permute-start.7) | collective-permute-done | bytes 131104 | tf_op jit(solution)/shard_map/ppermute | solution.py:415
  34.1 0.0 collective-permute-done.6.refs_2_
  34.1 3.8 %collective-permute-done.5.refs_1_ = f32[128,256]{1,0:T(8,128)S(1)} collective-permute-done((f32[128,256]{1,0:T(8,128)S(1)}, f32[128,256]{1,0:T(8,128)S(1)}, u32[]{:S(2)}, u32[]{:S(2)}) %collective-permute-start.5) | collective-permute-done | bytes 131104 | tf_op jit(solution)/shard_map/ppermute | solution.py:415
  37.9 0.5 shard_map.57
  38.4 0.5 collective-permute-start.10
  38.9 0.4 collective-permute-start.9
  39.4 1.0 %collective-permute-start.8 = (f32[128,256]{1,0:T(8,128)S(1)}, f32[128,256]{1,0:T(8,128)S(1)}, u32[]{:S(2)}, u32[]{:S(2)}) collective-permute-start(f32[128,256]{1,0:T(8,128)S(1)} %get-tuple-element.68), channel_id=1, source_target_pairs={{0,32},{32,64},{64,96},{96,0},{1,33},{33,65},{65,97},{97,1},{2,34}... | collective-permute-start | bytes 393224 | tf_op jit(solution)/shard_map/ppermute | solution.py:415
  40.4 0.0 copy-start.3
  40.4 0.3 shard_map.58.refs_3_
  40.7 3.9 %collective-permute-done.10.refs_2_ = f32[128,256]{1,0:T(8,128)S(1)} collective-permute-done((f32[128,256]{1,0:T(8,128)S(1)}, f32[128,256]{1,0:T(8,128)S(1)}, u32[]{:S(2)}, u32[]{:S(2)}) %collective-permute-start.10) | collective-permute-done | bytes 131104 | tf_op jit(solution)/shard_map/ppermute | solution.py:415
  44.6 0.0 collective-permute-done.9.refs_1_
  44.6 3.0 %collective-permute-done.8.refs_0_ = f32[128,256]{1,0:T(8,128)S(1)} collective-permute-done((f32[128,256]{1,0:T(8,128)S(1)}, f32[128,256]{1,0:T(8,128)S(1)}, u32[]{:S(2)}, u32[]{:S(2)}) %collective-permute-start.8) | collective-permute-done | bytes 131104 | tf_op jit(solution)/shard_map/ppermute | solution.py:415
  47.6 0.6 %shard_map.59 = (f32[128,128]{1,0:T(8,128)S(1)}, f32[128,128]{1,0:T(8,128)S(1)}, f32[128,128]{1,0:T(8,128)S(1)}, f32[128,128]{1,0:T(8,128)S(1)}) custom-call(f32[128,256]{1,0:T(8,128)S(1)} %collective-permute-done.8.refs_0_, f32[128,256]{1,0:T(8,128)S(1)} %collective-permute-done.9.refs_1_, f32[128,256]{1,0:T(8,128)S(1)} %collective-permute-done.10.refs_2_, ...), custom_call_target="tpu_custom_call" | custom-call | flops 1000000 | bytes 1024 | tf_op jit(solution)/shard_map/pallas_call | solution.py:351
  48.3 0.3 collective-permute-start.11
  48.5 0.8 %collective-permute-start.12 = (f32[128,128]{1,0:T(8,128)S(1)}, f32[128,128]{1,0:T(8,128)S(1)}, u32[]{:S(2)}, u32[]{:S(2)}) collective-permute-start(f32[128,128]{1,0:T(8,128)S(1)} %get-tuple-element.73), channel_id=1, source_target_pairs={{0,2},{2,4},{4,6},{6,0},{1,3},{3,5},{5,7},{7,1},{8,10},{10,12},{12... | collective-permute-start | bytes 196616 | tf_op jit(solution)/shard_map/ppermute | solution.py:415
  49.3 1.9 %collective-permute-start.13 = (f32[128,128]{1,0:T(8,128)S(1)}, f32[128,128]{1,0:T(8,128)S(1)}, u32[]{:S(2)}, u32[]{:S(2)}) collective-permute-start(f32[128,128]{1,0:T(8,128)S(1)} %get-tuple-element.74), channel_id=1, source_target_pairs={{0,6},{2,0},{4,2},{6,4},{1,7},{3,1},{5,3},{7,5},{8,14},{10,8},{12,... | collective-permute-start | bytes 196616 | tf_op jit(solution)/shard_map/ppermute | solution.py:415
  51.2 1.9 %collective-permute-done.11.refs_4_ = f32[128,128]{1,0:T(8,128)S(1)} collective-permute-done((f32[128,128]{1,0:T(8,128)S(1)}, f32[128,128]{1,0:T(8,128)S(1)}, u32[]{:S(2)}, u32[]{:S(2)}) %collective-permute-start.11) | collective-permute-done | bytes 65568 | tf_op jit(solution)/shard_map/ppermute | solution.py:415
  53.1 0.5 collective-permute-done.12.refs_5_
  53.5 0.0 collective-permute-done.13.refs_6_
  53.5 0.2 shard_map.60
  53.8 2.7 %collective-permute-start.14 = (f32[4,128,128]{2,1,0:T(8,128)S(1)}, f32[4,128,128]{2,1,0:T(8,128)S(1)}, u32[]{:S(2)}, u32[]{:S(2)}) collective-permute-start(f32[4,128,128]{2,1,0:T(8,128)S(1)} %get-tuple-element.75), channel_id=1, source_target_pairs={{0,1},{1,0},{2,3},{3,2},{4,5},{5,4},{6,7},{7,6},{8,9},{9,8},{10,11... | collective-permute-start | bytes 786440 | tf_op jit(solution)/shard_map/ppermute | solution.py:410
  56.5 0.0 copy-done.3
  56.5 0.4 shard_map.61.refs_4_
  56.9 0.7 %collective-permute-done.14.refs_2_ = f32[4,128,128]{2,1,0:T(8,128)S(1)} collective-permute-done((f32[4,128,128]{2,1,0:T(8,128)S(1)}, f32[4,128,128]{2,1,0:T(8,128)S(1)}, u32[]{:S(2)}, u32[]{:S(2)}) %collective-permute-start.14) | collective-permute-done | bytes 262176 | tf_op jit(solution)/shard_map/ppermute | solution.py:410
  57.7 1.2 %shard_map.62 = bf16[256,1024]{1,0:T(8,128)(2,1)} custom-call(f32[4,256,128]{2,1,0:T(8,128)S(1)} %get-tuple-element.50.refs_0_, f32[4,256,128]{2,1,0:T(8,128)S(1)} %get-tuple-element.51.refs_1_, f32[4,128,128]{2,1,0:T(8,128)S(1)} %collective-permute-done.14.refs_2_, f32[1,128]{1,0:T(1,128)S(1)} %bitcast.2, bf16[256,512]{1,0:T(8,128)(2,1)S(1)} %shard_map.61.refs_4_), custom_call_target="tpu_custom_call" | custom-call | flops 1000000 | bytes 1024 | tf_op jit(solution)/shard_map/pallas_call | solution.py:351
Async XLA Ops:
  0.8 4.0 %copy-start.1 = (f32[4,3072]{1,0:T(4,128)S(1)}, f32[4,3072]{1,0:T(4,128)}, u32[]{:S(2)}) copy-start(f32[4,3072]{1,0:T(4,128)} %refs_2_.3) | copy-start | bytes 147460
  0.8 5.5 %copy-start.2 = (f32[8,256]{1,0:T(8,128)S(1)}, f32[8,256]{1,0:T(8,128)}, u32[]{:S(2)}) copy-start(f32[8,256]{1,0:T(8,128)} %refs_5_.5) | copy-start | bytes 24580
  0.8 5.5 %collective-permute-start = (bf16[3,3072]{1,0:T(4,128)(2,1)S(1)}, bf16[3,3072]{1,0:T(4,128)(2,1)S(1)}, u32[]{:S(2)}, u32[]{:S(2)}) collective-permute-start(bf16[3,3072]{1,0:T(4,128)(2,1)S(1)} %slice.3), channel_id=1, source_target_pairs={{0,1},{1,2},{2,3},{3,4},{4,5},{5,6},{6,7},{7,8},{8,9},{9,10},{10,1... | collective-permute-start | bytes 55304 | tf_op jit(solution)/shard_map/ppermute | solution.py:429
  9.4 8.3 %collective-permute-start.1 = (f32[4,128,256]{2,1,0:T(8,128)S(1)}, f32[4,128,256]{2,1,0:T(8,128)S(1)}, u32[]{:S(2)}, u32[]{:S(2)}) collective-permute-start(f32[4,128,256]{2,1,0:T(8,128)S(1)} %get-tuple-element.55), channel_id=1, source_target_pairs={{0,1},{1,0},{2,3},{3,2},{4,5},{5,4},{6,7},{7,6},{8,9},{9,8},{10,11... | collective-permute-start | bytes 1572872 | tf_op jit(solution)/shard_map/ppermute | solution.py:410
  17.7 5.9 %copy-start = (bf16[256,3072]{1,0:T(8,128)(2,1)S(1)}, bf16[256,3072]{1,0:T(8,128)(2,1)}, u32[]{:S(2)}) copy-start(bf16[256,3072]{1,0:T(8,128)(2,1)} %refs_0_.5) | copy-start | bytes 4718596
  18.0 6.9 %collective-permute-start.2 = (f32[128,256]{1,0:T(8,128)S(1)}, f32[128,256]{1,0:T(8,128)S(1)}, u32[]{:S(2)}, u32[]{:S(2)}) collective-permute-start(f32[128,256]{1,0:T(8,128)S(1)} %get-tuple-element.56.refs_6_), channel_id=1, source_target_pairs={{0,4},{2,6},{4,0},{6,2},{1,5},{3,7},{5,1},{7,3},{8,12},{10,14},{12... | collective-permute-start | bytes 393224 | tf_op jit(solution)/shard_map/ppermute | solution.py:415
  20.8 6.8 %collective-permute-start.3 = (f32[128,256]{1,0:T(8,128)S(1)}, f32[128,256]{1,0:T(8,128)S(1)}, u32[]{:S(2)}, u32[]{:S(2)}) collective-permute-start(f32[128,256]{1,0:T(8,128)S(1)} %get-tuple-element.59), channel_id=1, source_target_pairs={{0,2},{2,4},{4,6},{6,0},{1,3},{3,5},{5,7},{7,1},{8,10},{10,12},{12... | collective-permute-start | bytes 393224 | tf_op jit(solution)/shard_map/ppermute | solution.py:415
  20.9 6.7 %collective-permute-start.4 = (f32[128,256]{1,0:T(8,128)S(1)}, f32[128,256]{1,0:T(8,128)S(1)}, u32[]{:S(2)}, u32[]{:S(2)}) collective-permute-start(f32[128,256]{1,0:T(8,128)S(1)} %get-tuple-element.60), channel_id=1, source_target_pairs={{0,6},{2,0},{4,2},{6,4},{1,7},{3,1},{5,3},{7,5},{8,14},{10,8},{12,... | collective-permute-start | bytes 393224 | tf_op jit(solution)/shard_map/ppermute | solution.py:415
  28.1 6.0 %collective-permute-start.7 = (f32[128,256]{1,0:T(8,128)S(1)}, f32[128,256]{1,0:T(8,128)S(1)}, u32[]{:S(2)}, u32[]{:S(2)}) collective-permute-start(f32[128,256]{1,0:T(8,128)S(1)} %get-tuple-element.62.refs_0_), channel_id=1, source_target_pairs={{0,16},{8,24},{16,0},{24,8},{1,17},{9,25},{17,1},{25,9},{2,18},{10... | collective-permute-start | bytes 393224 | tf_op jit(solution)/shard_map/ppermute | solution.py:415
  28.2 5.9 %collective-permute-start.6 = (f32[128,256]{1,0:T(8,128)S(1)}, f32[128,256]{1,0:T(8,128)S(1)}, u32[]{:S(2)}, u32[]{:S(2)}) collective-permute-start(f32[128,256]{1,0:T(8,128)S(1)} %get-tuple-element.62.refs_0_), channel_id=1, source_target_pairs={{0,24},{8,0},{16,8},{24,16},{1,25},{9,1},{17,9},{25,17},{2,26},{10... | collective-permute-start | bytes 393224 | tf_op jit(solution)/shard_map/ppermute | solution.py:415
  28.3 9.6 %collective-permute-start.5 = (f32[128,256]{1,0:T(8,128)S(1)}, f32[128,256]{1,0:T(8,128)S(1)}, u32[]{:S(2)}, u32[]{:S(2)}) collective-permute-start(f32[128,256]{1,0:T(8,128)S(1)} %get-tuple-element.62.refs_0_), channel_id=1, source_target_pairs={{0,8},{8,16},{16,24},{24,0},{1,9},{9,17},{17,25},{25,1},{2,10},{10... | collective-permute-start | bytes 393224 | tf_op jit(solution)/shard_map/ppermute | solution.py:415
  38.4 6.2 %collective-permute-start.10 = (f32[128,256]{1,0:T(8,128)S(1)}, f32[128,256]{1,0:T(8,128)S(1)}, u32[]{:S(2)}, u32[]{:S(2)}) collective-permute-start(f32[128,256]{1,0:T(8,128)S(1)} %get-tuple-element.68), channel_id=1, source_target_pairs={{0,64},{32,96},{64,0},{96,32},{1,65},{33,97},{65,1},{97,33},{2,66}... | collective-permute-start | bytes 393224 | tf_op jit(solution)/shard_map/ppermute | solution.py:415
  38.9 5.7 %collective-permute-start.9 = (f32[128,256]{1,0:T(8,128)S(1)}, f32[128,256]{1,0:T(8,128)S(1)}, u32[]{:S(2)}, u32[]{:S(2)}) collective-permute-start(f32[128,256]{1,0:T(8,128)S(1)} %get-tuple-element.68), channel_id=1, source_target_pairs={{0,96},{32,0},{64,32},{96,64},{1,97},{33,1},{65,33},{97,65},{2,98}... | collective-permute-start | bytes 393224 | tf_op jit(solution)/shard_map/ppermute | solution.py:415
  39.4 8.3 %collective-permute-start.8 = (f32[128,256]{1,0:T(8,128)S(1)}, f32[128,256]{1,0:T(8,128)S(1)}, u32[]{:S(2)}, u32[]{:S(2)}) collective-permute-start(f32[128,256]{1,0:T(8,128)S(1)} %get-tuple-element.68), channel_id=1, source_target_pairs={{0,32},{32,64},{64,96},{96,0},{1,33},{33,65},{65,97},{97,1},{2,34}... | collective-permute-start | bytes 393224 | tf_op jit(solution)/shard_map/ppermute | solution.py:415
  40.4 16.1 %copy-start.3 = (f32[128]{0:T(128)S(1)}, f32[128]{0:T(128)}, u32[]{:S(2)}) copy-start(f32[128]{0:T(128)} %param.7) | copy-start | bytes 1540
  48.3 4.8 %collective-permute-start.11 = (f32[128,128]{1,0:T(8,128)S(1)}, f32[128,128]{1,0:T(8,128)S(1)}, u32[]{:S(2)}, u32[]{:S(2)}) collective-permute-start(f32[128,128]{1,0:T(8,128)S(1)} %get-tuple-element.72), channel_id=1, source_target_pairs={{0,4},{2,6},{4,0},{6,2},{1,5},{3,7},{5,1},{7,3},{8,12},{10,14},{12... | collective-permute-start | bytes 196616 | tf_op jit(solution)/shard_map/ppermute | solution.py:415
  48.5 5.0 %collective-permute-start.12 = (f32[128,128]{1,0:T(8,128)S(1)}, f32[128,128]{1,0:T(8,128)S(1)}, u32[]{:S(2)}, u32[]{:S(2)}) collective-permute-start(f32[128,128]{1,0:T(8,128)S(1)} %get-tuple-element.73), channel_id=1, source_target_pairs={{0,2},{2,4},{4,6},{6,0},{1,3},{3,5},{5,7},{7,1},{8,10},{10,12},{12... | collective-permute-start | bytes 196616 | tf_op jit(solution)/shard_map/ppermute | solution.py:415
  49.3 4.2 %collective-permute-start.13 = (f32[128,128]{1,0:T(8,128)S(1)}, f32[128,128]{1,0:T(8,128)S(1)}, u32[]{:S(2)}, u32[]{:S(2)}) collective-permute-start(f32[128,128]{1,0:T(8,128)S(1)} %get-tuple-element.74), channel_id=1, source_target_pairs={{0,6},{2,0},{4,2},{6,4},{1,7},{3,1},{5,3},{7,5},{8,14},{10,8},{12,... | collective-permute-start | bytes 196616 | tf_op jit(solution)/shard_map/ppermute | solution.py:415
  53.8 3.9 %collective-permute-start.14 = (f32[4,128,128]{2,1,0:T(8,128)S(1)}, f32[4,128,128]{2,1,0:T(8,128)S(1)}, u32[]{:S(2)}, u32[]{:S(2)}) collective-permute-start(f32[4,128,128]{2,1,0:T(8,128)S(1)} %get-tuple-element.75), channel_id=1, source_target_pairs={{0,1},{1,0},{2,3},{3,2},{4,5},{5,4},{6,7},{7,6},{8,9},{9,8},{10,11... | collective-permute-start | bytes 786440 | tf_op jit(solution)/shard_map/ppermute | solution.py:410
